TPU v7x, 32 devices: a whole 2x2x4 slice. The times are simulated.
32 devices in a mesh: ctx: 8 (over z, y), exp: 4 (over x, core).
Axes of the slice: x: 2, y: 2, z: 4, core: 2. Of those that a mesh axis runs over, the one named last changes fastest.
Arguments:
- tokens: bfloat16 [1024, 4096], P('ctx'), may hold values from -6 to 6
- ada_shift: float32 [4096], replicated, may hold values from -3 to 3
- ada_scale: float32 [4096], replicated, may hold values from -3 to 3
- ada_gate: float32 [4096], replicated, may hold values from -6 to 6
- router: bfloat16 [4, 4096, 2], P('exp'), may hold values from -0.09375 to 0.09375
- expert_up: bfloat16 [4, 4096, 16384], P('exp', None, 'ctx'), may hold values from -0.09375 to 0.09375
- expert_down: bfloat16 [4, 16384, 4096], P('exp', 'ctx'), may hold values from -0.0625 to 0.0625
- picked_ids: int32 [4, 2, 32], P('exp'), may hold values from 0 to 1023, as said below
- out_grad: bfloat16 [1024, 4096], P('ctx'), may hold values from -6 to 6
Outputs:
- block_out: bfloat16 [1024, 4096], P('ctx')
- tokens_grad: bfloat16 [1024, 4096], P('ctx')
- up_grad: bfloat16 [4, 4096, 16384], P('exp', None, 'ctx')
- down_grad: bfloat16 [4, 16384, 4096], P('exp', 'ctx')
- router_grad: float32 [4, 4096, 2], P('exp')
- shift_grad: float32 [4096], replicated
- scale_grad: float32 [4096], replicated
- gate_grad: float32 [4096], replicated
Inputs may be any that keep to these rules, and one draw needn't show every extreme that they name: Row picked_ids[e, j] lists 32 distinct tokens for expert e * 2 + j. Among the 128 tokens of any one index of ctx it picks at most 8, and for each expert exactly 8 from at least one such index.
All inputs are finite; a program needn't handle non-finite values.
Results may differ from a plain program's by a relative error of at most 0.007.
Values may be sent and summed in bfloat16 or wider, within the bound.
No kernel may reach another device: no remote copies, remote signals or barrier semaphores. Data moves between devices by JAX's collectives and lax.ppermute only.
A program may use at most 128 MiB of HBM per device.

v0:
```python
import jax
import jax.numpy as jnp
from jax import lax
from jax.sharding import PartitionSpec as P

MOST = 8


GELU_C = 0.7978845608028654


def gelu_tanh(values):
    inner_arg = GELU_C * (values + 0.044715 * values * values * values)
    return 0.5 * values * (1.0 + jnp.tanh(inner_arg))


def gelu_slope(values):
    inner_arg = GELU_C * (values + 0.044715 * values * values * values)
    tangent = jnp.tanh(inner_arg)
    return 0.5 * (1.0 + tangent) + 0.5 * values * (1.0 - tangent * tangent) * GELU_C * (
        1.0 + 3.0 * 0.044715 * values * values
    )


def select_table(token_ids, start_row, tok_count, most_rows):
    local_ids = token_ids - start_row
    inside = (local_ids >= 0) & (local_ids < tok_count)
    position = jnp.cumsum(inside.astype(jnp.int32)) - 1
    slot_hit = (position[:, None] == jnp.arange(most_rows, dtype=jnp.int32)[None, :]) & inside[
        :, None
    ]
    token_hit = local_ids[:, None] == jnp.arange(tok_count, dtype=jnp.int32)[None, :]
    return lax.dot_general(
        slot_hit.astype(jnp.float32),
        token_hit.astype(jnp.float32),
        (((0,), (0,)), ((), ())),
        precision=lax.Precision.HIGHEST,
    )


def sum_experts(values):
    return lax.psum(values, "exp")


def per_device(
    tokens, ada_shift, ada_scale, ada_gate, router, expert_up, expert_down, picked_ids, out_grad
):
    highest = lax.Precision.HIGHEST
    tok_count = tokens.shape[0]
    width = tokens.shape[1]
    pair_count = picked_ids.shape[1]
    ctx_size = lax.axis_size("ctx")
    members = ctx_size // pair_count
    ctx_place = lax.axis_index("ctx")
    my_group = ctx_place // members
    start_row = ctx_place * tok_count
    tables = jnp.stack(
        [
            select_table(picked_ids[0, slot_index], start_row, tok_count, MOST)
            for slot_index in range(pair_count)
        ]
    )

    def deliver(row_data):
        everyone = lax.all_gather(row_data, "ctx", axis=0, tiled=True)
        everyone = everyone.reshape(ctx_size, pair_count, MOST, width)
        chosen = lax.dynamic_index_in_dim(everyone, my_group, 1, keepdims=False)
        return chosen.reshape(ctx_size * MOST, width)

    def send_back(left, product):
        group_mask = (jnp.arange(pair_count, dtype=jnp.int32) == my_group).astype(jnp.float32)[
            None, :, None, None
        ]
        dest_count = pair_count * MOST * lax.axis_size("ctx") // (pair_count * MOST)
        product_rows = product(left).reshape(dest_count, 1, MOST, width)
        summed = lax.psum_scatter(
            (product_rows * group_mask).reshape(pair_count * MOST * lax.axis_size("ctx"), width),
            "ctx",
            scatter_dimension=0,
            tiled=True,
        )
        return summed.reshape(pair_count, MOST, width)

    inputs = tokens.astype(jnp.float32)
    centered = inputs - jnp.mean(inputs, axis=1, keepdims=True)
    inverse_std = lax.rsqrt(jnp.mean(centered * centered, axis=1, keepdims=True) + 1e-06)
    normed = centered * inverse_std
    hidden = (normed * (1.0 + ada_scale) + ada_shift).astype(jnp.bfloat16)
    router_cols = router[0]
    logits = jnp.dot(hidden, router_cols, preferred_element_type=jnp.float32)
    weights = jax.nn.sigmoid(logits)
    row_weight = jnp.einsum("jmt,tj->jm", tables, weights, precision=highest)
    sent_rows = jnp.einsum(
        "jmt,td->jmd", tables.astype(jnp.bfloat16), hidden, preferred_element_type=jnp.float32
    ).astype(jnp.bfloat16)
    up_slice = expert_up[0]
    down_slice = expert_down[0]
    expert_rows = deliver(sent_rows)
    pre_act = jnp.dot(expert_rows, up_slice, preferred_element_type=jnp.float32)
    activated = gelu_tanh(pre_act).astype(jnp.bfloat16)

    def down_product(row_block):
        return jnp.dot(row_block, down_slice, preferred_element_type=jnp.float32)

    expert_out = send_back(activated, down_product)
    contrib = jnp.einsum(
        "jmt,jmd->td", tables, row_weight[:, :, None] * expert_out, precision=highest
    )
    mixture = sum_experts(contrib)
    block_out = (inputs + ada_gate * mixture).astype(jnp.bfloat16)
    grad_in = out_grad.astype(jnp.float32)
    grad_mix = ada_gate * grad_in
    mix_rows = jnp.einsum("jmt,td->jmd", tables, grad_mix, precision=highest)
    grad_rows = (row_weight[:, :, None] * mix_rows).astype(jnp.bfloat16)
    grad_weight = jnp.sum(mix_rows * expert_out, axis=2)
    grad_logit = grad_weight * row_weight * (1.0 - row_weight)
    logit_tok = jnp.einsum("jmt,jm->tj", tables, grad_logit, precision=highest)
    expert_grads = deliver(grad_rows)
    grad_act = lax.dot_general(
        expert_grads, down_slice, (((1,), (1,)), ((), ())), preferred_element_type=jnp.float32
    )
    grad_pre = (grad_act * gelu_slope(pre_act)).astype(jnp.bfloat16)
    down_grad = lax.dot_general(
        activated, expert_grads, (((0,), (0,)), ((), ())), preferred_element_type=jnp.float32
    ).astype(jnp.bfloat16)
    up_grad = lax.dot_general(
        expert_rows, grad_pre, (((0,), (0,)), ((), ())), preferred_element_type=jnp.float32
    ).astype(jnp.bfloat16)

    def up_product(row_block):
        return lax.dot_general(
            row_block, up_slice, (((1,), (1,)), ((), ())), preferred_element_type=jnp.float32
        )

    back_rows = send_back(grad_pre, up_product)
    grad_local = jnp.einsum("jmt,jmd->td", tables, back_rows, precision=highest)
    grad_local = grad_local + lax.dot_general(
        logit_tok, router_cols.astype(jnp.float32), (((1,), (1,)), ((), ())), precision=highest
    )
    grad_hidden = sum_experts(grad_local)
    grad_norm = grad_hidden * (1.0 + ada_scale)
    tokens_grad = (
        grad_in
        + inverse_std
        * (
            grad_norm
            - jnp.mean(grad_norm, axis=1, keepdims=True)
            - normed * jnp.mean(grad_norm * normed, axis=1, keepdims=True)
        )
    ).astype(jnp.bfloat16)
    router_part = lax.dot_general(
        hidden.astype(jnp.float32), logit_tok, (((0,), (0,)), ((), ())), precision=highest
    )
    vectors = jnp.stack(
        [
            jnp.sum(grad_hidden, axis=0),
            jnp.sum(grad_hidden * normed, axis=0),
            jnp.sum(grad_in * mixture, axis=0),
        ]
    )
    router_total, vector_total = lax.psum((router_part, vectors), "ctx")
    return (
        block_out,
        tokens_grad,
        up_grad[None],
        down_grad[None],
        router_total[None],
        vector_total[0],
        vector_total[1],
        vector_total[2],
    )


def solution(mesh):
    in_specs = (
        P("ctx", None),
        P(),
        P(),
        P(),
        P("exp", None, None),
        P("exp", None, "ctx"),
        P("exp", "ctx", None),
        P("exp", None, None),
        P("ctx", None),
    )
    out_specs = (
        P("ctx", None),
        P("ctx", None),
        P("exp", None, "ctx"),
        P("exp", "ctx", None),
        P("exp", None, None),
        P(),
        P(),
        P(),
    )
    return jax.shard_map(
        per_device, mesh=mesh, in_specs=in_specs, out_specs=out_specs, check_vma=False
    )
```

profile of v0, /device:TPU:0, one launch (start us, length us, event | category | flops | bytes accessed | tf_op | source)
XLA Modules:
  0.0 455.0 jit_solution(5060405514987887031)
XLA Ops:
  7.3 0.8 compare_and_fusion.1
  8.0 0.8 fusion.71
  8.8 0.8 fusion.83
  9.6 1.5 convert_reduce_fusion
  11.0 1.7 fusion.26
  12.7 0.1 copy.21
  12.8 0.1 reduce-window.16
  12.8 0.1 add_reduce_fusion.1
  13.0 0.1 copy.22
  13.1 0.1 reduce-window.17
  13.1 0.1 add_reduce_fusion
  13.2 0.3 convolution_bitcast_fusion.4
  13.5 0.3 convolution_bitcast_fusion.3
  13.7 0.5 fusion.21
  14.2 0.9 convolution_convert_fusion
  15.2 0.0 reduce-scatter.3.cloned.1.call-start
  15.2 0.1 mul.188
  15.3 0.1 mul.189
  15.4 42.8 %all-gather.3.cloned.1.call-done = bf16[16,8,4096]{2,1,0:T(8,128)(2,1)} async-done(((bf16[2,8,4096]{2,1,0:T(8,128)(2,1)}), bf16[16,8,4096]{2,1,0:T(8,128)(2,1)}) %all-gather.3.cloned.1.call-update) | async-done | bytes 1048592 | tf_op jit(solution)/shard_map/all_gather | solution.py:65
  58.2 9.0 %fusion.6 = f32[64,2048]{1,0:T(8,128)S(1)} fusion(bf16[1,4096,2048]{2,1,0:T(8,128)(2,1)} %param.14, bf16[8,2,8,4096]{3,2,1,0:T(8,128)(2,1)} %bitcast.107, s32[]{:T(128)S(6)} %select_n.11), kind=kOutput, calls=%fused_computation.6 | convolution fusion | flops 1073741824 | bytes 17825796 | tf_op jit(solution)/shard_map/dot_general | solution.py:99
  67.1 8.8 %fusion.2 = f32[8,8,4096]{2,1,0:T(8,128)S(1)} fusion(bf16[1,2048,4096]{2,1,0:T(8,128)(2,1)} %param.15, f32[64,2048]{1,0:T(8,128)S(1)} %fusion.6), kind=kOutput, calls=%fused_computation.2 | convolution fusion | flops 1074921472 | bytes 18350080 | tf_op jit(solution)/shard_map/dot_general | solution.py:103
  76.0 1.6 bitcast_multiply_fusion.1
  77.6 0.0 all-gather.5.cloned.1.call-start
  77.6 0.4 fusion.35
  78.0 0.2 fusion.70
  78.2 66.6 %reduce-scatter.3.cloned.1.call-done = f32[16,4096]{1,0:T(8,128)} async-done(((f32[128,4096]{1,0:T(8,128)}), f32[16,4096]{1,0:T(8,128)}) %reduce-scatter.3.cloned.1.call-update) | async-done | bytes 262160 | tf_op jit(solution)/shard_map/reduce_scatter | solution.py:76
  144.7 3.1 fusion.53
  147.9 0.2 reduce-scatter.5.cloned.1.call-start
  148.1 39.0 %all-gather.5.cloned.1.call-done = bf16[16,8,4096]{2,1,0:T(8,128)(2,1)} async-done(((bf16[2,8,4096]{2,1,0:T(8,128)(2,1)}), bf16[16,8,4096]{2,1,0:T(8,128)(2,1)}) %all-gather.5.cloned.1.call-update) | async-done | bytes 1048592 | tf_op jit(solution)/shard_map/all_gather | solution.py:65
  187.2 11.2 %fusion.17 = bf16[64,2048]{1,0:T(8,128)(2,1)S(1)} fusion(bf16[1,2048,4096]{2,1,0:T(8,128)(2,1)} %param.15, f32[64,2048]{1,0:T(8,128)S(1)} %fusion.6, bf16[8,2,8,4096]{3,2,1,0:T(8,128)(2,1)} %bitcast.109, s32[]{:T(128)S(6)} %select_n.11), kind=kOutput, calls=%fused_computation.28 | convolution fusion | flops 1076232192 | bytes 18087940 | tf_op jit(solution)/shard_map/dot_general | solution.py:119
  198.3 11.0 %fusion = f32[8,8,4096]{2,1,0:T(8,128)S(1)} fusion(bf16[1,4096,2048]{2,1,0:T(8,128)(2,1)} %param.14, bf16[64,2048]{1,0:T(8,128)(2,1)S(1)} %fusion.17), kind=kOutput, calls=%fused_computation | convolution fusion | flops 1073741824 | bytes 18087936 | tf_op jit(solution)/shard_map/dot_general | solution.py:131
  209.3 1.6 bitcast_multiply_fusion
  210.9 3.2 convolution_bitcast_fusion.1
  214.1 0.1 fusion.69
  214.2 63.1 %reduce-scatter.5.cloned.1.call-done = f32[16,4096]{1,0:T(8,128)} async-done(((f32[128,4096]{1,0:T(8,128)}), f32[16,4096]{1,0:T(8,128)}) %reduce-scatter.5.cloned.1.call-update) | async-done | bytes 262160 | tf_op jit(solution)/shard_map/reduce_scatter | solution.py:76
  277.4 2.8 convolution_bitcast_fusion
  280.2 2.4 convolution_add_fusion
  282.6 0.3 all-reduce.5.cloned.1.call-start
  282.9 1.1 convolution_bitcast_fusion.2
  284.0 9.6 %convert_bitcast_fusion = bf16[1,2048,4096]{2,1,0:T(8,128)(2,1)} fusion(bf16[8,2,8,4096]{3,2,1,0:T(8,128)(2,1)} %bitcast.110, s32[]{:T(128)S(6)} %select_n.11, f32[64,2048]{1,0:T(8,128)S(1)} %fusion.6), kind=kOutput, calls=%fused_computation.8 | convolution fusion | flops 1083310080 | bytes 17825796 | tf_op jit(solution)/shard_map/dot_general | solution.py:123
  293.6 73.9 %all-reduce.7.cloned.1.call-done = (f32[128,4096]{1,0:T(8,128)}, f32[128,4096]{1,0:T(8,128)}) async-done(((f32[128,4096]{1,0:T(8,128)}, f32[128,4096]{1,0:T(8,128)}), (f32[128,4096]{1,0:T(8,128)}, f32[128,4096]{1,0:T(8,128)})) %all-reduce.7.cloned.1.call-update) | async-done | bytes 4194320 | tf_op jit(solution)/shard_map/psum | solution.py:42
  367.5 2.7 fusion.25
  370.2 4.3 fusion.32
  374.5 0.7 pad_maximum_fusion
  375.2 9.6 %convert_bitcast_fusion.1 = bf16[1,4096,2048]{2,1,0:T(8,128)(2,1)} fusion(bf16[64,2048]{1,0:T(8,128)(2,1)S(1)} %fusion.17, bf16[8,2,8,4096]{3,2,1,0:T(8,128)(2,1)} %bitcast.108, s32[]{:T(128)S(6)} %select_n.11), kind=kOutput, calls=%fused_computation.9 | convolution fusion | flops 1082130432 | bytes 17563652 | tf_op jit(solution)/shard_map/dot_general | solution.py:126
  384.8 60.3 %all-reduce.5.cloned.1.call-done = (f32[1,4096,2]{1,2,0:T(2,128)}, f32[3,4096]{1,0:T(4,128)}) async-done(((f32[1,4096,2]{1,2,0:T(2,128)}, f32[3,4096]{1,0:T(4,128)}), (f32[1,4096,2]{1,2,0:T(2,128)}, f32[3,4096]{1,0:T(4,128)})) %all-reduce.5.cloned.1.call-update) | async-done | bytes 81936 | tf_op jit(solution)/shard_map/psum | solution.py:161
  445.1 1.6 fusion.85
  446.7 1.4 copy.31
  (30 shorter events, 0.3 us)
Async XLA Ops:
  7.2 70.4 %copy-start = (bf16[1,4096,2]{1,2,0:T(2,128)(2,1)S(1)}, bf16[1,4096,2]{1,2,0:T(2,128)(2,1)}, u32[]{:S(2)}) copy-start(bf16[1,4096,2]{1,2,0:T(2,128)(2,1)} %param.13) | copy-start | bytes 49156
  7.2 6.6 %copy-start.1 = (bf16[128,4096]{1,0:T(8,128)(2,1)S(1)}, bf16[128,4096]{1,0:T(8,128)(2,1)}, u32[]{:S(2)}) copy-start(bf16[128,4096]{1,0:T(8,128)(2,1)} %param.9) | copy-start | bytes 3145732
  7.2 5.8 %copy-start.7 = (f32[4096]{0:T(1024)S(1)}, f32[4096]{0:T(1024)}, u32[]{:S(2)}) copy-start(f32[4096]{0:T(1024)} %param.11) | copy-start | bytes 49156
  7.2 6.5 %copy-start.6 = (f32[4096]{0:T(1024)S(1)}, f32[4096]{0:T(1024)}, u32[]{:S(2)}) copy-start(f32[4096]{0:T(1024)} %param.10) | copy-start | bytes 49156
  7.2 51.0 %all-gather.3.cloned.1.call-start = ((), (), s32[]{:S(2)}) async-start(), calls=%async_computation.2 | async-start | bytes 1179648 | tf_op jit(solution)/shard_map/all_gather | solution.py:65
  15.2 129.5 %reduce-scatter.3.cloned.1.call-start = ((), (), s32[]{:S(2)}) async-start(), calls=%async_computation.3 | async-start | bytes 2359296 | tf_op jit(solution)/shard_map/reduce_scatter | solution.py:76
  77.5 67.2 %copy-start.5 = (f32[4096]{0:T(1024)S(1)}, f32[4096]{0:T(1024)}, u32[]{:S(2)}) copy-start(f32[4096]{0:T(1024)} %param.12) | copy-start | bytes 49156
  77.6 109.6 %all-gather.5.cloned.1.call-start = ((), (), s32[]{:S(2)}) async-start(), calls=%async_computation.4 | async-start | bytes 1179648 | tf_op jit(solution)/shard_map/all_gather | solution.py:65
  147.9 129.5 %reduce-scatter.5.cloned.1.call-start = ((), (), s32[]{:S(2)}) async-start(), calls=%async_computation.5 | async-start | bytes 2359296 | tf_op jit(solution)/shard_map/reduce_scatter | solution.py:76
  209.3 1.7 copy-start.4
  210.9 156.6 %all-reduce.7.cloned.1.call-start = ((), (), s32[]{:S(2)}) async-start(), calls=%async_computation.7 | async-start | bytes 8388608 | tf_op jit(solution)/shard_map/psum | solution.py:42
  282.6 162.5 %all-reduce.5.cloned.1.call-start = ((), (), s32[]{:S(2)}) async-start(), calls=%async_computation.6 | async-start | bytes 196608 | tf_op jit(solution)/shard_map/psum | solution.py:161
  293.6 76.6 %copy-start.3 = (bf16[128,4096]{1,0:T(8,128)(2,1)S(1)}, bf16[128,4096]{1,0:T(8,128)(2,1)}, u32[]{:S(2)}) copy-start(bf16[128,4096]{1,0:T(8,128)(2,1)} %param.17) | copy-start | bytes 3145732
  367.5 2.7 copy-start.2
Sparse Core Ops, SparseCore 0:
  15.3 42.8 all-gather.2
  77.7 66.9 reduce-scatter.2
  148.0 39.1 all-gather.4
  211.0 66.3 reduce-scatter.4
  282.7 84.7 all-reduce.6
  375.4 69.7 all-reduce.4
where the time goes:
time: 456 us; the launch traced here: 455 us
  waiting for transfers between devices  346 us (76%)
  matrix products  73.8 us (16%)
  other arithmetic  17.1 us (4%)
  between operations  14.3 us (3%)
    reduce_scatter x2, waiting for transfers between devices, send_back(): lax.psum_scatter((product_rows * group_mask).reshape(pair_count * MOST *...  130 us
    all_gather x2, waiting for transfers between devices, deliver(): everyone = lax.all_gather(row_data, 'ctx', axis=0, tiled=True)  81.8 us
    psum x1, waiting for transfers between devices, sum_experts(): return lax.psum(values, 'exp')  73.9 us
    psum x1, waiting for transfers between devices, per_device(): router_total, vector_total = lax.psum((router_part, vectors), 'ctx')  60.3 us
    dot_general x1, matrix products, per_device(): lax.dot_general(expert_grads, down_slice, (((1,), (1,)), ((), ())), prefe...  11.2 us
    dot_general x1, matrix products, up_product(): lax.dot_general(row_block, up_slice, (((1,), (1,)), ((), ())), preferred_...  11 us
    dot_general x1, matrix products, per_device(): lax.dot_general(expert_rows, grad_pre, (((0,), (0,)), ((), ())), preferre...  9.6 us
    dot_general x1, matrix products, per_device(): lax.dot_general(activated, expert_grads, (((0,), (0,)), ((), ())), prefer...  9.59 us
  transfers between devices with their start and end apart: 6, of which 6 were waited for; matrix products, arithmetic and copies ran while one was open for 5% of the time, Pallas kernels for 0%

commit v1 on v0

v1 whole, which is shorter than its diff:
```python
import functools

import jax
import jax.numpy as jnp
from jax import lax
from jax.experimental import pallas as pl
from jax.experimental.pallas import tpu as pltpu
from jax.sharding import PartitionSpec as P

MOST = 8
GROUP = 2 * MOST
SIDE = 8
GELU_C = 0.7978845608028654
MIB = 1 << 20
f32, bf16 = jnp.float32, jnp.bfloat16
WHOLE = pl.BlockSpec(memory_space=pltpu.VMEM)
SCALARS = pl.BlockSpec(memory_space=pltpu.SMEM)


def dot(left, right, left_dim, right_dim):
    return lax.dot_general(
        left, right, (((left_dim,), (right_dim,)), ((), ())), preferred_element_type=f32
    )


def iota(shape, dim):
    return lax.broadcasted_iota(jnp.int32, shape, dim)


def select_body(place, picked, tokens, grads, own_o, other_o, ids_o):
    tok_count = tokens.shape[0]
    cap = picked.shape[1]
    start = place[0] * tok_count
    group = place[1]
    ids = picked[...].astype(f32)
    lanes, rows = iota((cap, cap), 1), iota((cap, cap), 0)
    eye = (lanes == rows).astype(f32)
    before = (rows < lanes).astype(f32)
    slot = (iota((GROUP, cap), 0) % MOST).astype(f32)
    tables = []
    for which in range(2):
        row = jnp.where(group == which, ids[0:1], ids[1:2]) - start.astype(f32)
        inside = ((row >= 0.0) & (row < float(tok_count))).astype(f32)
        inside_col = jnp.sum(eye * inside, axis=1, keepdims=True)
        local_col = jnp.sum(eye * row, axis=1, keepdims=True)
        rank = jnp.sum(before * inside_col, axis=0, keepdims=True)
        hit = jnp.where(rank == slot, 1.0, 0.0) * inside
        token_hit = (local_col == iota((cap, tok_count), 1).astype(f32)).astype(f32)
        tables.append(dot(hit, token_hit, 1, 0))
    table = jnp.concatenate(tables, axis=0).astype(bf16)
    second = (iota((2 * GROUP, 1), 0) % GROUP) >= MOST
    rows = jnp.where(second, dot(table, grads[...], 1, 0), dot(table, tokens[...], 1, 0)).astype(bf16)
    own_o[...] = rows[:GROUP]
    other_o[...] = rows[GROUP:]
    number = (iota((SIDE, tok_count), 1) + 1).astype(bf16)
    ids_row = dot(number, table, 1, 1) - 1.0
    kind = (iota((SIDE, 2 * GROUP), 1) % GROUP) >= MOST
    want = iota((SIDE, 2 * GROUP), 0) == 1
    ids_o[...] = jnp.where(kind == want, ids_row, -1.0)


def select(place, picked, tokens, grads):
    width = tokens.shape[1]
    return pl.pallas_call(
        select_body,
        in_specs=[SCALARS, WHOLE, WHOLE, WHOLE],
        out_specs=[WHOLE, WHOLE, WHOLE],
        out_shape=[
            jax.ShapeDtypeStruct((GROUP, width), bf16),
            jax.ShapeDtypeStruct((GROUP, width), bf16),
            jax.ShapeDtypeStruct((SIDE, 2 * GROUP), f32),
        ],
        compiler_params=pltpu.CompilerParams(vmem_limit_bytes=16 * MIB),
        name="select",
    )(place, picked, tokens, grads)


def expert_body(
    steps, blocks, counts, near, far, shift, scale, gate, column, up, down,
    hid_o, grows_o, act_o, gpre_o, keep_o, send_o, normed_s, eo_s, back_s, weight_s,
):
    index = pl.program_id(0)
    width = hid_o.shape[1]
    chunk = up.shape[2]
    half = blocks // 2

    def slots(block):
        source = near if block < half else far
        at = GROUP * (block % half)
        parts = [source[at + GROUP * k : at + GROUP * (k + 1), :].astype(f32) for k in range(2)]
        return [jnp.concatenate([p[k * MOST : (k + 1) * MOST] for p in parts], axis=0) for k in range(2)]

    @pl.when(index == 0)
    def _():
        one = 1.0 + scale[...]
        place = iota((GROUP, 1), 0)
        for block in range(0, blocks, 2):
            tok, grd = slots(block)
            rows = pl.ds(block * MOST, GROUP)
            limit = jnp.where(place < MOST, counts[block], counts[block + 1] + MOST)
            filled = (place < limit).astype(f32)
            centered = tok - jnp.mean(tok, axis=1, keepdims=True)
            inverse_std = lax.rsqrt(jnp.mean(centered * centered, axis=1, keepdims=True) + 1e-06)
            normed = centered * inverse_std
            normed_s[rows, :] = normed
            hidden = ((normed * one + shift[...]) * filled).astype(bf16)
            hid_o[rows, :] = hidden
            logit = jnp.sum(hidden.astype(f32) * column[...], axis=1, keepdims=True)
            weight = 1.0 / (1.0 + jnp.exp(-logit))
            weight_s[rows, :] = jnp.broadcast_to(weight, (GROUP, 128))
            grows_o[rows, :] = (weight * (gate[...] * grd)).astype(bf16)
        eo_s[...] = jnp.zeros_like(eo_s)
        back_s[...] = jnp.zeros_like(back_s)

    up_block, down_block = up[0], down[0]
    pre = dot(hid_o[...], up_block, 1, 0)
    grad_act = dot(grows_o[...], down_block, 1, 1)
    square = pre * pre
    tangent = jnp.tanh(GELU_C * (pre + 0.044715 * square * pre))
    act = (0.5 * pre * (1.0 + tangent)).astype(bf16)
    slope = 0.5 * (1.0 + tangent) + 0.5 * pre * (1.0 - tangent * tangent) * GELU_C * (
        1.0 + 3.0 * 0.044715 * square
    )
    grad_pre = (grad_act * slope).astype(bf16)
    here = pl.ds(pl.multiple_of(index * chunk, chunk), chunk)
    act_o[:, here] = act
    gpre_o[:, here] = grad_pre
    eo_s[...] += dot(act, down_block, 1, 0)
    back_s[...] += dot(grad_pre, up_block, 1, 1)

    @pl.when(index == steps - 1)
    def _():
        gate_v = shift_v = scale_v = router_v = jnp.zeros((1, width), f32)
        for block in range(0, blocks, 2):
            _, grd = slots(block)
            rows = pl.ds(block * MOST, GROUP)
            weight = weight_s[rows, 0:1]
            eo = eo_s[rows, :]
            grad_logit = jnp.sum(gate[...] * grd * eo, axis=1, keepdims=True) * weight * (1.0 - weight)
            eo = weight * eo
            back = back_s[rows, :] + grad_logit * column[...]
            gate_v += jnp.sum(grd * eo, axis=0, keepdims=True)
            shift_v += jnp.sum(back, axis=0, keepdims=True)
            scale_v += jnp.sum(back * normed_s[rows, :], axis=0, keepdims=True)
            router_v += jnp.sum(grad_logit * hid_o[rows, :].astype(f32), axis=0, keepdims=True)
            for k in range(2):
                cut = slice(k * MOST, (k + 1) * MOST)
                pair = jnp.concatenate([eo[cut], back[cut]], axis=0)
                at = GROUP * ((block + k) % half)
                if block < half:
                    keep_o[at : at + GROUP, :] = pair
                else:
                    send_o[at : at + GROUP, :] = pair.astype(bf16)
        side = jnp.concatenate([gate_v, shift_v, scale_v, router_v, jnp.zeros((SIDE - 4, width), f32)], axis=0)
        at = GROUP * half
        keep_o[at : at + SIDE, :] = side
        send_o[at : at + GROUP, :] = jnp.concatenate([side, jnp.zeros_like(side)], axis=0).astype(bf16)


def experts(counts, near, far, shift, scale, gate, column, up, down):
    blocks = counts.shape[0]
    slot_count = blocks * MOST
    width, hid_count = up.shape[1], up.shape[2]
    chunk = min(256, hid_count)
    steps = hid_count // chunk
    rows = GROUP * blocks // 2
    return pl.pallas_call(
        functools.partial(expert_body, steps, blocks),
        grid=(steps,),
        in_specs=[SCALARS] + [WHOLE] * 6
        + [
            pl.BlockSpec((1, width, chunk), lambda i: (0, 0, i)),
            pl.BlockSpec((1, chunk, width), lambda i: (0, i, 0)),
        ],
        out_specs=[WHOLE] * 6,
        out_shape=[
            jax.ShapeDtypeStruct((slot_count, width), bf16),
            jax.ShapeDtypeStruct((slot_count, width), bf16),
            jax.ShapeDtypeStruct((slot_count, hid_count), bf16),
            jax.ShapeDtypeStruct((slot_count, hid_count), bf16),
            jax.ShapeDtypeStruct((rows + SIDE, width), f32),
            jax.ShapeDtypeStruct((rows + GROUP, width), bf16),
        ],
        scratch_shapes=[pltpu.VMEM((slot_count, width), f32)] * 3 + [pltpu.VMEM((slot_count, 128), f32)],
        compiler_params=pltpu.CompilerParams(vmem_limit_bytes=32 * MIB),
        cost_estimate=pl.CostEstimate(
            flops=8 * slot_count * width * hid_count, bytes_accessed=4 * width * hid_count, transcendentals=0
        ),
        name="experts",
    )(counts, near, far, shift, scale, gate, column, up, down)


def outer_body(left, right, out):
    out[0] = dot(left[...], right[...], 0, 0).astype(bf16)


def outer(left, right, name):
    depth, rows = left.shape
    columns = right.shape[1]
    step = min(rows, 2 * MIB // columns)
    return pl.pallas_call(
        outer_body,
        grid=(rows // step,),
        in_specs=[pl.BlockSpec((depth, step), lambda i: (0, i)), WHOLE],
        out_specs=pl.BlockSpec((1, step, columns), lambda i: (0, i, 0)),
        out_shape=jax.ShapeDtypeStruct((1, rows, columns), bf16),
        compiler_params=pltpu.CompilerParams(vmem_limit_bytes=24 * MIB),
        cost_estimate=pl.CostEstimate(
            flops=8 * depth * rows * columns, bytes_accessed=4 * rows * columns, transcendentals=0
        ),
        name=name,
    )(left, right)


def finish_body(own, recv, scale, gate, tokens, grads, block_o, tgrad_o, gate_o, shift_o, scale_o):
    count = tokens.shape[0]
    start = pl.program_id(0) * count
    numbers = (iota((count, 2 * GROUP), 0) + start).astype(f32)
    pieces = [(part, k) for part in (own, recv) for k in range(own.shape[0])]
    rows = jnp.concatenate([part[k, : 2 * GROUP, :] for part, k in pieces], axis=0)
    tables = [[], []]
    for part, k in pieces:
        ids = part[k, 2 * GROUP :, : 2 * GROUP].astype(f32)
        for kind in range(2):
            tables[kind].append((numbers == ids[3 + kind : 4 + kind]).astype(f32))
    mixture, grad_hidden = [dot(jnp.concatenate(t, axis=1).astype(bf16), rows, 1, 0) for t in tables]
    inputs = tokens[...].astype(f32)
    block_o[...] = (inputs + gate[...] * mixture).astype(bf16)
    centered = inputs - jnp.mean(inputs, axis=1, keepdims=True)
    inverse_std = lax.rsqrt(jnp.mean(centered * centered, axis=1, keepdims=True) + 1e-06)
    normed = centered * inverse_std
    grad_norm = grad_hidden * (1.0 + scale[...])
    tgrad_o[...] = (
        grads[...].astype(f32)
        + inverse_std
        * (
            grad_norm
            - jnp.mean(grad_norm, axis=1, keepdims=True)
            - normed * jnp.mean(grad_norm * normed, axis=1, keepdims=True)
        )
    ).astype(bf16)

    @pl.when(pl.program_id(0) == 0)
    def _():
        side = sum(part[k, 2 * GROUP :, :].astype(f32) for part, k in pieces)
        gate_o[...] = side[0:1]
        shift_o[...] = side[1:2]
        scale_o[...] = side[2:3]


def finish(own, recv, scale, gate, tokens, grads):
    tok_count, width = tokens.shape
    step = min(tok_count, 32)
    block = pl.BlockSpec((step, width), lambda i: (i, 0))
    vector = jax.ShapeDtypeStruct((1, width), f32)
    return pl.pallas_call(
        finish_body,
        grid=(tok_count // step,),
        in_specs=[WHOLE] * 4 + [block, block],
        out_specs=[block, block] + [WHOLE] * 3,
        out_shape=[jax.ShapeDtypeStruct((tok_count, width), bf16)] * 2 + [vector] * 3,
        compiler_params=pltpu.CompilerParams(vmem_limit_bytes=16 * MIB),
        name="finish",
    )(own, recv, scale, gate, tokens, grads)


def swap(values, axis, mask):
    size = lax.axis_size(axis)
    return lax.ppermute(values, axis, [(i, i ^ mask) for i in range(size)])


def halvings(size):
    masks = []
    while size > 1:
        size //= 2
        masks.append(size)
    return masks


def per_device(
    tokens, ada_shift, ada_scale, ada_gate, router, expert_up, expert_down, picked_ids, out_grad
):
    tok_count, width = tokens.shape
    ctx_size, exp_size = lax.axis_size("ctx"), lax.axis_size("exp")
    ctx_masks, exp_masks = halvings(ctx_size), halvings(exp_size)
    me = lax.axis_index("ctx")
    group = me // ctx_masks[0]
    picked = picked_ids[0]
    shift, scale, gate = ada_shift[None], ada_scale[None], ada_gate[None]
    place = jnp.stack([me, group]).astype(jnp.int32)
    own, other, ids = select(place, picked, tokens, out_grad)

    relative = [0]
    for mask in ctx_masks:
        relative = relative + [r ^ mask for r in relative]
    sources = me ^ jnp.array(relative, jnp.int32)
    own_ids = jnp.where(group == 0, picked[0], picked[1])
    counts = jnp.sum((own_ids // tok_count)[None, :] == sources[:, None], axis=1).astype(jnp.int32)
    columns = router[0].astype(f32).T
    column = jnp.where(group == 0, columns[0:1], columns[1:2])

    near, far = own, swap(other, "ctx", ctx_masks[0])
    for mask in ctx_masks[1:]:
        near = jnp.concatenate([near, far], axis=0)
        far = swap(near, "ctx", mask)
    hidden, grad_rows, act, grad_pre, keep, send = experts(
        counts, near, far, shift, scale, gate, column, expert_up, expert_down
    )

    rows = keep.shape[0] - SIDE
    blocks, side = keep[:rows], keep[rows:]
    send = send[: rows + SIDE]
    for mask in ctx_masks[:0:-1]:
        got = swap(send, "ctx", mask).astype(f32)
        blocks, side = blocks + got[:rows], side + got[rows:]
        rows //= 2
        send = jnp.concatenate([blocks[rows:], side], axis=0).astype(bf16)
        blocks = blocks[:rows]
    got = swap(send, "ctx", ctx_masks[0]).astype(f32)
    theirs = got[rows:]
    router_rows = jnp.where(
        group == 0, jnp.stack([side[3], theirs[3]], axis=1), jnp.stack([theirs[3], side[3]], axis=1)
    )
    mine = jnp.concatenate(
        [blocks, got[:rows], side[:3] + theirs[:3], jnp.pad(ids[:2], ((0, 3), (0, width - ids.shape[1])))],
        axis=0,
    ).astype(bf16)[None]
    far = swap(mine, "exp", exp_masks[0])
    for mask in exp_masks[1:]:
        mine = jnp.concatenate([mine, far], axis=0)
        far = swap(mine, "exp", mask)

    up_grad = outer(hidden, grad_pre, "up_grad")
    down_grad = outer(act, grad_rows, "down_grad")
    block_out, tokens_grad, gate_grad, shift_grad, scale_grad = finish(
        mine, far, scale, gate, tokens, out_grad
    )
    return (
        block_out,
        tokens_grad,
        up_grad,
        down_grad,
        router_rows[None],
        shift_grad[0],
        scale_grad[0],
        gate_grad[0],
    )


def solution(mesh):
    in_specs = (
        P("ctx", None),
        P(),
        P(),
        P(),
        P("exp", None, None),
        P("exp", None, "ctx"),
        P("exp", "ctx", None),
        P("exp", None, None),
        P("ctx", None),
    )
    out_specs = (
        P("ctx", None),
        P("ctx", None),
        P("exp", None, "ctx"),
        P("exp", "ctx", None),
        P("exp", None, None),
        P(),
        P(),
        P(),
    )
    return jax.shard_map(
        per_device, mesh=mesh, in_specs=in_specs, out_specs=out_specs, check_vma=False
    )
```

time: 456 us -> 114 us (0.25)
  waiting for transfers between devices: 346 us -> 42 us
  matrix products: 73.8 us -> 0 us
  Pallas kernels: 0 us -> 43.9 us
  other arithmetic: 17.1 us -> 1.57 us
  starting transfers between devices: 0.65 us -> 15.8 us
  between operations: 14.3 us -> 0.93 us
  local copies, waits for them, and re-layouts: 3.36 us -> 9.13 us
    psum x2 -> x0, waiting for transfers between devices: 134 us -> none  [the longest x1 73.9 us: sum_experts(): return lax.psum(values, 'exp')]
    reduce_scatter x2 -> x0, waiting for transfers between devices: 130 us -> none  [send_back(): lax.psum_scatter((product_rows * group_mask).reshape(pair_count * MOST *...]
    all_gather x2 -> x0, waiting for transfers between devices: 81.8 us -> none  [deliver(): everyone = lax.all_gather(row_data, 'ctx', axis=0, tiled=True)]
    dot_general x17 -> x0, matrix products: 73.8 us -> none  [the longest x1 11.2 us: per_device(): lax.dot_general(expert_grads, down_slice, (((1,), (1,)), ((), ())), prefe...]
    pallas_call x0 -> x5, Pallas kernels: none -> 43.9 us  [the longest x1 22.9 us: experts(): pl.pallas_call(functools.partial(expert_body, steps, blocks), grid=(steps...]
    ppermute x0 -> x8, waiting for transfers between devices: none -> 42 us  [swap(): return lax.ppermute(values, axis, [(i, i ^ mask) for i in range(size)])]
    ppermute x0 -> x8, starting transfers between devices: none -> 15.8 us  [swap(): return lax.ppermute(values, axis, [(i, i ^ mask) for i in range(size)])]
    reduce_sum x4 -> x1, other arithmetic: 10.1 us -> 0.18 us  [per_device(): jnp.sum((own_ids // tok_count)[None, :] == sources[:, None], axis=1)]
  transfers between devices with their start and end apart: 6 -> 8, of which waited for: 6 -> 6; matrix products, arithmetic and copies ran while one was open for 5% -> 1% of each run, Pallas kernels for 0% -> 14%
where the time goes in v1:
time: 114 us; the launch traced here: 113 us
  Pallas kernels  43.9 us (39%)
  waiting for transfers between devices  42 us (37%)
  starting transfers between devices  15.8 us (14%)
  local copies, waits for them, and re-layouts  9.13 us (8%)
  other arithmetic  1.57 us (1%)
    ppermute x8, waiting for transfers between devices, swap(): return lax.ppermute(values, axis, [(i, i ^ mask) for i in range(size)])  42 us
    pallas_call x1, Pallas kernels, experts(): pl.pallas_call(functools.partial(expert_body, steps, blocks), grid=(steps...  22.9 us
    pallas_call x2, Pallas kernels, outer(): pl.pallas_call(outer_body, grid=(rows // step,), in_specs=[pl.BlockSpec((...  16 us
    ppermute x8, starting transfers between devices, swap(): return lax.ppermute(values, axis, [(i, i ^ mask) for i in range(size)])  15.8 us
    unnamed x26, local copies, waits for them, and re-layouts  8.96 us
    pallas_call x1, Pallas kernels, finish(): pl.pallas_call(finish_body, grid=(tok_count // step,), in_specs=[WHOLE] *...  3.94 us
  transfers between devices with their start and end apart: 8, of which 6 were waited for; matrix products, arithmetic and copies ran while one was open for 1% of the time, Pallas kernels for 14%

profile of v1, /device:TPU:0, one launch (start us, length us, event | category | flops | bytes accessed | tf_op | source)
XLA Modules:
  0.0 113.4 jit_solution(15752623023503577548)
XLA Ops:
  0.6 0.0 copy-start.11
  0.6 0.0 copy-start.9
  0.7 0.0 copy-start.10
  0.7 0.1 pad_add_fusion.place
  0.8 1.2 %copy-done.1 = bf16[128,4096]{1,0:T(8,128)(2,1)S(1)} copy-done((bf16[128,4096]{1,0:T(8,128)(2,1)S(1)}, bf16[128,4096]{1,0:T(8,128)(2,1)}, u32[]{:S(2)}) %copy-start.1) | copy-done | bytes 1048600
  2.0 1.2 %copy-done.3 = bf16[128,4096]{1,0:T(8,128)(2,1)S(1)} copy-done((bf16[128,4096]{1,0:T(8,128)(2,1)S(1)}, bf16[128,4096]{1,0:T(8,128)(2,1)}, u32[]{:S(2)}) %copy-start.3) | copy-done | bytes 1048600
  3.2 0.7 copy-done.8
  3.9 1.1 select.23
  5.0 0.0 copy-start.5
  5.0 0.0 copy-start.6
  5.0 0.0 copy-start.7
  5.1 4.1 %collective-permute-start = (bf16[16,4096]{1,0:T(8,128)(2,1)S(1)}, bf16[16,4096]{1,0:T(8,128)(2,1)S(1)}, u32[]{:S(2)}, u32[]{:S(2)}) collective-permute-start(bf16[16,4096]{1,0:T(8,128)(2,1)S(1)} %get-tuple-element.23), channel_id=1, source_target_pairs={{0,16},{4,20},{8,24},{12,28},{16,0},{20,4},{24,8},{28,12},{1,17},{... | collective-permute-start | bytes 393224 | tf_op jit(solution)/shard_map/ppermute | solution.py:269
  9.2 0.0 copy-done.9
  9.2 0.0 copy-done.10
  9.2 0.0 copy-done.11
  9.2 0.2 convert_reduce_fusion.counts
  9.4 6.0 %collective-permute-done = bf16[16,4096]{1,0:T(8,128)(2,1)S(1)} collective-permute-done((bf16[16,4096]{1,0:T(8,128)(2,1)S(1)}, bf16[16,4096]{1,0:T(8,128)(2,1)S(1)}, u32[]{:S(2)}, u32[]{:S(2)}) %collective-permute-start) | collective-permute-done | bytes 131104 | tf_op jit(solution)/shard_map/ppermute | solution.py:269
  15.5 0.8 collective-permute-start.1
  16.3 6.8 %collective-permute-done.1 = bf16[32,4096]{1,0:T(8,128)(2,1)S(1)} collective-permute-done((bf16[32,4096]{1,0:T(8,128)(2,1)S(1)}, bf16[32,4096]{1,0:T(8,128)(2,1)S(1)}, u32[]{:S(2)}, u32[]{:S(2)}) %collective-permute-start.1) | collective-permute-done | bytes 262176 | tf_op jit(solution)/shard_map/ppermute | solution.py:269
  23.1 1.3 %collective-permute-start.2 = (bf16[64,4096]{1,0:T(8,128)(2,1)S(1)}, bf16[64,4096]{1,0:T(8,128)(2,1)S(1)}, u32[]{:S(2)}, u32[]{:S(2)}) collective-permute-start(bf16[64,4096]{1,0:T(8,128)(2,1)S(1)} %constant_dynamic-update-slice_fusion.near), channel_id=1, source_target_pairs={{0,4},{4,0},{8,12},{12,8},{16,20},{20,16},{24,28},{28,24},{1,5},{5... | collective-permute-start | bytes 1572872 | tf_op jit(solution)/shard_map/ppermute | solution.py:269
  24.4 10.9 %collective-permute-done.2.far = bf16[64,4096]{1,0:T(8,128)(2,1)S(1)} collective-permute-done((bf16[64,4096]{1,0:T(8,128)(2,1)S(1)}, bf16[64,4096]{1,0:T(8,128)(2,1)S(1)}, u32[]{:S(2)}, u32[]{:S(2)}) %collective-permute-start.2) | collective-permute-done | bytes 524320 | tf_op jit(solution)/shard_map/ppermute | solution.py:269
  35.3 0.0 copy-done.5
  35.3 0.0 copy-done.6
  35.3 0.0 copy-done.7
  35.3 0.0 copy-start
  35.3 5.8 %copy-done = bf16[1,4096,2048]{2,1,0:T(8,128)(2,1)S(1)} copy-done((bf16[1,4096,2048]{2,1,0:T(8,128)(2,1)S(1)}, bf16[1,4096,2048]{2,1,0:T(8,128)(2,1)}, u32[]{:S(2)}) %copy-start) | copy-done | bytes 16777240
  41.1 22.9 %experts.1 = (bf16[64,4096]{1,0:T(8,128)(2,1)S(1)}, bf16[64,4096]{1,0:T(8,128)(2,1)S(1)}, bf16[64,2048]{1,0:T(8,128)(2,1)S(1)}, bf16[64,2048]{1,0:T(8,128)(2,1)S...) custom-call(s32[8]{0:T(128)S(1)} %convert_reduce_fusion.counts, ...), custom_call_target="tpu_custom_call" | custom-call | flops 4294967296 | bytes 33554432 | tf_op jit(solution)/shard_map/experts/pallas_call | solution.py:167
  64.1 1.4 %collective-permute-start.3 = (bf16[72,4096]{1,0:T(8,128)(2,1)S(1)}, bf16[72,4096]{1,0:T(8,128)(2,1)S(1)}, u32[]{:S(2)}, u32[]{:S(2)}) collective-permute-start(bf16[72,4096]{1,0:T(8,128)(2,1)S(1)} %slice.80), channel_id=1, source_target_pairs={{0,4},{4,0},{8,12},{12,8},{16,20},{20,16},{24,28},{28,24},{1,5},{5... | collective-permute-start | bytes 1769480 | tf_op jit(solution)/shard_map/ppermute | solution.py:269
  65.4 11.3 %collective-permute-done.3 = bf16[72,4096]{1,0:T(8,128)(2,1)S(1)} collective-permute-done((bf16[72,4096]{1,0:T(8,128)(2,1)S(1)}, bf16[72,4096]{1,0:T(8,128)(2,1)S(1)}, u32[]{:S(2)}, u32[]{:S(2)}) %collective-permute-start.3) | collective-permute-done | bytes 589856 | tf_op jit(solution)/shard_map/ppermute | solution.py:269
  76.8 0.1 convert_element_type.30
  76.9 0.1 slice_add_fusion
  77.1 3.1 %collective-permute-start.4 = (bf16[40,4096]{1,0:T(8,128)(2,1)S(1)}, bf16[40,4096]{1,0:T(8,128)(2,1)S(1)}, u32[]{:S(2)}, u32[]{:S(2)}) collective-permute-start(bf16[40,4096]{1,0:T(8,128)(2,1)S(1)} %pad_maximum_fusion.1), channel_id=1, source_target_pairs={{0,8},{4,12},{8,0},{12,4},{16,24},{20,28},{24,16},{28,20},{1,9},{5... | collective-permute-start | bytes 983048 | tf_op jit(solution)/shard_map/ppermute | solution.py:269
  80.3 8.0 %up_grad.1 = bf16[1,4096,2048]{2,1,0:T(8,128)(2,1)} custom-call(bf16[64,4096]{1,0:T(8,128)(2,1)S(1)} %get-tuple-element.29.left, bf16[64,2048]{1,0:T(8,128)(2,1)S(1)} %get-tuple-element.30.right), custom_call_target="tpu_custom_call" | custom-call | flops 4294967296 | bytes 33554432 | tf_op jit(solution)/shard_map/up_grad/pallas_call | solution.py:201
  88.3 0.0 collective-permute-done.4
  88.4 0.1 fusion
  88.5 3.4 %collective-permute-start.5 = (bf16[24,4096]{1,0:T(8,128)(2,1)S(1)}, bf16[24,4096]{1,0:T(8,128)(2,1)S(1)}, u32[]{:S(2)}, u32[]{:S(2)}) collective-permute-start(bf16[24,4096]{1,0:T(8,128)(2,1)S(1)} %pad_maximum_fusion.4), channel_id=1, source_target_pairs={{0,16},{4,20},{8,24},{12,28},{16,0},{20,4},{24,8},{28,12},{1,17},{... | collective-permute-start | bytes 589832 | tf_op jit(solution)/shard_map/ppermute | solution.py:269
  91.9 8.0 %down_grad.1 = bf16[1,2048,4096]{2,1,0:T(8,128)(2,1)} custom-call(bf16[64,2048]{1,0:T(8,128)(2,1)S(1)} %get-tuple-element.31.left, bf16[64,4096]{1,0:T(8,128)(2,1)S(1)} %get-tuple-element.32.right), custom_call_target="tpu_custom_call" | custom-call | flops 4294967296 | bytes 33554432 | tf_op jit(solution)/shard_map/down_grad/pallas_call | solution.py:201
  99.9 0.0 collective-permute-done.5
  99.9 0.0 copy-start.2
  100.0 0.0 copy-start.4
  100.1 1.6 %collective-permute-start.6 = (bf16[1,40,4096]{2,1,0:T(8,128)(2,1)S(1)}, bf16[1,40,4096]{2,1,0:T(8,128)(2,1)S(1)}, u32[]{:S(2)}, u32[]{:S(2)}) collective-permute-start(bf16[1,40,4096]{2,1,0:T(8,128)(2,1)S(1)} %pad_maximum_fusion.2), channel_id=1, source_target_pairs={{0,2},{1,3},{2,0},{3,1},{4,6},{5,7},{6,4},{7,5},{8,10},{9,11},{10,... | collective-permute-start | bytes 983048 | tf_op jit(solution)/shard_map/ppermute | solution.py:269
  101.6 5.6 %collective-permute-done.6 = bf16[1,40,4096]{2,1,0:T(8,128)(2,1)S(1)} collective-permute-done((bf16[1,40,4096]{2,1,0:T(8,128)(2,1)S(1)}, bf16[1,40,4096]{2,1,0:T(8,128)(2,1)S(1)}, u32[]{:S(2)}, u32[]{:S(2)}) %collective-permute-start.6) | collective-permute-done | bytes 327712 | tf_op jit(solution)/shard_map/ppermute | solution.py:269
  107.2 0.1 pad_maximum_fusion.own
  107.3 0.1 collective-permute-start.7
  107.4 0.7 maximum_select_fusion
  108.0 1.4 %collective-permute-done.7.recv = bf16[2,40,4096]{2,1,0:T(8,128)(2,1)S(1)} collective-permute-done((bf16[2,40,4096]{2,1,0:T(8,128)(2,1)S(1)}, bf16[2,40,4096]{2,1,0:T(8,128)(2,1)S(1)}, u32[]{:S(2)}, u32[]{:S(2)}) %collective-permute-start.7) | collective-permute-done | bytes 655392 | tf_op jit(solution)/shard_map/ppermute | solution.py:269
  109.4 0.0 copy-done.2
  109.4 3.9 %finish.1 = (bf16[128,4096]{1,0:T(8,128)(2,1)}, bf16[128,4096]{1,0:T(8,128)(2,1)}, f32[1,4096]{1,0:T(1,128)}, f32[1,4096]{1,0:T(1,128)}, f32[1,4096]{1,0:T(1,128)}) custom-call(bf16[2,40,4096]{2,1,0:T(8,128)(2,1)S(1)} %pad_maximum_fusion.own, bf16[2,40,4096]{2,1,0:T(8,128)(2,1)S(1)} %collective-permute-done.7.recv, f32[1,4096]{1,0:T(1,128)S(1)} %bitcast.31, ...), custom_call_target="tpu_custom_call" | custom-call | tf_op jit(solution)/shard_map/finish/pallas_call | solution.py:256
  (29 shorter events, 0.5 us)
Async XLA Ops:
  0.6 8.6 %copy-start.11 = (s32[8]{0:T(128)S(1)}, s32[8]{0:T(128)}, u32[]{:S(2)}) copy-start(s32[8]{0:T(128)} %constant.41.clone) | copy-start | bytes 100
  0.6 8.5 %copy-start.9 = (s32[1,2,32]{2,1,0:T(2,128)S(1)}, s32[1,2,32]{2,1,0:T(2,128)}, u32[]{:S(2)}) copy-start(s32[1,2,32]{2,1,0:T(2,128)} %param.17) | copy-start | bytes 772
  0.7 8.5 %copy-start.10 = (bf16[1,4096,2]{1,2,0:T(2,128)(2,1)S(1)}, bf16[1,4096,2]{1,2,0:T(2,128)(2,1)}, u32[]{:S(2)}) copy-start(bf16[1,4096,2]{1,2,0:T(2,128)(2,1)} %param.14) | copy-start | bytes 49156
  0.8 1.2 %copy-start.1 = (bf16[128,4096]{1,0:T(8,128)(2,1)S(1)}, bf16[128,4096]{1,0:T(8,128)(2,1)}, u32[]{:S(2)}) copy-start(bf16[128,4096]{1,0:T(8,128)(2,1)} %tokens.3) | copy-start | bytes 3145732
  2.0 1.2 %copy-start.3 = (bf16[128,4096]{1,0:T(8,128)(2,1)S(1)}, bf16[128,4096]{1,0:T(8,128)(2,1)}, u32[]{:S(2)}) copy-start(bf16[128,4096]{1,0:T(8,128)(2,1)} %grads.3) | copy-start | bytes 3145732
  3.2 0.7 copy-start.8
  5.0 30.3 %copy-start.5 = (f32[4096]{0:T(1024)S(1)}, f32[4096]{0:T(1024)}, u32[]{:S(2)}) copy-start(f32[4096]{0:T(1024)} %param.12) | copy-start | bytes 49156
  5.0 30.3 %copy-start.6 = (f32[4096]{0:T(1024)S(1)}, f32[4096]{0:T(1024)}, u32[]{:S(2)}) copy-start(f32[4096]{0:T(1024)} %param.13) | copy-start | bytes 49156
  5.0 30.3 %copy-start.7 = (f32[4096]{0:T(1024)S(1)}, f32[4096]{0:T(1024)}, u32[]{:S(2)}) copy-start(f32[4096]{0:T(1024)} %param.11) | copy-start | bytes 49156
  5.1 10.4 %collective-permute-start = (bf16[16,4096]{1,0:T(8,128)(2,1)S(1)}, bf16[16,4096]{1,0:T(8,128)(2,1)S(1)}, u32[]{:S(2)}, u32[]{:S(2)}) collective-permute-start(bf16[16,4096]{1,0:T(8,128)(2,1)S(1)} %get-tuple-element.23), channel_id=1, source_target_pairs={{0,16},{4,20},{8,24},{12,28},{16,0},{20,4},{24,8},{28,12},{1,17},{... | collective-permute-start | bytes 393224 | tf_op jit(solution)/shard_map/ppermute | solution.py:269
  15.5 7.6 %collective-permute-start.1 = (bf16[32,4096]{1,0:T(8,128)(2,1)S(1)}, bf16[32,4096]{1,0:T(8,128)(2,1)S(1)}, u32[]{:S(2)}, u32[]{:S(2)}) collective-permute-start(bf16[32,4096]{1,0:T(8,128)(2,1)S(1)} %pad_maximum_fusion.3), channel_id=1, source_target_pairs={{0,8},{4,12},{8,0},{12,4},{16,24},{20,28},{24,16},{28,20},{1,9},{5... | collective-permute-start | bytes 786440 | tf_op jit(solution)/shard_map/ppermute | solution.py:269
  23.1 12.3 %collective-permute-start.2 = (bf16[64,4096]{1,0:T(8,128)(2,1)S(1)}, bf16[64,4096]{1,0:T(8,128)(2,1)S(1)}, u32[]{:S(2)}, u32[]{:S(2)}) collective-permute-start(bf16[64,4096]{1,0:T(8,128)(2,1)S(1)} %constant_dynamic-update-slice_fusion.near), channel_id=1, source_target_pairs={{0,4},{4,0},{8,12},{12,8},{16,20},{20,16},{24,28},{28,24},{1,5},{5... | collective-permute-start | bytes 1572872 | tf_op jit(solution)/shard_map/ppermute | solution.py:269
  35.3 5.8 %copy-start = (bf16[1,4096,2048]{2,1,0:T(8,128)(2,1)S(1)}, bf16[1,4096,2048]{2,1,0:T(8,128)(2,1)}, u32[]{:S(2)}) copy-start(bf16[1,4096,2048]{2,1,0:T(8,128)(2,1)} %up.1) | copy-start | bytes 50331652
  64.1 12.7 %collective-permute-start.3 = (bf16[72,4096]{1,0:T(8,128)(2,1)S(1)}, bf16[72,4096]{1,0:T(8,128)(2,1)S(1)}, u32[]{:S(2)}, u32[]{:S(2)}) collective-permute-start(bf16[72,4096]{1,0:T(8,128)(2,1)S(1)} %slice.80), channel_id=1, source_target_pairs={{0,4},{4,0},{8,12},{12,8},{16,20},{20,16},{24,28},{28,24},{1,5},{5... | collective-permute-start | bytes 1769480 | tf_op jit(solution)/shard_map/ppermute | solution.py:269
  77.1 11.2 %collective-permute-start.4 = (bf16[40,4096]{1,0:T(8,128)(2,1)S(1)}, bf16[40,4096]{1,0:T(8,128)(2,1)S(1)}, u32[]{:S(2)}, u32[]{:S(2)}) collective-permute-start(bf16[40,4096]{1,0:T(8,128)(2,1)S(1)} %pad_maximum_fusion.1), channel_id=1, source_target_pairs={{0,8},{4,12},{8,0},{12,4},{16,24},{20,28},{24,16},{28,20},{1,9},{5... | collective-permute-start | bytes 983048 | tf_op jit(solution)/shard_map/ppermute | solution.py:269
  88.5 11.4 %collective-permute-start.5 = (bf16[24,4096]{1,0:T(8,128)(2,1)S(1)}, bf16[24,4096]{1,0:T(8,128)(2,1)S(1)}, u32[]{:S(2)}, u32[]{:S(2)}) collective-permute-start(bf16[24,4096]{1,0:T(8,128)(2,1)S(1)} %pad_maximum_fusion.4), channel_id=1, source_target_pairs={{0,16},{4,20},{8,24},{12,28},{16,0},{20,4},{24,8},{28,12},{1,17},{... | collective-permute-start | bytes 589832 | tf_op jit(solution)/shard_map/ppermute | solution.py:269
  99.9 9.5 %copy-start.2 = (bf16[128,4096]{1,0:T(8,128)(2,1)S(1)}, bf16[128,4096]{1,0:T(8,128)(2,1)}, u32[]{:S(2)}) copy-start(bf16[128,4096]{1,0:T(8,128)(2,1)} %tokens.3) | copy-start | bytes 3145732
  100.0 9.5 %copy-start.4 = (bf16[128,4096]{1,0:T(8,128)(2,1)S(1)}, bf16[128,4096]{1,0:T(8,128)(2,1)}, u32[]{:S(2)}) copy-start(bf16[128,4096]{1,0:T(8,128)(2,1)} %grads.3) | copy-start | bytes 3145732
  100.1 7.1 %collective-permute-start.6 = (bf16[1,40,4096]{2,1,0:T(8,128)(2,1)S(1)}, bf16[1,40,4096]{2,1,0:T(8,128)(2,1)S(1)}, u32[]{:S(2)}, u32[]{:S(2)}) collective-permute-start(bf16[1,40,4096]{2,1,0:T(8,128)(2,1)S(1)} %pad_maximum_fusion.2), channel_id=1, source_target_pairs={{0,2},{1,3},{2,0},{3,1},{4,6},{5,7},{6,4},{7,5},{8,10},{9,11},{10,... | collective-permute-start | bytes 983048 | tf_op jit(solution)/shard_map/ppermute | solution.py:269
  107.3 2.2 %collective-permute-start.7 = (bf16[2,40,4096]{2,1,0:T(8,128)(2,1)S(1)}, bf16[2,40,4096]{2,1,0:T(8,128)(2,1)S(1)}, u32[]{:S(2)}, u32[]{:S(2)}) collective-permute-start(bf16[2,40,4096]{2,1,0:T(8,128)(2,1)S(1)} %pad_maximum_fusion.own), channel_id=1, source_target_pairs={{0,1},{1,0},{2,3},{3,2},{4,5},{5,4},{6,7},{7,6},{8,9},{9,8},{10,11... | collective-permute-start | bytes 1966088 | tf_op jit(solution)/shard_map/ppermute | solution.py:269

commit v2 on v1

v2 whole, which is shorter than its diff:
```python
import functools

import jax
import jax.numpy as jnp
from jax import lax
from jax.experimental import pallas as pl
from jax.experimental.pallas import tpu as pltpu
from jax.sharding import PartitionSpec as P

MOST = 8
GROUP = 2 * MOST
PARTS = 4
SIDE = 8
GELU_C = 0.7978845608028654
MIB = 1 << 20
f32, bf16 = jnp.float32, jnp.bfloat16
WHOLE = pl.BlockSpec(memory_space=pltpu.VMEM)
SCALARS = pl.BlockSpec(memory_space=pltpu.SMEM)
ORDER = pl.BlockSpec(memory_space=pl.ANY)


def in_hbm(*arrays):
    return [pltpu.with_memory_space_constraint(array, pltpu.HBM) for array in arrays]


def start_copies(pairs, sems):
    copies = [pltpu.make_async_copy(a, b, sems.at[k]) for k, (a, b) in enumerate(pairs)]
    for copy in copies:
        copy.start()
    return copies


def dot(left, right, left_dim, right_dim):
    return lax.dot_general(
        left, right, (((left_dim,), (right_dim,)), ((), ())), preferred_element_type=f32
    )


def iota(shape, dim):
    return lax.broadcasted_iota(jnp.int32, shape, dim)


def select_body(place, picked_h, tokens_h, grads_h, own_o, other_o, ids_o, picked, tokens, grads, sems):
    tok_count = tokens.shape[0]
    pairs = [(picked_h, picked)]
    for k in range(PARTS):
        cut = pl.ds(k * (tok_count // PARTS), tok_count // PARTS)
        pairs += [(tokens_h.at[cut], tokens.at[cut]), (grads_h.at[cut], grads.at[cut])]
    copies = start_copies(pairs, sems)
    cap = picked.shape[2]
    start = place[0] * tok_count
    group = place[1]
    copies[0].wait()
    ids = picked[0].astype(f32)
    lanes, rows = iota((cap, cap), 1), iota((cap, cap), 0)
    eye = (lanes == rows).astype(f32)
    before = (rows < lanes).astype(f32)
    slot = (iota((GROUP, cap), 0) % MOST).astype(f32)
    tables = []
    for which in range(2):
        row = jnp.where(group == which, ids[0:1], ids[1:2]) - start.astype(f32)
        inside = ((row >= 0.0) & (row < float(tok_count))).astype(f32)
        inside_col = jnp.sum(eye * inside, axis=1, keepdims=True)
        local_col = jnp.sum(eye * row, axis=1, keepdims=True)
        rank = jnp.sum(before * inside_col, axis=0, keepdims=True)
        hit = jnp.where(rank == slot, 1.0, 0.0) * inside
        token_hit = (local_col == iota((cap, tok_count), 1).astype(f32)).astype(f32)
        tables.append(dot(hit, token_hit, 1, 0))
    table = jnp.concatenate(tables, axis=0).astype(bf16)
    second = (iota((2 * GROUP, 1), 0) % GROUP) >= MOST
    for copy in copies[1:]:
        copy.wait()
    rows = jnp.where(second, dot(table, grads[...], 1, 0), dot(table, tokens[...], 1, 0)).astype(bf16)
    own_o[...] = rows[:GROUP]
    other_o[...] = rows[GROUP:]
    number = (iota((SIDE, tok_count), 1) + 1).astype(bf16)
    ids_row = dot(number, table, 1, 1) - 1.0
    kind = (iota((SIDE, 2 * GROUP), 1) % GROUP) >= MOST
    want = iota((SIDE, 2 * GROUP), 0) == 1
    ids_o[...] = jnp.where(kind == want, ids_row, -1.0)


def select(place, picked, tokens, grads):
    width = tokens.shape[1]
    return pl.pallas_call(
        select_body,
        in_specs=[SCALARS] + [ORDER] * 3,
        out_specs=[WHOLE, WHOLE, WHOLE],
        scratch_shapes=[
            pltpu.VMEM(picked.shape, jnp.int32),
            pltpu.VMEM(tokens.shape, bf16),
            pltpu.VMEM(grads.shape, bf16),
            pltpu.SemaphoreType.DMA((1 + 2 * PARTS,)),
        ],
        out_shape=[
            jax.ShapeDtypeStruct((GROUP, width), bf16),
            jax.ShapeDtypeStruct((GROUP, width), bf16),
            jax.ShapeDtypeStruct((SIDE, 2 * GROUP), f32),
        ],
        compiler_params=pltpu.CompilerParams(vmem_limit_bytes=16 * MIB),
        name="select",
    )(place, *in_hbm(picked, tokens, grads))


def expert_body(
    places, counts, near_t, far_t, near_g, far_g, column, shift_h, scale_h, gate_h, up_h, down_h, _,
    hid_o, grows_o, act_o, gpre_o, eo_keep, back_keep, eo_send, back_send, side_o,
    normed_s, eo_s, back_s, weight_s, shift, scale, gate, up, down, vector_sems, up_sems, down_sems,
):
    width = hid_o.shape[1]
    blocks = len(places)
    slots, chunk = up.shape[0], up.shape[2]
    steps = up_h.shape[2] // chunk
    half = blocks // 2

    def fetch(step):
        here = pl.ds(step * chunk, chunk)
        slot = step % slots
        return (
            pltpu.make_async_copy(up_h.at[0, :, here], up.at[slot], up_sems.at[slot]),
            pltpu.make_async_copy(down_h.at[0, here, :], down.at[slot], down_sems.at[slot]),
        )

    vectors = start_copies(((shift_h, shift), (scale_h, scale), (gate_h, gate)), vector_sems)
    fetches = [fetch(step) for step in range(steps)]
    for step in range(min(slots, steps)):
        for copy in fetches[step]:
            copy.start()

    def pair(near, far, block):
        at = MOST * (block % half)
        return (near if block < half else far).at[at : at + GROUP, :]

    for copy in vectors:
        copy.wait()
    one = 1.0 + scale[...]
    place = iota((GROUP, 1), 0)
    for block in range(0, blocks, 2):
        tok = pair(near_t, far_t, block)[...].astype(f32)
        grd = pair(near_g, far_g, places[block])[...].astype(f32)
        rows = pl.ds(block * MOST, GROUP)
        limit = jnp.where(place < MOST, counts[block], counts[block + 1] + MOST)
        filled = (place < limit).astype(f32)
        centered = tok - jnp.mean(tok, axis=1, keepdims=True)
        inverse_std = lax.rsqrt(jnp.mean(centered * centered, axis=1, keepdims=True) + 1e-06)
        normed = centered * inverse_std
        normed_s[rows, :] = normed
        hidden = ((normed * one + shift[...]) * filled).astype(bf16)
        hid_o[rows, :] = hidden
        logit = jnp.sum(hidden.astype(f32) * column[...], axis=1, keepdims=True)
        weight = 1.0 / (1.0 + jnp.exp(-logit))
        weight_s[rows, :] = jnp.broadcast_to(weight, (GROUP, 128))
        grows_o[rows, :] = (weight * (gate[...] * grd)).astype(bf16)

    for step in range(steps):
        slot = step % slots
        for copy in fetches[step]:
            copy.wait()
        up_block, down_block = up[slot], down[slot]
        pre = dot(hid_o[...], up_block, 1, 0)
        grad_act = dot(grows_o[...], down_block, 1, 1)
        square = pre * pre
        tangent = jnp.tanh(GELU_C * (pre + 0.044715 * square * pre))
        act = (0.5 * pre * (1.0 + tangent)).astype(bf16)
        slope = 0.5 * (1.0 + tangent) + 0.5 * pre * (1.0 - tangent * tangent) * GELU_C * (
            1.0 + 3.0 * 0.044715 * square
        )
        grad_pre = (grad_act * slope).astype(bf16)
        here = pl.ds(step * chunk, chunk)
        act_o[:, here] = act
        gpre_o[:, here] = grad_pre
        eo, back = dot(act, down_block, 1, 0), dot(grad_pre, up_block, 1, 1)
        if step == 0:
            eo_s[...] = eo
            back_s[...] = back
        else:
            eo_s[...] += eo
            back_s[...] += back
        if step + slots < steps:
            for copy in fetches[step + slots]:
                copy.start()

    gate_v = shift_v = scale_v = router_v = jnp.zeros((1, width), f32)
    for block in range(0, blocks, 2):
        grd = pair(near_g, far_g, places[block])[...].astype(f32)
        rows = pl.ds(block * MOST, GROUP)
        weight = weight_s[rows, 0:1]
        eo = eo_s[rows, :]
        grad_logit = jnp.sum(gate[...] * grd * eo, axis=1, keepdims=True) * weight * (1.0 - weight)
        eo = weight * eo
        back = back_s[rows, :] + grad_logit * column[...]
        gate_v += jnp.sum(grd * eo, axis=0, keepdims=True)
        shift_v += jnp.sum(back, axis=0, keepdims=True)
        scale_v += jnp.sum(back * normed_s[rows, :], axis=0, keepdims=True)
        router_v += jnp.sum(grad_logit * hid_o[rows, :].astype(f32), axis=0, keepdims=True)
        for values, keep, send, at in ((eo, eo_keep, eo_send, block), (back, back_keep, back_send, places[block])):
            if at < half:
                pair(keep, None, at)[...] = values
            else:
                pair(None, send, at)[...] = values.astype(bf16)
    side = jnp.concatenate([gate_v, shift_v, scale_v, router_v, jnp.zeros((SIDE - 4, width), f32)], axis=0)
    side_o[...] = side
    eo_send[MOST * half :, :] = jnp.concatenate([side, jnp.zeros_like(side)], axis=0).astype(bf16)


def experts(places, counts, near_t, far_t, near_g, far_g, shift, scale, gate, column, up, down, behind):
    blocks = counts.shape[0]
    slot_count = blocks * MOST
    width, hid_count = up.shape[1], up.shape[2]
    chunk = min(256, hid_count)
    buffers = min(3, hid_count // chunk)
    rows = MOST * blocks // 2
    return pl.pallas_call(
        functools.partial(expert_body, places),
        in_specs=[SCALARS] + [WHOLE] * 5 + [ORDER] * 6,
        out_specs=[WHOLE] * 9,
        out_shape=[
            jax.ShapeDtypeStruct((slot_count, width), bf16),
            jax.ShapeDtypeStruct((slot_count, width), bf16),
            jax.ShapeDtypeStruct((slot_count, hid_count), bf16),
            jax.ShapeDtypeStruct((slot_count, hid_count), bf16),
            jax.ShapeDtypeStruct((rows, width), f32),
            jax.ShapeDtypeStruct((rows, width), f32),
            jax.ShapeDtypeStruct((rows + GROUP, width), bf16),
            jax.ShapeDtypeStruct((rows, width), bf16),
            jax.ShapeDtypeStruct((SIDE, width), f32),
        ],
        scratch_shapes=[pltpu.VMEM((slot_count, width), f32)] * 3
        + [pltpu.VMEM((slot_count, 128), f32)]
        + [pltpu.VMEM((1, width), f32)] * 3
        + [pltpu.VMEM((buffers, width, chunk), bf16), pltpu.VMEM((buffers, chunk, width), bf16)]
        + [pltpu.SemaphoreType.DMA((n,)) for n in (3, buffers, buffers)],
        compiler_params=pltpu.CompilerParams(vmem_limit_bytes=36 * MIB),
        cost_estimate=pl.CostEstimate(
            flops=8 * slot_count * width * hid_count, bytes_accessed=4 * width * hid_count, transcendentals=0
        ),
        name="experts",
    )(counts, near_t, far_t, near_g, far_g, column, *in_hbm(shift, scale, gate, up, down), behind)


def outer_body(left, right, *refs):
    out, done = refs[-2:]
    out[0] = dot(left[...], right[...], 0, 0).astype(bf16)
    done[...] = jnp.zeros_like(done)


def outer(left, right, behind, name, first, count, into=None):
    depth, rows = left.shape
    columns = right.shape[1]
    step = min(rows // 4, 2 * MIB // columns)
    each = rows // 4 // step
    before = [] if into is None else [into]
    return pl.pallas_call(
        outer_body,
        grid=(count * each,),
        in_specs=[pl.BlockSpec((depth, step), lambda i: (0, i + first * each)), WHOLE]
        + [ORDER] * (1 + len(before)),
        out_specs=[pl.BlockSpec((1, step, columns), lambda i: (0, i + first * each, 0)), WHOLE],
        out_shape=[jax.ShapeDtypeStruct((1, rows, columns), bf16), jax.ShapeDtypeStruct((8, 128), f32)],
        input_output_aliases={3: 0} if before else {},
        compiler_params=pltpu.CompilerParams(vmem_limit_bytes=24 * MIB),
        cost_estimate=pl.CostEstimate(
            flops=2 * depth * rows * columns * count, bytes_accessed=rows * columns * count, transcendentals=0
        ),
        name=name,
    )(left, right, behind, *before)


def fold_body(last, keep_e, keep_b, got_e, got_b, side, _, *outs):
    rows = keep_e.shape[0]
    got = got_e[...].astype(f32)
    eo = keep_e[...] + got[:rows]
    back = keep_b[...] + got_b[...].astype(f32)
    total = side[...] + got[rows:]
    outs[0][...] = total
    low, high = slice(0, rows // 2), slice(rows // 2, rows)
    if last:
        outs[1][...] = jnp.concatenate([eo[low], back[low]], axis=0)
        outs[2][...] = jnp.concatenate([eo[high], back[high], total], axis=0).astype(bf16)
    else:
        outs[1][...] = eo[low]
        outs[2][...] = back[low]
        outs[3][...] = jnp.concatenate([eo[high], total], axis=0).astype(bf16)
        outs[4][...] = back[high].astype(bf16)


def fold(keep, got, side, behind):
    rows, width = keep[0].shape
    last = rows == 2 * MOST
    sizes = [(SIDE, f32)]
    if last:
        sizes += [(rows, f32), (rows + SIDE, bf16)]
    else:
        sizes += [(rows // 2, f32)] * 2 + [(rows // 2 + SIDE, bf16), (rows // 2, bf16)]
    return pl.pallas_call(
        functools.partial(fold_body, last),
        in_specs=[WHOLE] * 5 + [ORDER],
        out_specs=[WHOLE] * len(sizes),
        out_shape=[jax.ShapeDtypeStruct((size, width), kind) for size, kind in sizes],
        compiler_params=pltpu.CompilerParams(vmem_limit_bytes=16 * MIB),
        name="fold",
    )(*keep, *got, side, behind)


def pack_body(keep, got, side, ids, _, mine_o):
    theirs = got[...].astype(f32)
    width = theirs.shape[1]
    total = side[...] + theirs[GROUP:]
    numbers = jnp.concatenate([ids[0:2], jnp.full((2, width - ids.shape[1]), -1.0, f32)], axis=1)
    mine_o[...] = jnp.concatenate(
        [keep[...], theirs[:GROUP], total[0:3], numbers, jnp.zeros((SIDE - 5, width), f32)], axis=0
    ).astype(bf16)


def pack(keep, got, side, ids, behind):
    width = keep.shape[1]
    return pl.pallas_call(
        pack_body,
        in_specs=[WHOLE] * 4 + [ORDER],
        out_specs=WHOLE,
        out_shape=jax.ShapeDtypeStruct((2 * GROUP + SIDE, width), bf16),
        compiler_params=pltpu.CompilerParams(vmem_limit_bytes=16 * MIB),
        name="pack",
    )(keep, got, side, ids, behind)


def relay_body(rows, _, rows_o):
    rows_o[...] = rows[...]


def relay(rows, behind):
    return pl.pallas_call(
        relay_body,
        in_specs=[WHOLE, ORDER],
        out_specs=WHOLE,
        out_shape=jax.ShapeDtypeStruct(rows.shape, rows.dtype),
        compiler_params=pltpu.CompilerParams(vmem_limit_bytes=16 * MIB),
        name="relay",
    )(rows, behind)


def normalize_body(tokens, normed_o, inverse_o):
    inputs = tokens[...].astype(f32)
    centered = inputs - jnp.mean(inputs, axis=1, keepdims=True)
    inverse_std = lax.rsqrt(jnp.mean(centered * centered, axis=1, keepdims=True) + 1e-06)
    normed_o[...] = centered * inverse_std
    inverse_o[...] = jnp.broadcast_to(inverse_std, inverse_o.shape)


def normalize(tokens):
    tok_count, width = tokens.shape
    step = min(tok_count, 16)
    return pl.pallas_call(
        normalize_body,
        grid=(tok_count // step,),
        in_specs=[pl.BlockSpec((step, width), lambda i: (i, 0))],
        out_specs=[pl.BlockSpec((step, width), lambda i: (i, 0)), pl.BlockSpec((step, 128), lambda i: (i, 0))],
        out_shape=[jax.ShapeDtypeStruct((tok_count, width), f32), jax.ShapeDtypeStruct((tok_count, 128), f32)],
        compiler_params=pltpu.CompilerParams(vmem_limit_bytes=16 * MIB),
        cost_estimate=pl.CostEstimate(flops=10 * tok_count * width, bytes_accessed=6 * tok_count * width, transcendentals=0),
        name="normalize",
    )(tokens)


def finish_body(
    parts, place, side, got, inverse, scale_h, gate_h, tokens_h, grads_h, normed_h, *refs
):
    pieces = refs[:-16]
    block_h, tgrad_h, gate_o, shift_o, scale_o, router_o = refs[-16:-10]
    scale, gate, tokens, grads, normed, block_s, tgrad_s, vector_sems, in_sems, out_sems = refs[-10:]
    total = tokens.shape[0]
    count = total // parts
    cuts = [pl.ds(k * count, count) for k in range(parts)]
    vectors = start_copies(((scale_h, scale), (gate_h, gate)), vector_sems)
    arrays = ((tokens_h, tokens), (grads_h, grads), (normed_h, normed))
    arrivals = [start_copies([(a.at[cut], b.at[cut]) for a, b in arrays], in_sems.at[k]) for k, cut in enumerate(cuts)]

    rows = jnp.concatenate([piece[: 2 * GROUP, :] for piece in pieces], axis=0)
    ids = [piece[2 * GROUP :, : 2 * GROUP].astype(f32) for piece in pieces]
    ids = [jnp.concatenate([each[3 + kind : 4 + kind] for each in ids], axis=1) for kind in range(2)]
    vector = sum(piece[2 * GROUP :, :].astype(f32) for piece in pieces)
    gate_o[...] = vector[0:1]
    shift_o[...] = vector[1:2]
    scale_o[...] = vector[2:3]
    own, other = side[3:4], got[...].astype(f32)[GROUP + 3 : GROUP + 4]
    first = place[1] == 0
    router_o[0:1] = jnp.where(first, own, other)
    router_o[1:2] = jnp.where(first, other, own)
    for copy in vectors:
        copy.wait()
    one = 1.0 + scale[...]
    departures = []
    for k, cut in enumerate(cuts):
        numbers = (iota((count, rows.shape[0]), 0) + k * count).astype(f32)
        table = jnp.concatenate([(numbers == each).astype(f32) for each in ids], axis=0)
        sums = dot(table.astype(bf16), rows, 1, 0)
        for copy in arrivals[k]:
            copy.wait()
        block_s[cut, :] = (tokens[cut, :].astype(f32) + gate[...] * sums[:count]).astype(bf16)
        grad_norm = sums[count:] * one
        center = jnp.mean(grad_norm, axis=1, keepdims=True)
        along = jnp.mean(grad_norm * normed[cut, :], axis=1, keepdims=True)
        tgrad_s[cut, :] = (
            grads[cut, :].astype(f32) + inverse[cut, 0:1] * (grad_norm - center - normed[cut, :] * along)
        ).astype(bf16)
        departures += start_copies(((block_s.at[cut], block_h.at[cut]), (tgrad_s.at[cut], tgrad_h.at[cut])), out_sems.at[k])
    for copy in departures:
        copy.wait()


def finish(place, side, got, pieces, scale, gate, tokens, grads, normed, inverse):
    tok_count, width = tokens.shape
    parts = 4
    vector = jax.ShapeDtypeStruct((1, width), f32)
    return pl.pallas_call(
        functools.partial(finish_body, parts),
        in_specs=[SCALARS] + [WHOLE] * 3 + [ORDER] * 5 + [WHOLE] * len(pieces),
        out_specs=[ORDER, ORDER] + [WHOLE] * 4,
        out_shape=[jax.ShapeDtypeStruct((tok_count, width), bf16)] * 2
        + [vector] * 3
        + [jax.ShapeDtypeStruct((2, width), f32)],
        scratch_shapes=[pltpu.VMEM((1, width), f32)] * 2
        + [pltpu.VMEM((tok_count, width), kind) for kind in (bf16, bf16, f32, bf16, bf16)]
        + [pltpu.SemaphoreType.DMA(shape) for shape in ((2,), (parts, 3), (parts, 2))],
        compiler_params=pltpu.CompilerParams(vmem_limit_bytes=24 * MIB),
        name="finish",
    )(place, side, got, inverse, *in_hbm(scale, gate, tokens, grads), normed, *pieces)


def swap(values, axis, mask):
    size = lax.axis_size(axis)
    return lax.ppermute(values, axis, [(i, i ^ mask) for i in range(size)])


def halvings(size):
    masks = []
    while size > 1:
        size //= 2
        masks.append(size)
    return masks


def per_device(
    tokens, ada_shift, ada_scale, ada_gate, router, expert_up, expert_down, picked_ids, out_grad
):
    tok_count, width = tokens.shape
    ctx_size, exp_size = lax.axis_size("ctx"), lax.axis_size("exp")
    ctx_masks, exp_masks = halvings(ctx_size), halvings(exp_size)
    me = lax.axis_index("ctx")
    group = me // ctx_masks[0]
    picked = picked_ids[0]
    shift, scale, gate = ada_shift[None], ada_scale[None], ada_gate[None]
    place = jnp.stack([me, group]).astype(jnp.int32)
    own, other, ids = select(place, picked_ids, tokens, out_grad)

    orders = ctx_masks[1:], ctx_masks[:0:-1]
    relative = []
    for order in orders:
        blocks = [0]
        for mask in [ctx_masks[0], *order]:
            blocks = blocks + [r ^ mask for r in blocks]
        relative.append(blocks)
    places = [relative[1].index(r) for r in relative[0]]
    sources = me ^ jnp.array(relative[0], jnp.int32)
    own_ids = jnp.where(group == 0, picked[0], picked[1])
    counts = jnp.sum((own_ids // tok_count)[None, :] == sources[:, None], axis=1).astype(jnp.int32)
    columns = router[0].astype(f32).T
    column = jnp.where(group == 0, columns[0:1], columns[1:2])

    normed, inverse = normalize(tokens)
    got = swap(other, "ctx", ctx_masks[0])
    near = [jnp.concatenate([own[cut], got[cut]], axis=0) for cut in (slice(0, MOST), slice(MOST, GROUP))]
    far = [swap(near[k], "ctx", orders[k][0]) for k in range(2)]
    for masks in zip(orders[0][1:], orders[1][1:]):
        near = [jnp.concatenate([near[k], far[k]], axis=0) for k in range(2)]
        far = [swap(near[k], "ctx", masks[k]) for k in range(2)]
    hidden, grad_rows, act, grad_pre, eo_keep, back_keep, eo_send, back_send, side = experts(
        places, counts, near[0], far[0], near[1], far[1], shift, scale, gate, column, expert_up, expert_down, inverse
    )

    rows = eo_keep.shape[0]
    keep, send = [eo_keep, back_keep], [eo_send[: rows + SIDE], back_send]
    behind = side
    for step, masks in enumerate(zip(orders[0][::-1], orders[1][::-1])):
        got = [swap(send[k], "ctx", masks[k]) for k in range(2)]
        if step == 0:
            up_grad, behind = outer(hidden, grad_pre, behind, "up_grad", 0, 3)
        elif step == 1:
            down_grad, behind = outer(act, grad_rows, behind, "down_grad", 0, 2)
        side, *rest = fold(keep, got, side, behind)
        keep, send = rest[:-2], rest[-2:]
        behind = side
    keep, send = rest
    got = swap(send, "ctx", ctx_masks[0])
    down_grad, behind = outer(act, grad_rows, behind, "down_grad", 2, 2, down_grad)
    mine = pack(keep, got, side, ids, behind)
    pieces = [mine]
    for step, mask in enumerate(exp_masks):
        come = [swap(piece, "exp", mask) for piece in pieces]
        if step == 0:
            up_grad, behind = outer(hidden, grad_pre, mine, "up_grad", 3, 1, up_grad)
            come = [relay(piece, behind) for piece in come]
        pieces = pieces + come
    block_out, tokens_grad, gate_grad, shift_grad, scale_grad, router_rows = finish(
        place, side, got, pieces, scale, gate, tokens, out_grad, normed, inverse
    )
    return (
        block_out,
        tokens_grad,
        up_grad,
        down_grad,
        router_rows.T[None],
        shift_grad[0],
        scale_grad[0],
        gate_grad[0],
    )


def solution(mesh):
    in_specs = (
        P("ctx", None),
        P(),
        P(),
        P(),
        P("exp", None, None),
        P("exp", None, "ctx"),
        P("exp", "ctx", None),
        P("exp", None, None),
        P("ctx", None),
    )
    out_specs = (
        P("ctx", None),
        P("ctx", None),
        P("exp", None, "ctx"),
        P("exp", "ctx", None),
        P("exp", None, None),
        P(),
        P(),
        P(),
    )
    return jax.shard_map(
        per_device, mesh=mesh, in_specs=in_specs, out_specs=out_specs, check_vma=False
    )
```

time: 114 us -> 89.2 us (0.78)
  waiting for transfers between devices: 42 us -> 14 us
  local copies, waits for them, and re-layouts: 9.13 us -> 1.27 us
  Pallas kernels: 43.9 us -> 51.1 us
  starting transfers between devices: 15.8 us -> 19 us
    ppermute x8 -> x13, waiting for transfers between devices: 42 us -> 14 us  [swap(): return lax.ppermute(values, axis, [(i, i ^ mask) for i in range(size)])]
    unnamed x26 -> x2, local copies, waits for them, and re-layouts: 8.96 us -> 1.22 us
    pallas_call x5 -> x12, Pallas kernels: 43.9 us -> 51.1 us  [the longest x1 21.8 us: experts(): pl.pallas_call(functools.partial(expert_body, places), in_specs=[SCALARS]...]
    ppermute x8 -> x13, starting transfers between devices: 15.8 us -> 19 us  [swap(): return lax.ppermute(values, axis, [(i, i ^ mask) for i in range(size)])]
  transfers between devices with their start and end apart: 8 -> 13, of which waited for: 6 -> 9; matrix products, arithmetic and copies ran while one was open for 1% -> 3% of each run, Pallas kernels for 14% -> 24%
where the time goes in v2:
time: 89.2 us; the launch traced here: 88.8 us
  Pallas kernels  51.1 us (57%)
  starting transfers between devices  19 us (21%)
  waiting for transfers between devices  14 us (16%)
  other arithmetic  2.49 us (3%)
  local copies, waits for them, and re-layouts  1.27 us (1%)
  between operations  0.93 us (1%)
    pallas_call x1, Pallas kernels, experts(): pl.pallas_call(functools.partial(expert_body, places), in_specs=[SCALARS]...  21.8 us
    pallas_call x4, Pallas kernels, outer(): pl.pallas_call(outer_body, grid=(count * each,), in_specs=[pl.BlockSpec((...  19.3 us
    ppermute x13, starting transfers between devices, swap(): return lax.ppermute(values, axis, [(i, i ^ mask) for i in range(size)])  19 us
    ppermute x13, waiting for transfers between devices, swap(): return lax.ppermute(values, axis, [(i, i ^ mask) for i in range(size)])  14 us
    pallas_call x1, Pallas kernels, finish(): pl.pallas_call(functools.partial(finish_body, parts), in_specs=[SCALARS]...  5.11 us
    pallas_call x1, Pallas kernels, select(): pl.pallas_call(select_body, in_specs=[SCALARS] + [ORDER] * 3, out_specs=[...  2.55 us
    pallas_call x1, Pallas kernels, normalize(): pl.pallas_call(normalize_body, grid=(tok_count // step,), in_specs=[pl.Bl...  2.06 us
  transfers between devices with their start and end apart: 13, of which 9 were waited for; matrix products, arithmetic and copies ran while one was open for 3% of the time, Pallas kernels for 24%

profile of v2, /device:TPU:0, one launch (start us, length us, event | category | flops | bytes accessed | tf_op | source)
XLA Modules:
  0.0 88.8 jit_solution(984551137011295761)
XLA Ops:
  0.6 0.1 pad_add_fusion.place
  0.7 2.6 %select.22 = (bf16[16,4096]{1,0:T(8,128)(2,1)S(1)}, bf16[16,4096]{1,0:T(8,128)(2,1)S(1)}, f32[8,32]{1,0:T(8,128)S(1)}) custom-call(s32[2]{0:T(128)S(1)} %pad_add_fusion.place, s32[1,2,32]{2,1,0:T(2,128)} %picked_h.1, bf16[128,4096]{1,0:T(8,128)(2,1)} %tokens_h.3, bf16[128,4096]{1,0:T(8,128)(2,1)} %grads_h.3), custom_call_target="tpu_custom_call" | custom-call | tf_op jit(solution)/shard_map/select/pallas_call | solution.py:85
  3.3 4.1 %collective-permute-start = (bf16[16,4096]{1,0:T(8,128)(2,1)S(1)}, bf16[16,4096]{1,0:T(8,128)(2,1)S(1)}, u32[]{:S(2)}, u32[]{:S(2)}) collective-permute-start(bf16[16,4096]{1,0:T(8,128)(2,1)S(1)} %get-tuple-element.45), channel_id=1, source_target_pairs={{0,16},{4,20},{8,24},{12,28},{16,0},{20,4},{24,8},{28,12},{1,17},{... | collective-permute-start | bytes 393224 | tf_op jit(solution)/shard_map/ppermute | solution.py:432
  7.4 0.0 copy-start
  7.4 1.2 %copy-done = bf16[128,4096]{1,0:T(8,128)(2,1)S(1)} copy-done((bf16[128,4096]{1,0:T(8,128)(2,1)S(1)}, bf16[128,4096]{1,0:T(8,128)(2,1)}, u32[]{:S(2)}) %copy-start) | copy-done | bytes 1048600
  8.6 2.1 %normalize.1 = (f32[128,4096]{1,0:T(8,128)S(1)}, f32[128,128]{1,0:T(8,128)S(1)}) custom-call(bf16[128,4096]{1,0:T(8,128)(2,1)S(1)} %copy-done), custom_call_target="tpu_custom_call" | custom-call | flops 5242880 | bytes 3145728 | tf_op jit(solution)/shard_map/normalize/pallas_call | solution.py:353
  10.7 0.7 convert_bitcast_fusion
  11.5 0.8 and_select_fusion
  12.2 1.5 %collective-permute-done = bf16[16,4096]{1,0:T(8,128)(2,1)S(1)} collective-permute-done((bf16[16,4096]{1,0:T(8,128)(2,1)S(1)}, bf16[16,4096]{1,0:T(8,128)(2,1)S(1)}, u32[]{:S(2)}, u32[]{:S(2)}) %collective-permute-start) | collective-permute-done | bytes 131104 | tf_op jit(solution)/shard_map/ppermute | solution.py:432
  13.7 1.6 %collective-permute-start.3 = (bf16[16,4096]{1,0:T(8,128)(2,1)S(1)}, bf16[16,4096]{1,0:T(8,128)(2,1)S(1)}, u32[]{:S(2)}, u32[]{:S(2)}) collective-permute-start(bf16[16,4096]{1,0:T(8,128)(2,1)S(1)} %pad_maximum_fusion.3), channel_id=1, source_target_pairs={{0,4},{4,0},{8,12},{12,8},{16,20},{20,16},{24,28},{28,24},{1,5},{5... | collective-permute-start | bytes 393224 | tf_op jit(solution)/shard_map/ppermute | solution.py:432
  15.4 0.7 collective-permute-start.1
  16.1 2.6 %collective-permute-done.3 = bf16[16,4096]{1,0:T(8,128)(2,1)S(1)} collective-permute-done((bf16[16,4096]{1,0:T(8,128)(2,1)S(1)}, bf16[16,4096]{1,0:T(8,128)(2,1)S(1)}, u32[]{:S(2)}, u32[]{:S(2)}) %collective-permute-start.3) | collective-permute-done | bytes 131104 | tf_op jit(solution)/shard_map/ppermute | solution.py:432
  18.8 1.2 %collective-permute-start.4 = (bf16[32,4096]{1,0:T(8,128)(2,1)S(1)}, bf16[32,4096]{1,0:T(8,128)(2,1)S(1)}, u32[]{:S(2)}, u32[]{:S(2)}) collective-permute-start(bf16[32,4096]{1,0:T(8,128)(2,1)S(1)} %pad_maximum_fusion.1.near_g), channel_id=1, source_target_pairs={{0,8},{4,12},{8,0},{12,4},{16,24},{20,28},{24,16},{28,20},{1,9},{5... | collective-permute-start | bytes 786440 | tf_op jit(solution)/shard_map/ppermute | solution.py:432
  20.0 0.7 collective-permute-done.1
  20.8 0.8 collective-permute-start.2
  21.6 0.7 broadcast_xor_fusion
  22.3 0.2 convert_reduce_fusion.counts
  22.5 3.6 %collective-permute-done.4.far_g = bf16[32,4096]{1,0:T(8,128)(2,1)S(1)} collective-permute-done((bf16[32,4096]{1,0:T(8,128)(2,1)S(1)}, bf16[32,4096]{1,0:T(8,128)(2,1)S(1)}, u32[]{:S(2)}, u32[]{:S(2)}) %collective-permute-start.4) | collective-permute-done | bytes 262176 | tf_op jit(solution)/shard_map/ppermute | solution.py:432
  26.0 1.2 %collective-permute-done.2.far_t = bf16[32,4096]{1,0:T(8,128)(2,1)S(1)} collective-permute-done((bf16[32,4096]{1,0:T(8,128)(2,1)S(1)}, bf16[32,4096]{1,0:T(8,128)(2,1)S(1)}, u32[]{:S(2)}, u32[]{:S(2)}) %collective-permute-start.2) | collective-permute-done | bytes 262176 | tf_op jit(solution)/shard_map/ppermute | solution.py:432
  27.2 21.8 %experts.1 = (bf16[64,4096]{1,0:T(8,128)(2,1)S(1)}, bf16[64,4096]{1,0:T(8,128)(2,1)S(1)}, bf16[64,2048]{1,0:T(8,128)(2,1)S(1)}, bf16[64,2048]{1,0:T(8,128)(2,1)S...) custom-call(s32[8]{0:T(128)S(1)} %convert_reduce_fusion.counts, ...), custom_call_target="tpu_custom_call" | custom-call | flops 4294967296 | bytes 33554432 | tf_op jit(solution)/shard_map/experts/pallas_call | solution.py:213
  49.1 1.6 %collective-permute-start.5 = (bf16[40,4096]{1,0:T(8,128)(2,1)S(1)}, bf16[40,4096]{1,0:T(8,128)(2,1)S(1)}, u32[]{:S(2)}, u32[]{:S(2)}) collective-permute-start(bf16[40,4096]{1,0:T(8,128)(2,1)S(1)} %slice.37), channel_id=1, source_target_pairs={{0,4},{4,0},{8,12},{12,8},{16,20},{20,16},{24,28},{28,24},{1,5},{5... | collective-permute-start | bytes 983048 | tf_op jit(solution)/shard_map/ppermute | solution.py:432
  50.7 0.3 collective-permute-start.6
  51.0 6.6 %up_grad.2 = (bf16[1,4096,2048]{2,1,0:T(8,128)(2,1)}, f32[8,128]{1,0:T(8,128)S(1)}) custom-call(bf16[64,4096]{1,0:T(8,128)(2,1)S(1)} %get-tuple-element.52.left, bf16[64,2048]{1,0:T(8,128)(2,1)S(1)} %get-tuple-element.53.right, f32[8,4096]{1,0:T(8,128)S(1)} %get-tuple-element.51.refs_0_.side), custom_call_target="tpu_custom_call" | custom-call | flops 3221225472 | bytes 25165824 | tf_op jit(solution)/shard_map/up_grad/pallas_call | solution.py:253
  57.6 0.0 collective-permute-done.6.got_b
  57.6 0.0 collective-permute-done.5.got_e
  57.6 0.1 fold.2
  57.7 1.4 %collective-permute-start.8 = (bf16[16,4096]{1,0:T(8,128)(2,1)S(1)}, bf16[16,4096]{1,0:T(8,128)(2,1)S(1)}, u32[]{:S(2)}, u32[]{:S(2)}) collective-permute-start(bf16[16,4096]{1,0:T(8,128)(2,1)S(1)} %get-tuple-element.58), channel_id=1, source_target_pairs={{0,4},{4,0},{8,12},{12,8},{16,20},{20,16},{24,28},{28,24},{1,5},{5... | collective-permute-start | bytes 393224 | tf_op jit(solution)/shard_map/ppermute | solution.py:432
  59.2 0.9 collective-permute-start.7
  60.0 4.7 %down_grad.2 = (bf16[1,2048,4096]{2,1,0:T(8,128)(2,1)}, f32[8,128]{1,0:T(8,128)S(1)}) custom-call(bf16[64,2048]{1,0:T(8,128)(2,1)S(1)} %get-tuple-element.60.left, bf16[64,4096]{1,0:T(8,128)(2,1)S(1)} %get-tuple-element.61.right, f32[8,4096]{1,0:T(8,128)S(1)} %get-tuple-element.59.refs_0_.side), custom_call_target="tpu_custom_call" | custom-call | flops 2147483648 | bytes 16777216 | tf_op jit(solution)/shard_map/down_grad/pallas_call | solution.py:253
  64.7 0.0 collective-permute-done.8.got_b
  64.7 0.1 collective-permute-done.7.got_e
  64.8 0.1 fold.3
  64.9 4.6 %collective-permute-start.9 = (bf16[24,4096]{1,0:T(8,128)(2,1)S(1)}, bf16[24,4096]{1,0:T(8,128)(2,1)S(1)}, u32[]{:S(2)}, u32[]{:S(2)}) collective-permute-start(bf16[24,4096]{1,0:T(8,128)(2,1)S(1)} %get-tuple-element.64), channel_id=1, source_target_pairs={{0,16},{4,20},{8,24},{12,28},{16,0},{20,4},{24,8},{28,12},{1,17},{... | collective-permute-start | bytes 589832 | tf_op jit(solution)/shard_map/ppermute | solution.py:432
  69.5 4.7 %down_grad.3 = (bf16[1,2048,4096]{2,1,0:T(8,128)(2,1)}, f32[8,128]{1,0:T(8,128)S(1)}) custom-call(bf16[64,2048]{1,0:T(8,128)(2,1)S(1)} %get-tuple-element.60.left, bf16[64,4096]{1,0:T(8,128)(2,1)S(1)} %get-tuple-element.61.right, f32[8,4096]{1,0:T(8,128)S(1)} %get-tuple-element.63.refs_0_.side, ...), custom_call_target="tpu_custom_call", output_to_operand_aliasing={{0}: (3, {})} | custom-call | flops 2147483648 | bytes 16777216 | tf_op jit(solution)/shard_map/down_grad/pallas_call | solution.py:253
  74.2 0.4 collective-permute-done.9.got
  74.6 1.6 %collective-permute-start.10 = (bf16[40,4096]{1,0:T(8,128)(2,1)S(1)}, bf16[40,4096]{1,0:T(8,128)(2,1)S(1)}, u32[]{:S(2)}, u32[]{:S(2)}) collective-permute-start(bf16[40,4096]{1,0:T(8,128)(2,1)S(1)} %pack.1.refs_0_), channel_id=1, source_target_pairs={{0,2},{1,3},{2,0},{3,1},{4,6},{5,7},{6,4},{7,5},{8,10},{9,11},{10,... | collective-permute-start | bytes 983048 | tf_op jit(solution)/shard_map/ppermute | solution.py:432
  76.2 0.0 collective-permute-start.11
  76.2 3.3 %up_grad.3 = (bf16[1,4096,2048]{2,1,0:T(8,128)(2,1)}, f32[8,128]{1,0:T(8,128)S(1)}) custom-call(bf16[64,4096]{1,0:T(8,128)(2,1)S(1)} %get-tuple-element.52.left, bf16[64,2048]{1,0:T(8,128)(2,1)S(1)} %get-tuple-element.53.right, bf16[40,4096]{1,0:T(8,128)(2,1)S(1)} %pack.1.refs_0_, ...), custom_call_target="tpu_custom_call", output_to_operand_aliasing={{0}: (3, {})} | custom-call | flops 1073741824 | bytes 8388608 | tf_op jit(solution)/shard_map/up_grad/pallas_call | solution.py:253
  79.5 2.3 %collective-permute-done.10.rows = bf16[40,4096]{1,0:T(8,128)(2,1)S(1)} collective-permute-done((bf16[40,4096]{1,0:T(8,128)(2,1)S(1)}, bf16[40,4096]{1,0:T(8,128)(2,1)S(1)}, u32[]{:S(2)}, u32[]{:S(2)}) %collective-permute-start.10) | collective-permute-done | bytes 327712 | tf_op jit(solution)/shard_map/ppermute | solution.py:432
  81.8 0.1 collective-permute-start.12
  81.9 0.0 collective-permute-done.11.refs_2_
  81.9 1.6 %collective-permute-done.12.refs_3_ = bf16[40,4096]{1,0:T(8,128)(2,1)S(1)} collective-permute-done((bf16[40,4096]{1,0:T(8,128)(2,1)S(1)}, bf16[40,4096]{1,0:T(8,128)(2,1)S(1)}, u32[]{:S(2)}, u32[]{:S(2)}) %collective-permute-start.12) | collective-permute-done | bytes 327712 | tf_op jit(solution)/shard_map/ppermute | solution.py:432
  83.5 5.1 %finish.1 = (bf16[128,4096]{1,0:T(8,128)(2,1)}, bf16[128,4096]{1,0:T(8,128)(2,1)}, f32[1,4096]{1,0:T(1,128)}, f32[1,4096]{1,0:T(1,128)}, f32[1,4096]{1,0:T(1,128)}, /*index=5*/f32[2,4096]{1,0:T(2,128)}) custom-call(s32[2]{0:T(128)S(1)} %pad_add_fusion.place, f32[8,4096]{1,0:T(8,128)S(1)} %get-tuple-element.63.refs_0_.side, ...), custom_call_target="tpu_custom_call" | custom-call | tf_op jit(solution)/shard_map/finish/pallas_call | solution.py:415
  (10 shorter events, 0.2 us)
Async XLA Ops:
  3.3 10.4 %collective-permute-start = (bf16[16,4096]{1,0:T(8,128)(2,1)S(1)}, bf16[16,4096]{1,0:T(8,128)(2,1)S(1)}, u32[]{:S(2)}, u32[]{:S(2)}) collective-permute-start(bf16[16,4096]{1,0:T(8,128)(2,1)S(1)} %get-tuple-element.45), channel_id=1, source_target_pairs={{0,16},{4,20},{8,24},{12,28},{16,0},{20,4},{24,8},{28,12},{1,17},{... | collective-permute-start | bytes 393224 | tf_op jit(solution)/shard_map/ppermute | solution.py:432
  7.4 1.2 %copy-start = (bf16[128,4096]{1,0:T(8,128)(2,1)S(1)}, bf16[128,4096]{1,0:T(8,128)(2,1)}, u32[]{:S(2)}) copy-start(bf16[128,4096]{1,0:T(8,128)(2,1)} %tokens_h.3) | copy-start | bytes 3145732
  13.7 5.0 %collective-permute-start.3 = (bf16[16,4096]{1,0:T(8,128)(2,1)S(1)}, bf16[16,4096]{1,0:T(8,128)(2,1)S(1)}, u32[]{:S(2)}, u32[]{:S(2)}) collective-permute-start(bf16[16,4096]{1,0:T(8,128)(2,1)S(1)} %pad_maximum_fusion.3), channel_id=1, source_target_pairs={{0,4},{4,0},{8,12},{12,8},{16,20},{20,16},{24,28},{28,24},{1,5},{5... | collective-permute-start | bytes 393224 | tf_op jit(solution)/shard_map/ppermute | solution.py:432
  15.4 5.4 %collective-permute-start.1 = (bf16[16,4096]{1,0:T(8,128)(2,1)S(1)}, bf16[16,4096]{1,0:T(8,128)(2,1)S(1)}, u32[]{:S(2)}, u32[]{:S(2)}) collective-permute-start(bf16[16,4096]{1,0:T(8,128)(2,1)S(1)} %pad_maximum_fusion.2), channel_id=1, source_target_pairs={{0,8},{4,12},{8,0},{12,4},{16,24},{20,28},{24,16},{28,20},{1,9},{5... | collective-permute-start | bytes 393224 | tf_op jit(solution)/shard_map/ppermute | solution.py:432
  18.8 7.2 %collective-permute-start.4 = (bf16[32,4096]{1,0:T(8,128)(2,1)S(1)}, bf16[32,4096]{1,0:T(8,128)(2,1)S(1)}, u32[]{:S(2)}, u32[]{:S(2)}) collective-permute-start(bf16[32,4096]{1,0:T(8,128)(2,1)S(1)} %pad_maximum_fusion.1.near_g), channel_id=1, source_target_pairs={{0,8},{4,12},{8,0},{12,4},{16,24},{20,28},{24,16},{28,20},{1,9},{5... | collective-permute-start | bytes 786440 | tf_op jit(solution)/shard_map/ppermute | solution.py:432
  20.8 6.4 %collective-permute-start.2 = (bf16[32,4096]{1,0:T(8,128)(2,1)S(1)}, bf16[32,4096]{1,0:T(8,128)(2,1)S(1)}, u32[]{:S(2)}, u32[]{:S(2)}) collective-permute-start(bf16[32,4096]{1,0:T(8,128)(2,1)S(1)} %pad_maximum_fusion.near_t), channel_id=1, source_target_pairs={{0,4},{4,0},{8,12},{12,8},{16,20},{20,16},{24,28},{28,24},{1,5},{5... | collective-permute-start | bytes 786440 | tf_op jit(solution)/shard_map/ppermute | solution.py:432
  49.1 8.5 %collective-permute-start.5 = (bf16[40,4096]{1,0:T(8,128)(2,1)S(1)}, bf16[40,4096]{1,0:T(8,128)(2,1)S(1)}, u32[]{:S(2)}, u32[]{:S(2)}) collective-permute-start(bf16[40,4096]{1,0:T(8,128)(2,1)S(1)} %slice.37), channel_id=1, source_target_pairs={{0,4},{4,0},{8,12},{12,8},{16,20},{20,16},{24,28},{28,24},{1,5},{5... | collective-permute-start | bytes 983048 | tf_op jit(solution)/shard_map/ppermute | solution.py:432
  50.7 6.9 %collective-permute-start.6 = (bf16[32,4096]{1,0:T(8,128)(2,1)S(1)}, bf16[32,4096]{1,0:T(8,128)(2,1)S(1)}, u32[]{:S(2)}, u32[]{:S(2)}) collective-permute-start(bf16[32,4096]{1,0:T(8,128)(2,1)S(1)} %get-tuple-element.50), channel_id=1, source_target_pairs={{0,8},{4,12},{8,0},{12,4},{16,24},{20,28},{24,16},{28,20},{1,9},{5... | collective-permute-start | bytes 786440 | tf_op jit(solution)/shard_map/ppermute | solution.py:432
  57.7 7.0 %collective-permute-start.8 = (bf16[16,4096]{1,0:T(8,128)(2,1)S(1)}, bf16[16,4096]{1,0:T(8,128)(2,1)S(1)}, u32[]{:S(2)}, u32[]{:S(2)}) collective-permute-start(bf16[16,4096]{1,0:T(8,128)(2,1)S(1)} %get-tuple-element.58), channel_id=1, source_target_pairs={{0,4},{4,0},{8,12},{12,8},{16,20},{20,16},{24,28},{28,24},{1,5},{5... | collective-permute-start | bytes 393224 | tf_op jit(solution)/shard_map/ppermute | solution.py:432
  59.2 5.7 %collective-permute-start.7 = (bf16[24,4096]{1,0:T(8,128)(2,1)S(1)}, bf16[24,4096]{1,0:T(8,128)(2,1)S(1)}, u32[]{:S(2)}, u32[]{:S(2)}) collective-permute-start(bf16[24,4096]{1,0:T(8,128)(2,1)S(1)} %get-tuple-element.57), channel_id=1, source_target_pairs={{0,8},{4,12},{8,0},{12,4},{16,24},{20,28},{24,16},{28,20},{1,9},{5... | collective-permute-start | bytes 589832 | tf_op jit(solution)/shard_map/ppermute | solution.py:432
  64.9 9.7 %collective-permute-start.9 = (bf16[24,4096]{1,0:T(8,128)(2,1)S(1)}, bf16[24,4096]{1,0:T(8,128)(2,1)S(1)}, u32[]{:S(2)}, u32[]{:S(2)}) collective-permute-start(bf16[24,4096]{1,0:T(8,128)(2,1)S(1)} %get-tuple-element.64), channel_id=1, source_target_pairs={{0,16},{4,20},{8,24},{12,28},{16,0},{20,4},{24,8},{28,12},{1,17},{... | collective-permute-start | bytes 589832 | tf_op jit(solution)/shard_map/ppermute | solution.py:432
  74.6 7.1 %collective-permute-start.10 = (bf16[40,4096]{1,0:T(8,128)(2,1)S(1)}, bf16[40,4096]{1,0:T(8,128)(2,1)S(1)}, u32[]{:S(2)}, u32[]{:S(2)}) collective-permute-start(bf16[40,4096]{1,0:T(8,128)(2,1)S(1)} %pack.1.refs_0_), channel_id=1, source_target_pairs={{0,2},{1,3},{2,0},{3,1},{4,6},{5,7},{6,4},{7,5},{8,10},{9,11},{10,... | collective-permute-start | bytes 983048 | tf_op jit(solution)/shard_map/ppermute | solution.py:432
  76.2 5.7 %collective-permute-start.11 = (bf16[40,4096]{1,0:T(8,128)(2,1)S(1)}, bf16[40,4096]{1,0:T(8,128)(2,1)S(1)}, u32[]{:S(2)}, u32[]{:S(2)}) collective-permute-start(bf16[40,4096]{1,0:T(8,128)(2,1)S(1)} %pack.1.refs_0_), channel_id=1, source_target_pairs={{0,1},{1,0},{2,3},{3,2},{4,5},{5,4},{6,7},{7,6},{8,9},{9,8},{10,11... | collective-permute-start | bytes 983048 | tf_op jit(solution)/shard_map/ppermute | solution.py:432
  81.8 1.7 %collective-permute-start.12 = (bf16[40,4096]{1,0:T(8,128)(2,1)S(1)}, bf16[40,4096]{1,0:T(8,128)(2,1)S(1)}, u32[]{:S(2)}, u32[]{:S(2)}) collective-permute-start(bf16[40,4096]{1,0:T(8,128)(2,1)S(1)} %relay.1.refs_1_), channel_id=1, source_target_pairs={{0,1},{1,0},{2,3},{3,2},{4,5},{5,4},{6,7},{7,6},{8,9},{9,8},{10,11... | collective-permute-start | bytes 983048 | tf_op jit(solution)/shard_map/ppermute | solution.py:432

commit v3 on v2

--- a/solution.py
+++ b/solution.py
@@ -11,8 +11,12 @@
 GROUP = 2 * MOST
 PARTS = 4
 SIDE = 8
+LANES = 128
 GELU_C = 0.7978845608028654
 MIB = 1 << 20
+CHUNK = 256
+SHARE = MIB // 2
+EARLY = (1, 1, 2)
 f32, bf16 = jnp.float32, jnp.bfloat16
 WHOLE = pl.BlockSpec(memory_space=pltpu.VMEM)
 SCALARS = pl.BlockSpec(memory_space=pltpu.SMEM)
@@ -21,6 +25,31 @@
 
 def in_hbm(*arrays):
     return [pltpu.with_memory_space_constraint(array, pltpu.HBM) for array in arrays]
+
+
+def fold_vector(row):
+    return jnp.concatenate([row[:, k : k + LANES] for k in range(0, row.shape[1], LANES)], axis=0)
+
+
+def spread(vector, rows):
+    depth = vector.shape[0]
+    if rows > depth:
+        return jnp.concatenate([vector, jnp.zeros((rows - depth, LANES), f32)], axis=0)
+    return jnp.concatenate([vector[k : k + rows] for k in range(0, depth, rows)], axis=1)
+
+
+def spread_columns(width, rows):
+    return LANES * max(1, width // LANES // rows)
+
+
+def unspread(columns, width):
+    rows = columns.shape[0]
+    depth, each = width // LANES, spread_columns(width, rows)
+    vectors = []
+    for at in range(0, columns.shape[1], each):
+        cuts = [columns[:, k : k + LANES] for k in range(at, at + each, LANES)]
+        vectors.append(jnp.concatenate(cuts, axis=0)[:depth])
+    return vectors
 
 
 def start_copies(pairs, sems):
@@ -102,38 +131,80 @@
     )(place, *in_hbm(picked, tokens, grads))
 
 
+def fetch(up_h, down_h, up, down, sems, first, count):
+    pairs = []
+    for k in range(count):
+        here = pl.ds((first + k) * CHUNK, CHUNK)
+        pairs += [(up_h.at[0, :, here], up.at[k]), (down_h.at[0, here, :], down.at[k])]
+    return start_copies(pairs, sems)
+
+
+def bring_body(first, up_h, down_h, _, up_o, down_o, done, sems):
+    copies = fetch(up_h, down_h, up_o, down_o, sems, first, up_o.shape[0])
+    done[...] = jnp.zeros_like(done)
+    for copy in copies:
+        copy.wait()
+
+
+def bring(up, down, behind, first, count):
+    width = up.shape[1]
+    return pl.pallas_call(
+        functools.partial(bring_body, first),
+        in_specs=[ORDER] * 3,
+        out_specs=[WHOLE] * 3,
+        out_shape=[
+            pltpu.VMEM((count, width, CHUNK), bf16),
+            pltpu.VMEM((count, CHUNK, width), bf16),
+            jax.ShapeDtypeStruct((8, 128), f32),
+        ],
+        scratch_shapes=[pltpu.SemaphoreType.DMA((2 * count,))],
+        compiler_params=pltpu.CompilerParams(vmem_limit_bytes=8 * MIB),
+        cost_estimate=pl.CostEstimate(flops=0, bytes_accessed=4 * count * width * CHUNK, transcendentals=0),
+        name="bring",
+    )(*in_hbm(up, down), behind)
+
+
+def join_body(first, near_t, near_g, far_t, far_g, _, tokens_o, grads_o):
+    if first:
+        rows = [ref[...].astype(f32) for ref in (near_t, far_t)]
+        tokens_o[...] = jnp.concatenate([r[:MOST] for r in rows], axis=0).astype(bf16)
+        grads_o[...] = jnp.concatenate([r[MOST:] for r in rows], axis=0).astype(bf16)
+    else:
+        tokens_o[...] = jnp.concatenate([near_t[...], far_t[...]], axis=0)
+        grads_o[...] = jnp.concatenate([near_g[...], far_g[...]], axis=0)
+
+
+def join(first, near, far, behind):
+    rows, width = near[0].shape
+    rows = rows if first else 2 * rows
+    return pl.pallas_call(
+        functools.partial(join_body, first),
+        in_specs=[WHOLE] * 4 + [ORDER],
+        out_specs=[WHOLE] * 2,
+        out_shape=[jax.ShapeDtypeStruct((rows, width), bf16)] * 2,
+        compiler_params=pltpu.CompilerParams(vmem_limit_bytes=8 * MIB),
+        name="join",
+    )(*near, *far, behind)
+
+
 def expert_body(
-    places, counts, near_t, far_t, near_g, far_g, column, shift_h, scale_h, gate_h, up_h, down_h, _,
-    hid_o, grows_o, act_o, gpre_o, eo_keep, back_keep, eo_send, back_send, side_o,
-    normed_s, eo_s, back_s, weight_s, shift, scale, gate, up, down, vector_sems, up_sems, down_sems,
+    places, counts, near_t, far_t, near_g, far_g, column, shift, one, gate, up_h, down_h, *refs
 ):
+    early, refs = refs[:-16], refs[-16:]
+    hid_o, grows_o, act_o, gpre_o, eo_keep, back_keep, eo_send, back_send, side_o = refs[:9]
+    normed_s, eo_s, back_s, weight_s, up_s, down_s, sems = refs[9:]
     width = hid_o.shape[1]
     blocks = len(places)
-    slots, chunk = up.shape[0], up.shape[2]
+    half = blocks // 2
+    chunk = up_s.shape[2]
+    at_hand = [(up.at[k], down.at[k]) for up, down in zip(early[::2], early[1::2]) for k in range(up.shape[0])]
     steps = up_h.shape[2] // chunk
-    half = blocks // 2
-
-    def fetch(step):
-        here = pl.ds(step * chunk, chunk)
-        slot = step % slots
-        return (
-            pltpu.make_async_copy(up_h.at[0, :, here], up.at[slot], up_sems.at[slot]),
-            pltpu.make_async_copy(down_h.at[0, here, :], down.at[slot], down_sems.at[slot]),
-        )
-
-    vectors = start_copies(((shift_h, shift), (scale_h, scale), (gate_h, gate)), vector_sems)
-    fetches = [fetch(step) for step in range(steps)]
-    for step in range(min(slots, steps)):
-        for copy in fetches[step]:
-            copy.start()
+    late = fetch(up_h, down_h, up_s, down_s, sems, len(at_hand), steps - len(at_hand))
 
     def pair(near, far, block):
         at = MOST * (block % half)
         return (near if block < half else far).at[at : at + GROUP, :]
 
-    for copy in vectors:
-        copy.wait()
-    one = 1.0 + scale[...]
     place = iota((GROUP, 1), 0)
     for block in range(0, blocks, 2):
         tok = pair(near_t, far_t, block)[...].astype(f32)
@@ -145,7 +216,7 @@
         inverse_std = lax.rsqrt(jnp.mean(centered * centered, axis=1, keepdims=True) + 1e-06)
         normed = centered * inverse_std
         normed_s[rows, :] = normed
-        hidden = ((normed * one + shift[...]) * filled).astype(bf16)
+        hidden = ((normed * one[...] + shift[...]) * filled).astype(bf16)
         hid_o[rows, :] = hidden
         logit = jnp.sum(hidden.astype(f32) * column[...], axis=1, keepdims=True)
         weight = 1.0 / (1.0 + jnp.exp(-logit))
@@ -153,10 +224,14 @@
         grows_o[rows, :] = (weight * (gate[...] * grd)).astype(bf16)
 
     for step in range(steps):
-        slot = step % slots
-        for copy in fetches[step]:
-            copy.wait()
-        up_block, down_block = up[slot], down[slot]
+        here = pl.ds(step * chunk, chunk)
+        if step < len(at_hand):
+            up_block, down_block = [ref[...] for ref in at_hand[step]]
+        else:
+            k = step - len(at_hand)
+            late[2 * k].wait()
+            late[2 * k + 1].wait()
+            up_block, down_block = up_s[k], down_s[k]
         pre = dot(hid_o[...], up_block, 1, 0)
         grad_act = dot(grows_o[...], down_block, 1, 1)
         square = pre * pre
@@ -166,7 +241,6 @@
             1.0 + 3.0 * 0.044715 * square
         )
         grad_pre = (grad_act * slope).astype(bf16)
-        here = pl.ds(step * chunk, chunk)
         act_o[:, here] = act
         gpre_o[:, here] = grad_pre
         eo, back = dot(act, down_block, 1, 0), dot(grad_pre, up_block, 1, 1)
@@ -176,9 +250,6 @@
         else:
             eo_s[...] += eo
             back_s[...] += back
-        if step + slots < steps:
-            for copy in fetches[step + slots]:
-                copy.start()
 
     gate_v = shift_v = scale_v = router_v = jnp.zeros((1, width), f32)
     for block in range(0, blocks, 2):
@@ -197,22 +268,24 @@
             if at < half:
                 pair(keep, None, at)[...] = values
             else:
-                pair(None, send, at)[...] = values.astype(bf16)
-    side = jnp.concatenate([gate_v, shift_v, scale_v, router_v, jnp.zeros((SIDE - 4, width), f32)], axis=0)
-    side_o[...] = side
-    eo_send[MOST * half :, :] = jnp.concatenate([side, jnp.zeros_like(side)], axis=0).astype(bf16)
-
-
-def experts(places, counts, near_t, far_t, near_g, far_g, shift, scale, gate, column, up, down, behind):
+                here = MOST * (at % half)
+                send[here : here + GROUP, :width] = values.astype(bf16)
+    sums = [fold_vector(row) for row in (gate_v, shift_v, scale_v, router_v)]
+    side_o[...] = jnp.concatenate(sums, axis=0)
+    rows = eo_send.shape[0]
+    eo_send[:, width:] = jnp.concatenate([spread(v, rows) for v in sums[:2]], axis=1).astype(bf16)
+    back_send[:, width:] = jnp.concatenate([spread(v, rows) for v in sums[2:]], axis=1).astype(bf16)
+
+
+def experts(places, counts, near_t, far_t, near_g, far_g, shift, one, gate, column, up, down, early):
     blocks = counts.shape[0]
     slot_count = blocks * MOST
     width, hid_count = up.shape[1], up.shape[2]
-    chunk = min(256, hid_count)
-    buffers = min(3, hid_count // chunk)
+    late = max(1, hid_count // CHUNK - sum(part.shape[0] for part in early[::2]))
     rows = MOST * blocks // 2
     return pl.pallas_call(
         functools.partial(expert_body, places),
-        in_specs=[SCALARS] + [WHOLE] * 5 + [ORDER] * 6,
+        in_specs=[SCALARS] + [WHOLE] * 8 + [ORDER] * 2 + [WHOLE] * len(early),
         out_specs=[WHOLE] * 9,
         out_shape=[
             jax.ShapeDtypeStruct((slot_count, width), bf16),
@@ -221,42 +294,51 @@
             jax.ShapeDtypeStruct((slot_count, hid_count), bf16),
             jax.ShapeDtypeStruct((rows, width), f32),
             jax.ShapeDtypeStruct((rows, width), f32),
-            jax.ShapeDtypeStruct((rows + GROUP, width), bf16),
-            jax.ShapeDtypeStruct((rows, width), bf16),
-            jax.ShapeDtypeStruct((SIDE, width), f32),
+            jax.ShapeDtypeStruct((rows, width + 2 * spread_columns(width, rows)), bf16),
+            jax.ShapeDtypeStruct((rows, width + 2 * spread_columns(width, rows)), bf16),
+            jax.ShapeDtypeStruct((4 * width // LANES, LANES), f32),
         ],
         scratch_shapes=[pltpu.VMEM((slot_count, width), f32)] * 3
         + [pltpu.VMEM((slot_count, 128), f32)]
-        + [pltpu.VMEM((1, width), f32)] * 3
-        + [pltpu.VMEM((buffers, width, chunk), bf16), pltpu.VMEM((buffers, chunk, width), bf16)]
-        + [pltpu.SemaphoreType.DMA((n,)) for n in (3, buffers, buffers)],
-        compiler_params=pltpu.CompilerParams(vmem_limit_bytes=36 * MIB),
+        + [pltpu.VMEM((late, width, CHUNK), bf16), pltpu.VMEM((late, CHUNK, width), bf16)]
+        + [pltpu.SemaphoreType.DMA((2 * late,))],
+        compiler_params=pltpu.CompilerParams(vmem_limit_bytes=(12 * max(1, slot_count // 64) + 4 * late) * MIB),
         cost_estimate=pl.CostEstimate(
             flops=8 * slot_count * width * hid_count, bytes_accessed=4 * width * hid_count, transcendentals=0
         ),
         name="experts",
-    )(counts, near_t, far_t, near_g, far_g, column, *in_hbm(shift, scale, gate, up, down), behind)
-
-
-def outer_body(left, right, *refs):
-    out, done = refs[-2:]
-    out[0] = dot(left[...], right[...], 0, 0).astype(bf16)
+    )(counts, near_t, far_t, near_g, far_g, column, shift, one, gate, *in_hbm(up, down), *early)
+
+
+def outer_body(step, left, right, *refs):
+    out_h, done, out, sems = refs[-4:]
     done[...] = jnp.zeros_like(done)
+    first = refs[-5]
+    copies = []
+    for k in range(out.shape[0] // step):
+        here = pl.ds(k * step, step)
+        out[here, :] = dot(left[:, first + k * step : first + (k + 1) * step], right[...], 0, 0).astype(bf16)
+        copies += start_copies([(out.at[here], out_h.at[0, pl.ds(first + k * step, step)])], sems.at[pl.ds(k, 1)])
+    for copy in copies:
+        copy.wait()
 
 
 def outer(left, right, behind, name, first, count, into=None):
     depth, rows = left.shape
     columns = right.shape[1]
-    step = min(rows // 4, 2 * MIB // columns)
-    each = rows // 4 // step
+    share = count * rows // 4
+    step = min(rows // 4, SHARE // columns)
     before = [] if into is None else [into]
-    return pl.pallas_call(
-        outer_body,
-        grid=(count * each,),
-        in_specs=[pl.BlockSpec((depth, step), lambda i: (0, i + first * each)), WHOLE]
-        + [ORDER] * (1 + len(before)),
-        out_specs=[pl.BlockSpec((1, step, columns), lambda i: (0, i + first * each, 0)), WHOLE],
+
+    def body(left, right, _, *refs):
+        outer_body(step, left, right, first * rows // 4, *refs[-4:])
+
+    return pl.pallas_call(
+        body,
+        in_specs=[WHOLE] * 2 + [ORDER] * (1 + len(before)),
+        out_specs=[ORDER, WHOLE],
         out_shape=[jax.ShapeDtypeStruct((1, rows, columns), bf16), jax.ShapeDtypeStruct((8, 128), f32)],
+        scratch_shapes=[pltpu.VMEM((share, columns), bf16), pltpu.SemaphoreType.DMA((share // step,))],
         input_output_aliases={3: 0} if before else {},
         compiler_params=pltpu.CompilerParams(vmem_limit_bytes=24 * MIB),
         cost_estimate=pl.CostEstimate(
@@ -267,58 +349,65 @@
 
 
 def fold_body(last, keep_e, keep_b, got_e, got_b, side, _, *outs):
-    rows = keep_e.shape[0]
-    got = got_e[...].astype(f32)
-    eo = keep_e[...] + got[:rows]
-    back = keep_b[...] + got_b[...].astype(f32)
-    total = side[...] + got[rows:]
-    outs[0][...] = total
+    rows, width = keep_e.shape
+    depth = width // LANES
+    got = [got_e[...].astype(f32), got_b[...].astype(f32)]
+    eo = keep_e[...] + got[0][:, :width]
+    back = keep_b[...] + got[1][:, :width]
+    theirs = unspread(got[0][:, width:], width) + unspread(got[1][:, width:], width)
+    sums = [side[k * depth : (k + 1) * depth] + v for k, v in enumerate(theirs)]
+    outs[0][...] = jnp.concatenate(sums, axis=0)
     low, high = slice(0, rows // 2), slice(rows // 2, rows)
     if last:
         outs[1][...] = jnp.concatenate([eo[low], back[low]], axis=0)
-        outs[2][...] = jnp.concatenate([eo[high], back[high], total], axis=0).astype(bf16)
+        send = jnp.concatenate([eo[high], back[high]], axis=0)
+        outs[2][...] = jnp.concatenate([send] + [spread(v, rows) for v in sums], axis=1).astype(bf16)
     else:
         outs[1][...] = eo[low]
         outs[2][...] = back[low]
-        outs[3][...] = jnp.concatenate([eo[high], total], axis=0).astype(bf16)
-        outs[4][...] = back[high].astype(bf16)
+        outs[3][...] = jnp.concatenate([eo[high]] + [spread(v, rows // 2) for v in sums[:2]], axis=1).astype(bf16)
+        outs[4][...] = jnp.concatenate([back[high]] + [spread(v, rows // 2) for v in sums[2:]], axis=1).astype(bf16)
 
 
 def fold(keep, got, side, behind):
     rows, width = keep[0].shape
     last = rows == 2 * MOST
-    sizes = [(SIDE, f32)]
+    shapes = [(side.shape, f32)]
     if last:
-        sizes += [(rows, f32), (rows + SIDE, bf16)]
+        shapes += [((rows, width), f32), ((rows, width + 4 * spread_columns(width, rows)), bf16)]
     else:
-        sizes += [(rows // 2, f32)] * 2 + [(rows // 2 + SIDE, bf16), (rows // 2, bf16)]
+        wide = width + 2 * spread_columns(width, rows // 2)
+        shapes += [((rows // 2, width), f32)] * 2 + [((rows // 2, wide), bf16)] * 2
     return pl.pallas_call(
         functools.partial(fold_body, last),
         in_specs=[WHOLE] * 5 + [ORDER],
-        out_specs=[WHOLE] * len(sizes),
-        out_shape=[jax.ShapeDtypeStruct((size, width), kind) for size, kind in sizes],
+        out_specs=[WHOLE] * len(shapes),
+        out_shape=[jax.ShapeDtypeStruct(shape, kind) for shape, kind in shapes],
         compiler_params=pltpu.CompilerParams(vmem_limit_bytes=16 * MIB),
         name="fold",
     )(*keep, *got, side, behind)
 
 
 def pack_body(keep, got, side, ids, _, mine_o):
+    width = keep.shape[1]
+    depth = width // LANES
     theirs = got[...].astype(f32)
-    width = theirs.shape[1]
-    total = side[...] + theirs[GROUP:]
-    numbers = jnp.concatenate([ids[0:2], jnp.full((2, width - ids.shape[1]), -1.0, f32)], axis=1)
-    mine_o[...] = jnp.concatenate(
-        [keep[...], theirs[:GROUP], total[0:3], numbers, jnp.zeros((SIDE - 5, width), f32)], axis=0
-    ).astype(bf16)
+    sums = [side[k * depth : (k + 1) * depth] + v for k, v in enumerate(unspread(theirs[:, width:], width)[:3])]
+    rows = mine_o.shape[0]
+    numbers = jnp.concatenate([ids[...], jnp.full((SIDE, LANES - ids.shape[1]), -1.0, f32)], axis=1)
+    numbers = jnp.concatenate([numbers, jnp.zeros((rows - SIDE, LANES), f32)], axis=0)
+    mine = jnp.concatenate([keep[...], theirs[:, :width]], axis=0)
+    mine_o[...] = jnp.concatenate([mine] + [spread(v, rows) for v in sums] + [numbers], axis=1).astype(bf16)
 
 
 def pack(keep, got, side, ids, behind):
     width = keep.shape[1]
+    rows = 2 * GROUP
     return pl.pallas_call(
         pack_body,
         in_specs=[WHOLE] * 4 + [ORDER],
         out_specs=WHOLE,
-        out_shape=jax.ShapeDtypeStruct((2 * GROUP + SIDE, width), bf16),
+        out_shape=jax.ShapeDtypeStruct((rows, width + 3 * spread_columns(width, rows) + LANES), bf16),
         compiler_params=pltpu.CompilerParams(vmem_limit_bytes=16 * MIB),
         name="pack",
     )(keep, got, side, ids, behind)
@@ -339,65 +428,73 @@
     )(rows, behind)
 
 
-def normalize_body(tokens, normed_o, inverse_o):
+def normalize_body(tokens, grads, shift, scale, gate, normed_o, inverse_o, tokens_o, grads_o, shift_o, one_o, gate_o):
     inputs = tokens[...].astype(f32)
     centered = inputs - jnp.mean(inputs, axis=1, keepdims=True)
     inverse_std = lax.rsqrt(jnp.mean(centered * centered, axis=1, keepdims=True) + 1e-06)
     normed_o[...] = centered * inverse_std
     inverse_o[...] = jnp.broadcast_to(inverse_std, inverse_o.shape)
-
-
-def normalize(tokens):
+    tokens_o[...] = tokens[...]
+    grads_o[...] = grads[...]
+    shift_o[...] = shift[...]
+    one_o[...] = 1.0 + scale[...]
+    gate_o[...] = gate[...]
+
+
+def normalize(tokens, grads, shift, scale, gate):
     tok_count, width = tokens.shape
-    step = min(tok_count, 16)
+    step = min(tok_count, 32)
+    wide = pl.BlockSpec((step, width), lambda i: (i, 0))
+    narrow = pl.BlockSpec((step, 128), lambda i: (i, 0))
+    line = pl.BlockSpec((1, width), lambda i: (0, 0))
     return pl.pallas_call(
         normalize_body,
         grid=(tok_count // step,),
-        in_specs=[pl.BlockSpec((step, width), lambda i: (i, 0))],
-        out_specs=[pl.BlockSpec((step, width), lambda i: (i, 0)), pl.BlockSpec((step, 128), lambda i: (i, 0))],
-        out_shape=[jax.ShapeDtypeStruct((tok_count, width), f32), jax.ShapeDtypeStruct((tok_count, 128), f32)],
+        in_specs=[wide, wide, line, line, line],
+        out_specs=[wide, narrow, wide, wide, line, line, line],
+        out_shape=[
+            jax.ShapeDtypeStruct((tok_count, width), f32),
+            jax.ShapeDtypeStruct((tok_count, 128), f32),
+            jax.ShapeDtypeStruct((tok_count, width), bf16),
+            jax.ShapeDtypeStruct((tok_count, width), bf16),
+        ]
+        + [jax.ShapeDtypeStruct((1, width), f32)] * 3,
         compiler_params=pltpu.CompilerParams(vmem_limit_bytes=16 * MIB),
         cost_estimate=pl.CostEstimate(flops=10 * tok_count * width, bytes_accessed=6 * tok_count * width, transcendentals=0),
         name="normalize",
-    )(tokens)
+    )(*in_hbm(tokens, grads, shift, scale, gate))
 
 
 def finish_body(
-    parts, place, side, got, inverse, scale_h, gate_h, tokens_h, grads_h, normed_h, *refs
+    parts, place, side, got, inverse, tokens, grads, normed, one, gate, *refs
 ):
-    pieces = refs[:-16]
-    block_h, tgrad_h, gate_o, shift_o, scale_o, router_o = refs[-16:-10]
-    scale, gate, tokens, grads, normed, block_s, tgrad_s, vector_sems, in_sems, out_sems = refs[-10:]
+    pieces = refs[:-14]
+    block_h, tgrad_h, gate_h, shift_h, scale_h, router_h = refs[-14:-8]
+    gate_s, shift_s, scale_s, router_s, block_s, tgrad_s, vector_sems, out_sems = refs[-8:]
     total = tokens.shape[0]
     count = total // parts
     cuts = [pl.ds(k * count, count) for k in range(parts)]
-    vectors = start_copies(((scale_h, scale), (gate_h, gate)), vector_sems)
-    arrays = ((tokens_h, tokens), (grads_h, grads), (normed_h, normed))
-    arrivals = [start_copies([(a.at[cut], b.at[cut]) for a, b in arrays], in_sems.at[k]) for k, cut in enumerate(cuts)]
-
-    rows = jnp.concatenate([piece[: 2 * GROUP, :] for piece in pieces], axis=0)
-    ids = [piece[2 * GROUP :, : 2 * GROUP].astype(f32) for piece in pieces]
-    ids = [jnp.concatenate([each[3 + kind : 4 + kind] for each in ids], axis=1) for kind in range(2)]
-    vector = sum(piece[2 * GROUP :, :].astype(f32) for piece in pieces)
-    gate_o[...] = vector[0:1]
-    shift_o[...] = vector[1:2]
-    scale_o[...] = vector[2:3]
-    own, other = side[3:4], got[...].astype(f32)[GROUP + 3 : GROUP + 4]
+    width = tokens.shape[1]
+    depth = width // LANES
+    rows = jnp.concatenate([piece[:, :width] for piece in pieces], axis=0)
+    ids = [piece[:, piece.shape[1] - LANES :].astype(f32)[:, : 2 * GROUP] for piece in pieces]
+    ids = [jnp.concatenate([each[kind : 1 + kind] for each in ids], axis=1) for kind in range(2)]
+    vector = sum(piece[:, width : piece.shape[1] - LANES].astype(f32) for piece in pieces)
+    gate_s[...], shift_s[...], scale_s[...] = unspread(vector, width)
+    own = side[3 * depth :]
+    other = unspread(got[...].astype(f32)[:, width:], width)[3]
     first = place[1] == 0
-    router_o[0:1] = jnp.where(first, own, other)
-    router_o[1:2] = jnp.where(first, other, own)
-    for copy in vectors:
-        copy.wait()
-    one = 1.0 + scale[...]
-    departures = []
+    for k, row in enumerate((jnp.where(first, own, other), jnp.where(first, other, own))):
+        router_s[k : k + 1] = jnp.concatenate([row[at : at + 1] for at in range(depth)], axis=1)
+    departures = start_copies(
+        ((gate_s, gate_h), (shift_s, shift_h), (scale_s, scale_h), (router_s, router_h)), vector_sems
+    )
     for k, cut in enumerate(cuts):
         numbers = (iota((count, rows.shape[0]), 0) + k * count).astype(f32)
         table = jnp.concatenate([(numbers == each).astype(f32) for each in ids], axis=0)
         sums = dot(table.astype(bf16), rows, 1, 0)
-        for copy in arrivals[k]:
-            copy.wait()
         block_s[cut, :] = (tokens[cut, :].astype(f32) + gate[...] * sums[:count]).astype(bf16)
-        grad_norm = sums[count:] * one
+        grad_norm = sums[count:] * one[...]
         center = jnp.mean(grad_norm, axis=1, keepdims=True)
         along = jnp.mean(grad_norm * normed[cut, :], axis=1, keepdims=True)
         tgrad_s[cut, :] = (
@@ -408,23 +505,24 @@
         copy.wait()
 
 
-def finish(place, side, got, pieces, scale, gate, tokens, grads, normed, inverse):
+def finish(place, side, got, pieces, one, gate, tokens, grads, normed, inverse):
     tok_count, width = tokens.shape
     parts = 4
-    vector = jax.ShapeDtypeStruct((1, width), f32)
+    vector = jax.ShapeDtypeStruct((width // LANES, LANES), f32)
     return pl.pallas_call(
         functools.partial(finish_body, parts),
-        in_specs=[SCALARS] + [WHOLE] * 3 + [ORDER] * 5 + [WHOLE] * len(pieces),
-        out_specs=[ORDER, ORDER] + [WHOLE] * 4,
+        in_specs=[SCALARS] + [WHOLE] * (8 + len(pieces)),
+        out_specs=[ORDER] * 6,
         out_shape=[jax.ShapeDtypeStruct((tok_count, width), bf16)] * 2
         + [vector] * 3
         + [jax.ShapeDtypeStruct((2, width), f32)],
-        scratch_shapes=[pltpu.VMEM((1, width), f32)] * 2
-        + [pltpu.VMEM((tok_count, width), kind) for kind in (bf16, bf16, f32, bf16, bf16)]
-        + [pltpu.SemaphoreType.DMA(shape) for shape in ((2,), (parts, 3), (parts, 2))],
+        scratch_shapes=[pltpu.VMEM(vector.shape, f32)] * 3
+        + [pltpu.VMEM((2, width), f32)]
+        + [pltpu.VMEM((tok_count, width), kind) for kind in (bf16, bf16)]
+        + [pltpu.SemaphoreType.DMA(shape) for shape in ((4,), (parts, 2))],
         compiler_params=pltpu.CompilerParams(vmem_limit_bytes=24 * MIB),
         name="finish",
-    )(place, side, got, inverse, *in_hbm(scale, gate, tokens, grads), normed, *pieces)
+    )(place, side, got, inverse, tokens, grads, normed, one, gate, *pieces)
 
 
 def swap(values, axis, mask):
@@ -467,19 +565,34 @@
     columns = router[0].astype(f32).T
     column = jnp.where(group == 0, columns[0:1], columns[1:2])
 
-    normed, inverse = normalize(tokens)
+    normed, inverse, near_tokens, near_grads, shift, one, gate = normalize(tokens, out_grad, shift, scale, gate)
+    early, brought, behind = [], 0, own
+
+    def bring_some(step):
+        nonlocal brought, behind
+        count = min(EARLY[step] if step < len(EARLY) else 0, expert_up.shape[2] // CHUNK - brought)
+        if count > 0:
+            *weights, behind = bring(expert_up, expert_down, behind, brought, count)
+            early.extend(weights)
+            brought += count
+
     got = swap(other, "ctx", ctx_masks[0])
-    near = [jnp.concatenate([own[cut], got[cut]], axis=0) for cut in (slice(0, MOST), slice(MOST, GROUP))]
+    bring_some(0)
+    near = join(True, [own, own], [got, got], behind)
     far = [swap(near[k], "ctx", orders[k][0]) for k in range(2)]
-    for masks in zip(orders[0][1:], orders[1][1:]):
-        near = [jnp.concatenate([near[k], far[k]], axis=0) for k in range(2)]
+    for step, masks in enumerate(zip(orders[0][1:], orders[1][1:])):
+        behind = near[0]
+        bring_some(1 + step)
+        near = join(False, near, far, behind)
         far = [swap(near[k], "ctx", masks[k]) for k in range(2)]
+    behind = near[0]
+    bring_some(len(orders[0]))
     hidden, grad_rows, act, grad_pre, eo_keep, back_keep, eo_send, back_send, side = experts(
-        places, counts, near[0], far[0], near[1], far[1], shift, scale, gate, column, expert_up, expert_down, inverse
+        places, counts, near[0], far[0], near[1], far[1], shift, one, gate, column, expert_up, expert_down, early
     )
 
     rows = eo_keep.shape[0]
-    keep, send = [eo_keep, back_keep], [eo_send[: rows + SIDE], back_send]
+    keep, send = [eo_keep, back_keep], [eo_send, back_send]
     behind = side
     for step, masks in enumerate(zip(orders[0][::-1], orders[1][::-1])):
         got = [swap(send[k], "ctx", masks[k]) for k in range(2)]
@@ -502,7 +615,7 @@
             come = [relay(piece, behind) for piece in come]
         pieces = pieces + come
     block_out, tokens_grad, gate_grad, shift_grad, scale_grad, router_rows = finish(
-        place, side, got, pieces, scale, gate, tokens, out_grad, normed, inverse
+        place, side, got, pieces, one, gate, near_tokens, near_grads, normed, inverse
     )
     return (
         block_out,
@@ -510,9 +623,9 @@
         up_grad,
         down_grad,
         router_rows.T[None],
-        shift_grad[0],
-        scale_grad[0],
-        gate_grad[0],
+        shift_grad.reshape(width),
+        scale_grad.reshape(width),
+        gate_grad.reshape(width),
     )
 
 

time: 89.2 us -> 81.2 us (0.910)
  waiting for transfers between devices: 14 us -> 10.6 us
  starting transfers between devices: 19 us -> 17.2 us
  other arithmetic: 2.49 us -> 1.02 us
  local copies, waits for them, and re-layouts: 1.27 us -> 0.01 us
    pallas_call x5 -> x10, Pallas kernels: 21.4 us -> 27 us  [the longest x4 15.3 us: outer(): pl.pallas_call(body, in_specs=[WHOLE] * 2 + [ORDER] * (1 + len(before)),...]
    pallas_call x1, Pallas kernels: 21.8 us -> 18 us  [experts(): pl.pallas_call(functools.partial(expert_body, places), in_specs=[SCALARS]...]
    ppermute x13, waiting for transfers between devices: 14 us -> 10.6 us  [swap(): return lax.ppermute(values, axis, [(i, i ^ mask) for i in range(size)])]
    pallas_call x1, Pallas kernels: 5.11 us -> 3.2 us  [finish(): pl.pallas_call(functools.partial(finish_body, parts), in_specs=[SCALARS]...]
    ppermute x13, starting transfers between devices: 19 us -> 17.2 us  [swap(): return lax.ppermute(values, axis, [(i, i ^ mask) for i in range(size)])]
    unnamed x2 -> x4, local copies, waits for them, and re-layouts: 1.22 us -> 0.01 us
  transfers between devices with their start and end apart: 13 -> 13, of which waited for: 9 -> 9; matrix products, arithmetic and copies ran while one was open for 3% -> 1% of each run, Pallas kernels for 24% -> 33%
where the time goes in v3:
time: 81.2 us; the launch traced here: 80.9 us
  Pallas kernels  51 us (63%)
  starting transfers between devices  17.2 us (21%)
  waiting for transfers between devices  10.6 us (13%)
  other arithmetic  1.02 us (1%)
  between operations  1 us (1%)
    pallas_call x1, Pallas kernels, experts(): pl.pallas_call(functools.partial(expert_body, places), in_specs=[SCALARS]...  18 us
    ppermute x13, starting transfers between devices, swap(): return lax.ppermute(values, axis, [(i, i ^ mask) for i in range(size)])  17.2 us
    pallas_call x4, Pallas kernels, outer(): pl.pallas_call(body, in_specs=[WHOLE] * 2 + [ORDER] * (1 + len(before)),...  15.3 us
    ppermute x13, waiting for transfers between devices, swap(): return lax.ppermute(values, axis, [(i, i ^ mask) for i in range(size)])  10.6 us
    pallas_call x3, Pallas kernels, bring(): pl.pallas_call(functools.partial(bring_body, first), in_specs=[ORDER] * 3...  8.65 us
    pallas_call x1, Pallas kernels, finish(): pl.pallas_call(functools.partial(finish_body, parts), in_specs=[SCALARS]...  3.2 us
    pallas_call x1, Pallas kernels, normalize(): pl.pallas_call(normalize_body, grid=(tok_count // step,), in_specs=[wide,...  3.07 us
    pallas_call x1, Pallas kernels, select(): pl.pallas_call(select_body, in_specs=[SCALARS] + [ORDER] * 3, out_specs=[...  2.55 us
  transfers between devices with their start and end apart: 13, of which 9 were waited for; matrix products, arithmetic and copies ran while one was open for 1% of the time, Pallas kernels for 33%

profile of v3, /device:TPU:0, one launch (start us, length us, event | category | flops | bytes accessed | tf_op | source)
XLA Modules:
  0.0 80.9 jit_solution(4324085769304461518)
XLA Ops:
  0.6 0.1 pad_add_fusion.place
  0.7 2.6 %select.22 = (bf16[16,4096]{1,0:T(8,128)(2,1)S(1)}, bf16[16,4096]{1,0:T(8,128)(2,1)S(1)}, f32[8,32]{1,0:T(8,128)S(1)}) custom-call(s32[2]{0:T(128)S(1)} %pad_add_fusion.place, s32[1,2,32]{2,1,0:T(2,128)} %picked_h.1, bf16[128,4096]{1,0:T(8,128)(2,1)} %tokens.1, bf16[128,4096]{1,0:T(8,128)(2,1)} %grads.1), custom_call_target="tpu_custom_call" | custom-call | tf_op jit(solution)/shard_map/select/pallas_call | solution.py:114
  3.3 4.1 %collective-permute-start = (bf16[16,4096]{1,0:T(8,128)(2,1)S(1)}, bf16[16,4096]{1,0:T(8,128)(2,1)S(1)}, u32[]{:S(2)}, u32[]{:S(2)}) collective-permute-start(bf16[16,4096]{1,0:T(8,128)(2,1)S(1)} %get-tuple-element.62), channel_id=1, source_target_pairs={{0,16},{4,20},{8,24},{12,28},{16,0},{20,4},{24,8},{28,12},{1,17},{... | collective-permute-start | bytes 393224 | tf_op jit(solution)/shard_map/ppermute | solution.py:530
  7.4 0.7 convert_bitcast_fusion
  8.1 0.0 copy-start
  8.2 2.3 %bring.3 = (bf16[1,4096,256]{2,1,0:T(8,128)(2,1)S(1)}, bf16[1,256,4096]{2,1,0:T(8,128)(2,1)S(1)}, f32[8,128]{1,0:T(8,128)S(1)}) custom-call(bf16[1,4096,2048]{2,1,0:T(8,128)(2,1)} %up_h.7, bf16[1,2048,4096]{2,1,0:T(8,128)(2,1)} %down_h.7, bf16[16,4096]{1,0:T(8,128)(2,1)S(1)} %get-tuple-element.61._.near_t.near_g), custom_call_target="tpu_custom_call" | custom-call | bytes 4194304 | tf_op jit(solution)/shard_map/bring/pallas_call | solution.py:151
  10.4 3.1 %normalize.1 = (f32[128,4096]{1,0:T(8,128)S(1)}, f32[128,128]{1,0:T(8,128)S(1)}, bf16[128,4096]{1,0:T(8,128)(2,1)S(1)}, bf16[128,4096]{1,0:T(8,128)(2,1)S(1)}, f...) custom-call(bf16[128,4096]{1,0:T(8,128)(2,1)} %tokens.1, bf16[128,4096]{1,0:T(8,128)(2,1)} %grads.1, ...), custom_call_target="tpu_custom_call" | custom-call | flops 5242880 | bytes 3145728 | tf_op jit(solution)/shard_map/normalize/pallas_call | solution.py:450
  13.5 0.2 collective-permute-done.far_t.far_g
  13.7 1.6 %collective-permute-start.2 = (bf16[16,4096]{1,0:T(8,128)(2,1)S(1)}, bf16[16,4096]{1,0:T(8,128)(2,1)S(1)}, u32[]{:S(2)}, u32[]{:S(2)}) collective-permute-start(bf16[16,4096]{1,0:T(8,128)(2,1)S(1)} %get-tuple-element.65.near_g), channel_id=1, source_target_pairs={{0,4},{4,0},{8,12},{12,8},{16,20},{20,16},{24,28},{28,24},{1,5},{5... | collective-permute-start | bytes 393224 | tf_op jit(solution)/shard_map/ppermute | solution.py:530
  15.4 1.4 %collective-permute-start.1 = (bf16[16,4096]{1,0:T(8,128)(2,1)S(1)}, bf16[16,4096]{1,0:T(8,128)(2,1)S(1)}, u32[]{:S(2)}, u32[]{:S(2)}) collective-permute-start(bf16[16,4096]{1,0:T(8,128)(2,1)S(1)} %get-tuple-element.64._.near_t), channel_id=1, source_target_pairs={{0,8},{4,12},{8,0},{12,4},{16,24},{20,28},{24,16},{28,20},{1,9},{5... | collective-permute-start | bytes 393224 | tf_op jit(solution)/shard_map/ppermute | solution.py:530
  16.7 0.0 copy-done
  16.7 0.0 copy-start.1
  16.7 2.3 %bring.4 = (bf16[1,4096,256]{2,1,0:T(8,128)(2,1)S(1)}, bf16[1,256,4096]{2,1,0:T(8,128)(2,1)S(1)}, f32[8,128]{1,0:T(8,128)S(1)}) custom-call(bf16[1,4096,2048]{2,1,0:T(8,128)(2,1)} %up_h.7, bf16[1,2048,4096]{2,1,0:T(8,128)(2,1)} %down_h.7, bf16[16,4096]{1,0:T(8,128)(2,1)S(1)} %get-tuple-element.64._.near_t), custom_call_target="tpu_custom_call" | custom-call | bytes 4194304 | tf_op jit(solution)/shard_map/bring/pallas_call | solution.py:151
  19.0 0.0 collective-permute-done.2.far_g
  19.0 1.3 %collective-permute-done.1.far_t = bf16[16,4096]{1,0:T(8,128)(2,1)S(1)} collective-permute-done((bf16[16,4096]{1,0:T(8,128)(2,1)S(1)}, bf16[16,4096]{1,0:T(8,128)(2,1)S(1)}, u32[]{:S(2)}, u32[]{:S(2)}) %collective-permute-start.1) | collective-permute-done | bytes 131104 | tf_op jit(solution)/shard_map/ppermute | solution.py:530
  20.4 1.4 %collective-permute-start.4 = (bf16[32,4096]{1,0:T(8,128)(2,1)S(1)}, bf16[32,4096]{1,0:T(8,128)(2,1)S(1)}, u32[]{:S(2)}, u32[]{:S(2)}) collective-permute-start(bf16[32,4096]{1,0:T(8,128)(2,1)S(1)} %get-tuple-element.68.near_g), channel_id=1, source_target_pairs={{0,8},{4,12},{8,0},{12,4},{16,24},{20,28},{24,16},{28,20},{1,9},{5... | collective-permute-start | bytes 786440 | tf_op jit(solution)/shard_map/ppermute | solution.py:530
  21.8 0.5 collective-permute-start.3
  22.3 0.0 copy-done.1
  22.3 0.2 convert_reduce_fusion.counts
  22.5 4.1 %bring.5 = (bf16[2,4096,256]{2,1,0:T(8,128)(2,1)S(1)}, bf16[2,256,4096]{2,1,0:T(8,128)(2,1)S(1)}, f32[8,128]{1,0:T(8,128)}) custom-call(bf16[1,4096,2048]{2,1,0:T(8,128)(2,1)} %up_h.7, bf16[1,2048,4096]{2,1,0:T(8,128)(2,1)} %down_h.7, bf16[32,4096]{1,0:T(8,128)(2,1)S(1)} %get-tuple-element.67._.near_t), custom_call_target="tpu_custom_call" | custom-call | bytes 8388608 | tf_op jit(solution)/shard_map/bring/pallas_call | solution.py:151
  26.6 0.2 collective-permute-done.4.far_g
  26.8 1.3 %collective-permute-done.3.far_t = bf16[32,4096]{1,0:T(8,128)(2,1)S(1)} collective-permute-done((bf16[32,4096]{1,0:T(8,128)(2,1)S(1)}, bf16[32,4096]{1,0:T(8,128)(2,1)S(1)}, u32[]{:S(2)}, u32[]{:S(2)}) %collective-permute-start.3) | collective-permute-done | bytes 262176 | tf_op jit(solution)/shard_map/ppermute | solution.py:530
  28.2 18.0 %experts.1 = (bf16[64,4096]{1,0:T(8,128)(2,1)S(1)}, bf16[64,4096]{1,0:T(8,128)(2,1)S(1)}, bf16[64,2048]{1,0:T(8,128)(2,1)S(1)}, bf16[64,2048]{1,0:T(8,128)(2,1)S...) custom-call(s32[8]{0:T(128)S(1)} %convert_reduce_fusion.counts, ...), custom_call_target="tpu_custom_call" | custom-call | flops 4294967296 | bytes 33554432 | tf_op jit(solution)/shard_map/experts/pallas_call | solution.py:286
  46.2 0.6 collective-permute-start.5
  46.7 0.6 collective-permute-start.6
  47.3 5.1 %up_grad.2 = (bf16[1,4096,2048]{2,1,0:T(8,128)(2,1)}, f32[8,128]{1,0:T(8,128)S(1)}) custom-call(bf16[64,4096]{1,0:T(8,128)(2,1)S(1)} %get-tuple-element.83.left, bf16[64,2048]{1,0:T(8,128)(2,1)S(1)} %get-tuple-element.84.right, f32[128,128]{1,0:T(8,128)S(1)} %get-tuple-element.82._.side), custom_call_target="tpu_custom_call" | custom-call | flops 3221225472 | bytes 25165824 | tf_op jit(solution)/shard_map/up_grad/pallas_call | solution.py:336
  52.5 0.3 collective-permute-done.5.got_e
  52.8 1.7 %collective-permute-done.6.got_b = bf16[32,4352]{1,0:T(8,128)(2,1)S(1)} collective-permute-done((bf16[32,4352]{1,0:T(8,128)(2,1)S(1)}, bf16[32,4352]{1,0:T(8,128)(2,1)S(1)}, u32[]{:S(2)}, u32[]{:S(2)}) %collective-permute-start.6) | collective-permute-done | bytes 278560 | tf_op jit(solution)/shard_map/ppermute | solution.py:530
  54.5 0.1 fold.2
  54.6 0.1 collective-permute-start.7
  54.7 1.4 %collective-permute-start.8 = (bf16[16,4608]{1,0:T(8,128)(2,1)S(1)}, bf16[16,4608]{1,0:T(8,128)(2,1)S(1)}, u32[]{:S(2)}, u32[]{:S(2)}) collective-permute-start(bf16[16,4608]{1,0:T(8,128)(2,1)S(1)} %get-tuple-element.89), channel_id=1, source_target_pairs={{0,4},{4,0},{8,12},{12,8},{16,20},{20,16},{24,28},{28,24},{1,5},{5... | collective-permute-start | bytes 442376 | tf_op jit(solution)/shard_map/ppermute | solution.py:530
  56.1 3.8 %down_grad.2 = (bf16[1,2048,4096]{2,1,0:T(8,128)(2,1)}, f32[8,128]{1,0:T(8,128)S(1)}) custom-call(bf16[64,2048]{1,0:T(8,128)(2,1)S(1)} %get-tuple-element.91.left, bf16[64,4096]{1,0:T(8,128)(2,1)S(1)} %get-tuple-element.92.right, f32[128,128]{1,0:T(8,128)S(1)} %get-tuple-element.90._.side), custom_call_target="tpu_custom_call" | custom-call | flops 2147483648 | bytes 16777216 | tf_op jit(solution)/shard_map/down_grad/pallas_call | solution.py:336
  60.0 0.0 collective-permute-done.7.got_e
  60.0 0.0 collective-permute-done.8.got_b
  60.0 0.1 fold.3
  60.1 3.9 %collective-permute-start.9 = (bf16[16,5120]{1,0:T(8,128)(2,1)S(1)}, bf16[16,5120]{1,0:T(8,128)(2,1)S(1)}, u32[]{:S(2)}, u32[]{:S(2)}) collective-permute-start(bf16[16,5120]{1,0:T(8,128)(2,1)S(1)} %get-tuple-element.95), channel_id=1, source_target_pairs={{0,16},{4,20},{8,24},{12,28},{16,0},{20,4},{24,8},{28,12},{1,17},{... | collective-permute-start | bytes 491528 | tf_op jit(solution)/shard_map/ppermute | solution.py:530
  64.0 3.8 %down_grad.3 = (bf16[1,2048,4096]{2,1,0:T(8,128)(2,1)}, f32[8,128]{1,0:T(8,128)S(1)}) custom-call(bf16[64,2048]{1,0:T(8,128)(2,1)S(1)} %get-tuple-element.91.left, bf16[64,4096]{1,0:T(8,128)(2,1)S(1)} %get-tuple-element.92.right, f32[128,128]{1,0:T(8,128)S(1)} %get-tuple-element.94._.side, ...), custom_call_target="tpu_custom_call", output_to_operand_aliasing={{0}: (3, {})} | custom-call | flops 2147483648 | bytes 16777216 | tf_op jit(solution)/shard_map/down_grad/pallas_call | solution.py:336
  67.8 1.2 %collective-permute-done.9.got = bf16[16,5120]{1,0:T(8,128)(2,1)S(1)} collective-permute-done((bf16[16,5120]{1,0:T(8,128)(2,1)S(1)}, bf16[16,5120]{1,0:T(8,128)(2,1)S(1)}, u32[]{:S(2)}, u32[]{:S(2)}) %collective-permute-start.9) | collective-permute-done | bytes 163872 | tf_op jit(solution)/shard_map/ppermute | solution.py:530
  69.1 1.5 %collective-permute-start.10 = (bf16[32,4608]{1,0:T(8,128)(2,1)S(1)}, bf16[32,4608]{1,0:T(8,128)(2,1)S(1)}, u32[]{:S(2)}, u32[]{:S(2)}) collective-permute-start(bf16[32,4608]{1,0:T(8,128)(2,1)S(1)} %pack.1._.refs_0_), channel_id=1, source_target_pairs={{0,2},{1,3},{2,0},{3,1},{4,6},{5,7},{6,4},{7,5},{8,10},{9,11},{10,... | collective-permute-start | bytes 884744 | tf_op jit(solution)/shard_map/ppermute | solution.py:530
  70.6 0.0 collective-permute-start.11
  70.6 2.5 %up_grad.3 = (bf16[1,4096,2048]{2,1,0:T(8,128)(2,1)}, f32[8,128]{1,0:T(8,128)S(1)}) custom-call(bf16[64,4096]{1,0:T(8,128)(2,1)S(1)} %get-tuple-element.83.left, bf16[64,2048]{1,0:T(8,128)(2,1)S(1)} %get-tuple-element.84.right, bf16[32,4608]{1,0:T(8,128)(2,1)S(1)} %pack.1._.refs_0_, ...), custom_call_target="tpu_custom_call", output_to_operand_aliasing={{0}: (3, {})} | custom-call | flops 1073741824 | bytes 8388608 | tf_op jit(solution)/shard_map/up_grad/pallas_call | solution.py:336
  73.1 2.8 %collective-permute-done.10.rows = bf16[32,4608]{1,0:T(8,128)(2,1)S(1)} collective-permute-done((bf16[32,4608]{1,0:T(8,128)(2,1)S(1)}, bf16[32,4608]{1,0:T(8,128)(2,1)S(1)}, u32[]{:S(2)}, u32[]{:S(2)}) %collective-permute-start.10) | collective-permute-done | bytes 294944 | tf_op jit(solution)/shard_map/ppermute | solution.py:530
  75.9 0.1 collective-permute-start.12
  76.0 0.0 collective-permute-done.11.refs_2_
  76.0 1.6 %collective-permute-done.12.refs_3_ = bf16[32,4608]{1,0:T(8,128)(2,1)S(1)} collective-permute-done((bf16[32,4608]{1,0:T(8,128)(2,1)S(1)}, bf16[32,4608]{1,0:T(8,128)(2,1)S(1)}, u32[]{:S(2)}, u32[]{:S(2)}) %collective-permute-start.12) | collective-permute-done | bytes 294944 | tf_op jit(solution)/shard_map/ppermute | solution.py:530
  77.5 3.2 %finish.1 = (bf16[128,4096]{1,0:T(8,128)(2,1)}, bf16[128,4096]{1,0:T(8,128)(2,1)}, f32[32,128]{1,0:T(8,128)}, f32[32,128]{1,0:T(8,128)}, f32[32,128]{1,0:T(8,128)}, /*index=5*/f32[2,4096]{1,0:T(2,128)}) custom-call(s32[2]{0:T(128)S(1)} %pad_add_fusion.place, f32[128,128]{1,0:T(8,128)S(1)} %get-tuple-element.94._.side, ...), custom_call_target="tpu_custom_call" | custom-call | tf_op jit(solution)/shard_map/finish/pallas_call | solution.py:512
  (7 shorter events, 0.1 us)
Async XLA Ops:
  3.3 10.4 %collective-permute-start = (bf16[16,4096]{1,0:T(8,128)(2,1)S(1)}, bf16[16,4096]{1,0:T(8,128)(2,1)S(1)}, u32[]{:S(2)}, u32[]{:S(2)}) collective-permute-start(bf16[16,4096]{1,0:T(8,128)(2,1)S(1)} %get-tuple-element.62), channel_id=1, source_target_pairs={{0,16},{4,20},{8,24},{12,28},{16,0},{20,4},{24,8},{28,12},{1,17},{... | collective-permute-start | bytes 393224 | tf_op jit(solution)/shard_map/ppermute | solution.py:530
  8.1 8.6 %copy-start = (s32[1,2,32]{2,1,0:T(2,128)S(1)}, s32[1,2,32]{2,1,0:T(2,128)}, u32[]{:S(2)}) copy-start(s32[1,2,32]{2,1,0:T(2,128)} %picked_h.1) | copy-start | bytes 772
  13.7 5.3 %collective-permute-start.2 = (bf16[16,4096]{1,0:T(8,128)(2,1)S(1)}, bf16[16,4096]{1,0:T(8,128)(2,1)S(1)}, u32[]{:S(2)}, u32[]{:S(2)}) collective-permute-start(bf16[16,4096]{1,0:T(8,128)(2,1)S(1)} %get-tuple-element.65.near_g), channel_id=1, source_target_pairs={{0,4},{4,0},{8,12},{12,8},{16,20},{20,16},{24,28},{28,24},{1,5},{5... | collective-permute-start | bytes 393224 | tf_op jit(solution)/shard_map/ppermute | solution.py:530
  15.4 5.0 %collective-permute-start.1 = (bf16[16,4096]{1,0:T(8,128)(2,1)S(1)}, bf16[16,4096]{1,0:T(8,128)(2,1)S(1)}, u32[]{:S(2)}, u32[]{:S(2)}) collective-permute-start(bf16[16,4096]{1,0:T(8,128)(2,1)S(1)} %get-tuple-element.64._.near_t), channel_id=1, source_target_pairs={{0,8},{4,12},{8,0},{12,4},{16,24},{20,28},{24,16},{28,20},{1,9},{5... | collective-permute-start | bytes 393224 | tf_op jit(solution)/shard_map/ppermute | solution.py:530
  16.7 5.6 %copy-start.1 = (s32[8]{0:T(128)S(1)}, s32[8]{0:T(128)}, u32[]{:S(2)}) copy-start(s32[8]{0:T(128)} %constant.38.clone) | copy-start | bytes 100
  20.4 6.5 %collective-permute-start.4 = (bf16[32,4096]{1,0:T(8,128)(2,1)S(1)}, bf16[32,4096]{1,0:T(8,128)(2,1)S(1)}, u32[]{:S(2)}, u32[]{:S(2)}) collective-permute-start(bf16[32,4096]{1,0:T(8,128)(2,1)S(1)} %get-tuple-element.68.near_g), channel_id=1, source_target_pairs={{0,8},{4,12},{8,0},{12,4},{16,24},{20,28},{24,16},{28,20},{1,9},{5... | collective-permute-start | bytes 786440 | tf_op jit(solution)/shard_map/ppermute | solution.py:530
  21.8 6.4 %collective-permute-start.3 = (bf16[32,4096]{1,0:T(8,128)(2,1)S(1)}, bf16[32,4096]{1,0:T(8,128)(2,1)S(1)}, u32[]{:S(2)}, u32[]{:S(2)}) collective-permute-start(bf16[32,4096]{1,0:T(8,128)(2,1)S(1)} %get-tuple-element.67._.near_t), channel_id=1, source_target_pairs={{0,4},{4,0},{8,12},{12,8},{16,20},{20,16},{24,28},{28,24},{1,5},{5... | collective-permute-start | bytes 786440 | tf_op jit(solution)/shard_map/ppermute | solution.py:530
  46.2 6.6 %collective-permute-start.5 = (bf16[32,4352]{1,0:T(8,128)(2,1)S(1)}, bf16[32,4352]{1,0:T(8,128)(2,1)S(1)}, u32[]{:S(2)}, u32[]{:S(2)}) collective-permute-start(bf16[32,4352]{1,0:T(8,128)(2,1)S(1)} %get-tuple-element.80), channel_id=1, source_target_pairs={{0,4},{4,0},{8,12},{12,8},{16,20},{20,16},{24,28},{28,24},{1,5},{5... | collective-permute-start | bytes 835592 | tf_op jit(solution)/shard_map/ppermute | solution.py:530
  46.7 7.8 %collective-permute-start.6 = (bf16[32,4352]{1,0:T(8,128)(2,1)S(1)}, bf16[32,4352]{1,0:T(8,128)(2,1)S(1)}, u32[]{:S(2)}, u32[]{:S(2)}) collective-permute-start(bf16[32,4352]{1,0:T(8,128)(2,1)S(1)} %get-tuple-element.81), channel_id=1, source_target_pairs={{0,8},{4,12},{8,0},{12,4},{16,24},{20,28},{24,16},{28,20},{1,9},{5... | collective-permute-start | bytes 835592 | tf_op jit(solution)/shard_map/ppermute | solution.py:530
  54.6 5.4 %collective-permute-start.7 = (bf16[16,4608]{1,0:T(8,128)(2,1)S(1)}, bf16[16,4608]{1,0:T(8,128)(2,1)S(1)}, u32[]{:S(2)}, u32[]{:S(2)}) collective-permute-start(bf16[16,4608]{1,0:T(8,128)(2,1)S(1)} %get-tuple-element.88), channel_id=1, source_target_pairs={{0,8},{4,12},{8,0},{12,4},{16,24},{20,28},{24,16},{28,20},{1,9},{5... | collective-permute-start | bytes 442376 | tf_op jit(solution)/shard_map/ppermute | solution.py:530
  54.7 5.3 %collective-permute-start.8 = (bf16[16,4608]{1,0:T(8,128)(2,1)S(1)}, bf16[16,4608]{1,0:T(8,128)(2,1)S(1)}, u32[]{:S(2)}, u32[]{:S(2)}) collective-permute-start(bf16[16,4608]{1,0:T(8,128)(2,1)S(1)} %get-tuple-element.89), channel_id=1, source_target_pairs={{0,4},{4,0},{8,12},{12,8},{16,20},{20,16},{24,28},{28,24},{1,5},{5... | collective-permute-start | bytes 442376 | tf_op jit(solution)/shard_map/ppermute | solution.py:530
  60.1 9.0 %collective-permute-start.9 = (bf16[16,5120]{1,0:T(8,128)(2,1)S(1)}, bf16[16,5120]{1,0:T(8,128)(2,1)S(1)}, u32[]{:S(2)}, u32[]{:S(2)}) collective-permute-start(bf16[16,5120]{1,0:T(8,128)(2,1)S(1)} %get-tuple-element.95), channel_id=1, source_target_pairs={{0,16},{4,20},{8,24},{12,28},{16,0},{20,4},{24,8},{28,12},{1,17},{... | collective-permute-start | bytes 491528 | tf_op jit(solution)/shard_map/ppermute | solution.py:530
  69.1 6.8 %collective-permute-start.10 = (bf16[32,4608]{1,0:T(8,128)(2,1)S(1)}, bf16[32,4608]{1,0:T(8,128)(2,1)S(1)}, u32[]{:S(2)}, u32[]{:S(2)}) collective-permute-start(bf16[32,4608]{1,0:T(8,128)(2,1)S(1)} %pack.1._.refs_0_), channel_id=1, source_target_pairs={{0,2},{1,3},{2,0},{3,1},{4,6},{5,7},{6,4},{7,5},{8,10},{9,11},{10,... | collective-permute-start | bytes 884744 | tf_op jit(solution)/shard_map/ppermute | solution.py:530
  70.6 5.4 %collective-permute-start.11 = (bf16[32,4608]{1,0:T(8,128)(2,1)S(1)}, bf16[32,4608]{1,0:T(8,128)(2,1)S(1)}, u32[]{:S(2)}, u32[]{:S(2)}) collective-permute-start(bf16[32,4608]{1,0:T(8,128)(2,1)S(1)} %pack.1._.refs_0_), channel_id=1, source_target_pairs={{0,1},{1,0},{2,3},{3,2},{4,5},{5,4},{6,7},{7,6},{8,9},{9,8},{10,11... | collective-permute-start | bytes 884744 | tf_op jit(solution)/shard_map/ppermute | solution.py:530
  75.9 1.6 %collective-permute-start.12 = (bf16[32,4608]{1,0:T(8,128)(2,1)S(1)}, bf16[32,4608]{1,0:T(8,128)(2,1)S(1)}, u32[]{:S(2)}, u32[]{:S(2)}) collective-permute-start(bf16[32,4608]{1,0:T(8,128)(2,1)S(1)} %relay.1.refs_1_), channel_id=1, source_target_pairs={{0,1},{1,0},{2,3},{3,2},{4,5},{5,4},{6,7},{7,6},{8,9},{9,8},{10,11... | collective-permute-start | bytes 884744 | tf_op jit(solution)/shard_map/ppermute | solution.py:530

commit v4 on v3

--- a/solution.py
+++ b/solution.py
@@ -348,7 +348,13 @@
     )(left, right, behind, *before)
 
 
-def fold_body(last, keep_e, keep_b, got_e, got_b, side, _, *outs):
+def number_columns(ids, rows):
+    blank = jnp.full((SIDE, LANES - ids.shape[1]), -1.0, f32)
+    numbers = jnp.concatenate([ids, blank], axis=1)
+    return jnp.concatenate([numbers, jnp.zeros((rows - SIDE, LANES), f32)], axis=0)
+
+
+def fold_body(last, keep_e, keep_b, got_e, got_b, side, ids, _, *outs):
     rows, width = keep_e.shape
     depth = width // LANES
     got = [got_e[...].astype(f32), got_b[...].astype(f32)]
@@ -359,7 +365,8 @@
     outs[0][...] = jnp.concatenate(sums, axis=0)
     low, high = slice(0, rows // 2), slice(rows // 2, rows)
     if last:
-        outs[1][...] = jnp.concatenate([eo[low], back[low]], axis=0)
+        mine = jnp.concatenate([eo[low], back[low]], axis=0)
+        outs[1][...] = jnp.concatenate([mine, number_columns(ids[:, :rows], rows)], axis=1).astype(bf16)
         send = jnp.concatenate([eo[high], back[high]], axis=0)
         outs[2][...] = jnp.concatenate([send] + [spread(v, rows) for v in sums], axis=1).astype(bf16)
     else:
@@ -369,63 +376,62 @@
         outs[4][...] = jnp.concatenate([back[high]] + [spread(v, rows // 2) for v in sums[2:]], axis=1).astype(bf16)
 
 
-def fold(keep, got, side, behind):
+def fold(keep, got, side, ids, behind):
     rows, width = keep[0].shape
     last = rows == 2 * MOST
     shapes = [(side.shape, f32)]
     if last:
-        shapes += [((rows, width), f32), ((rows, width + 4 * spread_columns(width, rows)), bf16)]
+        shapes += [((rows, width + LANES), bf16), ((rows, width + 4 * spread_columns(width, rows)), bf16)]
     else:
         wide = width + 2 * spread_columns(width, rows // 2)
         shapes += [((rows // 2, width), f32)] * 2 + [((rows // 2, wide), bf16)] * 2
     return pl.pallas_call(
         functools.partial(fold_body, last),
-        in_specs=[WHOLE] * 5 + [ORDER],
+        in_specs=[WHOLE] * 6 + [ORDER],
         out_specs=[WHOLE] * len(shapes),
         out_shape=[jax.ShapeDtypeStruct(shape, kind) for shape, kind in shapes],
         compiler_params=pltpu.CompilerParams(vmem_limit_bytes=16 * MIB),
         name="fold",
-    )(*keep, *got, side, behind)
-
-
-def pack_body(keep, got, side, ids, _, mine_o):
-    width = keep.shape[1]
+    )(*keep, *got, side, ids, behind)
+
+
+def pack_body(width, got, side, ids, *refs):
+    mine_o = refs[-1]
     depth = width // LANES
     theirs = got[...].astype(f32)
     sums = [side[k * depth : (k + 1) * depth] + v for k, v in enumerate(unspread(theirs[:, width:], width)[:3])]
     rows = mine_o.shape[0]
-    numbers = jnp.concatenate([ids[...], jnp.full((SIDE, LANES - ids.shape[1]), -1.0, f32)], axis=1)
-    numbers = jnp.concatenate([numbers, jnp.zeros((rows - SIDE, LANES), f32)], axis=0)
-    mine = jnp.concatenate([keep[...], theirs[:, :width]], axis=0)
-    mine_o[...] = jnp.concatenate([mine] + [spread(v, rows) for v in sums] + [numbers], axis=1).astype(bf16)
-
-
-def pack(keep, got, side, ids, behind):
-    width = keep.shape[1]
-    rows = 2 * GROUP
-    return pl.pallas_call(
-        pack_body,
-        in_specs=[WHOLE] * 4 + [ORDER],
+    numbers = number_columns(ids[:, rows:], rows)
+    mine_o[...] = jnp.concatenate(
+        [theirs[:, :width]] + [spread(v, rows) for v in sums] + [numbers], axis=1
+    ).astype(bf16)
+
+
+def pack(width, got, side, ids, *behind):
+    rows = got.shape[0]
+    return pl.pallas_call(
+        functools.partial(pack_body, width),
+        in_specs=[WHOLE] * 3 + [ORDER] * len(behind),
         out_specs=WHOLE,
         out_shape=jax.ShapeDtypeStruct((rows, width + 3 * spread_columns(width, rows) + LANES), bf16),
         compiler_params=pltpu.CompilerParams(vmem_limit_bytes=16 * MIB),
         name="pack",
-    )(keep, got, side, ids, behind)
-
-
-def relay_body(rows, _, rows_o):
-    rows_o[...] = rows[...]
-
-
-def relay(rows, behind):
+    )(got, side, ids, *behind)
+
+
+def relay_body(rows, *refs):
+    refs[-1][...] = rows[...]
+
+
+def relay(rows, *behind):
     return pl.pallas_call(
         relay_body,
-        in_specs=[WHOLE, ORDER],
+        in_specs=[WHOLE] + [ORDER] * len(behind),
         out_specs=WHOLE,
         out_shape=jax.ShapeDtypeStruct(rows.shape, rows.dtype),
         compiler_params=pltpu.CompilerParams(vmem_limit_bytes=16 * MIB),
         name="relay",
-    )(rows, behind)
+    )(rows, *behind)
 
 
 def normalize_body(tokens, grads, shift, scale, gate, normed_o, inverse_o, tokens_o, grads_o, shift_o, one_o, gate_o):
@@ -477,9 +483,10 @@
     width = tokens.shape[1]
     depth = width // LANES
     rows = jnp.concatenate([piece[:, :width] for piece in pieces], axis=0)
-    ids = [piece[:, piece.shape[1] - LANES :].astype(f32)[:, : 2 * GROUP] for piece in pieces]
+    ids = [piece[:, piece.shape[1] - LANES :].astype(f32)[:, : piece.shape[0]] for piece in pieces]
     ids = [jnp.concatenate([each[kind : 1 + kind] for each in ids], axis=1) for kind in range(2)]
-    vector = sum(piece[:, width : piece.shape[1] - LANES].astype(f32) for piece in pieces)
+    with_sums = [piece for piece in pieces if piece.shape[1] > width + LANES]
+    vector = sum(piece[:, width : piece.shape[1] - LANES].astype(f32) for piece in with_sums)
     gate_s[...], shift_s[...], scale_s[...] = unspread(vector, width)
     own = side[3 * depth :]
     other = unspread(got[...].astype(f32)[:, width:], width)[3]
@@ -597,23 +604,26 @@
     for step, masks in enumerate(zip(orders[0][::-1], orders[1][::-1])):
         got = [swap(send[k], "ctx", masks[k]) for k in range(2)]
         if step == 0:
-            up_grad, behind = outer(hidden, grad_pre, behind, "up_grad", 0, 3)
+            up_grad, behind = outer(hidden, grad_pre, behind, "up_grad", 0, 4)
         elif step == 1:
             down_grad, behind = outer(act, grad_rows, behind, "down_grad", 0, 2)
-        side, *rest = fold(keep, got, side, behind)
+        side, *rest = fold(keep, got, side, ids, behind)
         keep, send = rest[:-2], rest[-2:]
         behind = side
-    keep, send = rest
+    mine, send = rest
     got = swap(send, "ctx", ctx_masks[0])
-    down_grad, behind = outer(act, grad_rows, behind, "down_grad", 2, 2, down_grad)
-    mine = pack(keep, got, side, ids, behind)
-    pieces = [mine]
-    for step, mask in enumerate(exp_masks):
-        come = [swap(piece, "exp", mask) for piece in pieces]
-        if step == 0:
-            up_grad, behind = outer(hidden, grad_pre, mine, "up_grad", 3, 1, up_grad)
-            come = [relay(piece, behind) for piece in come]
-        pieces = pieces + come
+    down_grad, behind = outer(act, grad_rows, behind, "down_grad", 2, 1, down_grad)
+    come = swap(mine, "exp", exp_masks[0])
+    pieces = [mine, come]
+    mine = pack(width, got, side, ids, behind)
+    come = swap(mine, "exp", exp_masks[0])
+    down_grad, behind = outer(act, grad_rows, mine, "down_grad", 3, 1, down_grad)
+    for mask in exp_masks[1:]:
+        pieces = pieces + [swap(piece, "exp", mask) for piece in pieces]
+    last = [mine, relay(come, behind, *pieces[2:])]
+    for mask in exp_masks[1:]:
+        last = last + [swap(piece, "exp", mask) for piece in last]
+    pieces = pieces + last
     block_out, tokens_grad, gate_grad, shift_grad, scale_grad, router_rows = finish(
         place, side, got, pieces, one, gate, near_tokens, near_grads, normed, inverse
     )

time: 81.2 us -> 79.7 us (0.982)
  waiting for transfers between devices: 10.6 us -> 5.84 us
  starting transfers between devices: 17.2 us -> 20.5 us
    ppermute x13 -> x16, waiting for transfers between devices: 10.6 us -> 5.84 us  [swap(): return lax.ppermute(values, axis, [(i, i ^ mask) for i in range(size)])]
    ppermute x13 -> x16, starting transfers between devices: 17.2 us -> 20.5 us  [swap(): return lax.ppermute(values, axis, [(i, i ^ mask) for i in range(size)])]
  transfers between devices with their start and end apart: 13 -> 16, of which waited for: 9 -> 7; matrix products, arithmetic and copies ran while one was open for 1% -> 1% of each run, Pallas kernels for 33% -> 34%
where the time goes in v4:
time: 79.7 us; the launch traced here: 79.4 us
  Pallas kernels  51.1 us (64%)
  starting transfers between devices  20.5 us (26%)
  waiting for transfers between devices  5.84 us (7%)
  other arithmetic  1.02 us (1%)
  between operations  1.02 us (1%)
    ppermute x16, starting transfers between devices, swap(): return lax.ppermute(values, axis, [(i, i ^ mask) for i in range(size)])  20.5 us
    pallas_call x1, Pallas kernels, experts(): pl.pallas_call(functools.partial(expert_body, places), in_specs=[SCALARS]...  18 us
    pallas_call x4, Pallas kernels, outer(): pl.pallas_call(body, in_specs=[WHOLE] * 2 + [ORDER] * (1 + len(before)),...  15.2 us
    pallas_call x3, Pallas kernels, bring(): pl.pallas_call(functools.partial(bring_body, first), in_specs=[ORDER] * 3...  8.65 us
    ppermute x16, waiting for transfers between devices, swap(): return lax.ppermute(values, axis, [(i, i ^ mask) for i in range(size)])  5.84 us
    pallas_call x1, Pallas kernels, finish(): pl.pallas_call(functools.partial(finish_body, parts), in_specs=[SCALARS]...  3.24 us
    pallas_call x1, Pallas kernels, normalize(): pl.pallas_call(normalize_body, grid=(tok_count // step,), in_specs=[wide,...  3.07 us
    pallas_call x1, Pallas kernels, select(): pl.pallas_call(select_body, in_specs=[SCALARS] + [ORDER] * 3, out_specs=[...  2.55 us
  transfers between devices with their start and end apart: 16, of which 7 were waited for; matrix products, arithmetic and copies ran while one was open for 1% of the time, Pallas kernels for 34%

profile of v4, /device:TPU:0, one launch (start us, length us, event | category | flops | bytes accessed | tf_op | source)
XLA Modules:
  0.0 79.4 jit_solution(8900656896588034590)
XLA Ops:
  0.6 0.1 pad_add_fusion.place
  0.7 2.6 %select.22 = (bf16[16,4096]{1,0:T(8,128)(2,1)S(1)}, bf16[16,4096]{1,0:T(8,128)(2,1)S(1)}, f32[8,32]{1,0:T(8,128)S(1)}) custom-call(s32[2]{0:T(128)S(1)} %pad_add_fusion.place, s32[1,2,32]{2,1,0:T(2,128)} %picked_h.1, bf16[128,4096]{1,0:T(8,128)(2,1)} %tokens.1, bf16[128,4096]{1,0:T(8,128)(2,1)} %grads.1), custom_call_target="tpu_custom_call" | custom-call | tf_op jit(solution)/shard_map/select/pallas_call | solution.py:114
  3.3 4.1 %collective-permute-start = (bf16[16,4096]{1,0:T(8,128)(2,1)S(1)}, bf16[16,4096]{1,0:T(8,128)(2,1)S(1)}, u32[]{:S(2)}, u32[]{:S(2)}) collective-permute-start(bf16[16,4096]{1,0:T(8,128)(2,1)S(1)} %get-tuple-element.62), channel_id=1, source_target_pairs={{0,16},{4,20},{8,24},{12,28},{16,0},{20,4},{24,8},{28,12},{1,17},{... | collective-permute-start | bytes 393224 | tf_op jit(solution)/shard_map/ppermute | solution.py:537
  7.4 0.7 convert_bitcast_fusion
  8.1 0.0 copy-start
  8.2 2.3 %bring.3 = (bf16[1,4096,256]{2,1,0:T(8,128)(2,1)S(1)}, bf16[1,256,4096]{2,1,0:T(8,128)(2,1)S(1)}, f32[8,128]{1,0:T(8,128)S(1)}) custom-call(bf16[1,4096,2048]{2,1,0:T(8,128)(2,1)} %up_h.7, bf16[1,2048,4096]{2,1,0:T(8,128)(2,1)} %down_h.7, bf16[16,4096]{1,0:T(8,128)(2,1)S(1)} %get-tuple-element.61._.near_t.near_g), custom_call_target="tpu_custom_call" | custom-call | bytes 4194304 | tf_op jit(solution)/shard_map/bring/pallas_call | solution.py:151
  10.4 3.1 %normalize.1 = (f32[128,4096]{1,0:T(8,128)S(1)}, f32[128,128]{1,0:T(8,128)S(1)}, bf16[128,4096]{1,0:T(8,128)(2,1)S(1)}, bf16[128,4096]{1,0:T(8,128)(2,1)S(1)}, f...) custom-call(bf16[128,4096]{1,0:T(8,128)(2,1)} %tokens.1, bf16[128,4096]{1,0:T(8,128)(2,1)} %grads.1, ...), custom_call_target="tpu_custom_call" | custom-call | flops 5242880 | bytes 3145728 | tf_op jit(solution)/shard_map/normalize/pallas_call | solution.py:456
  13.5 0.2 collective-permute-done.far_t.far_g
  13.7 1.5 %collective-permute-start.1 = (bf16[16,4096]{1,0:T(8,128)(2,1)S(1)}, bf16[16,4096]{1,0:T(8,128)(2,1)S(1)}, u32[]{:S(2)}, u32[]{:S(2)}) collective-permute-start(bf16[16,4096]{1,0:T(8,128)(2,1)S(1)} %get-tuple-element.64._.near_t), channel_id=1, source_target_pairs={{0,8},{4,12},{8,0},{12,4},{16,24},{20,28},{24,16},{28,20},{1,9},{5... | collective-permute-start | bytes 393224 | tf_op jit(solution)/shard_map/ppermute | solution.py:537
  15.2 1.5 %collective-permute-start.2 = (bf16[16,4096]{1,0:T(8,128)(2,1)S(1)}, bf16[16,4096]{1,0:T(8,128)(2,1)S(1)}, u32[]{:S(2)}, u32[]{:S(2)}) collective-permute-start(bf16[16,4096]{1,0:T(8,128)(2,1)S(1)} %get-tuple-element.65.near_g), channel_id=1, source_target_pairs={{0,4},{4,0},{8,12},{12,8},{16,20},{20,16},{24,28},{28,24},{1,5},{5... | collective-permute-start | bytes 393224 | tf_op jit(solution)/shard_map/ppermute | solution.py:537
  16.7 0.0 copy-start.1
  16.7 2.3 %bring.4 = (bf16[1,4096,256]{2,1,0:T(8,128)(2,1)S(1)}, bf16[1,256,4096]{2,1,0:T(8,128)(2,1)S(1)}, f32[8,128]{1,0:T(8,128)S(1)}) custom-call(bf16[1,4096,2048]{2,1,0:T(8,128)(2,1)} %up_h.7, bf16[1,2048,4096]{2,1,0:T(8,128)(2,1)} %down_h.7, bf16[16,4096]{1,0:T(8,128)(2,1)S(1)} %get-tuple-element.64._.near_t), custom_call_target="tpu_custom_call" | custom-call | bytes 4194304 | tf_op jit(solution)/shard_map/bring/pallas_call | solution.py:151
  19.0 0.0 collective-permute-done.1.far_t
  19.0 1.1 %collective-permute-done.2.far_g = bf16[16,4096]{1,0:T(8,128)(2,1)S(1)} collective-permute-done((bf16[16,4096]{1,0:T(8,128)(2,1)S(1)}, bf16[16,4096]{1,0:T(8,128)(2,1)S(1)}, u32[]{:S(2)}, u32[]{:S(2)}) %collective-permute-start.2) | collective-permute-done | bytes 131104 | tf_op jit(solution)/shard_map/ppermute | solution.py:537
  20.2 1.6 %collective-permute-start.3 = (bf16[32,4096]{1,0:T(8,128)(2,1)S(1)}, bf16[32,4096]{1,0:T(8,128)(2,1)S(1)}, u32[]{:S(2)}, u32[]{:S(2)}) collective-permute-start(bf16[32,4096]{1,0:T(8,128)(2,1)S(1)} %get-tuple-element.67._.near_t), channel_id=1, source_target_pairs={{0,4},{4,0},{8,12},{12,8},{16,20},{20,16},{24,28},{28,24},{1,5},{5... | collective-permute-start | bytes 786440 | tf_op jit(solution)/shard_map/ppermute | solution.py:537
  21.8 0.7 collective-permute-start.4
  22.5 0.2 convert_reduce_fusion.counts
  22.6 4.1 %bring.5 = (bf16[2,4096,256]{2,1,0:T(8,128)(2,1)S(1)}, bf16[2,256,4096]{2,1,0:T(8,128)(2,1)S(1)}, f32[8,128]{1,0:T(8,128)}) custom-call(bf16[1,4096,2048]{2,1,0:T(8,128)(2,1)} %up_h.7, bf16[1,2048,4096]{2,1,0:T(8,128)(2,1)} %down_h.7, bf16[32,4096]{1,0:T(8,128)(2,1)S(1)} %get-tuple-element.67._.near_t), custom_call_target="tpu_custom_call" | custom-call | bytes 8388608 | tf_op jit(solution)/shard_map/bring/pallas_call | solution.py:151
  26.8 0.1 collective-permute-done.3.far_t
  26.9 1.3 %collective-permute-done.4.far_g = bf16[32,4096]{1,0:T(8,128)(2,1)S(1)} collective-permute-done((bf16[32,4096]{1,0:T(8,128)(2,1)S(1)}, bf16[32,4096]{1,0:T(8,128)(2,1)S(1)}, u32[]{:S(2)}, u32[]{:S(2)}) %collective-permute-start.4) | collective-permute-done | bytes 262176 | tf_op jit(solution)/shard_map/ppermute | solution.py:537
  28.2 18.0 %experts.1 = (bf16[64,4096]{1,0:T(8,128)(2,1)S(1)}, bf16[64,4096]{1,0:T(8,128)(2,1)S(1)}, bf16[64,2048]{1,0:T(8,128)(2,1)S(1)}, bf16[64,2048]{1,0:T(8,128)(2,1)S...) custom-call(s32[8]{0:T(128)S(1)} %convert_reduce_fusion.counts, ...), custom_call_target="tpu_custom_call" | custom-call | flops 4294967296 | bytes 33554432 | tf_op jit(solution)/shard_map/experts/pallas_call | solution.py:286
  46.2 0.6 collective-permute-start.5
  46.7 0.6 collective-permute-start.6
  47.4 6.4 %up_grad.1 = (bf16[1,4096,2048]{2,1,0:T(8,128)(2,1)}, f32[8,128]{1,0:T(8,128)S(1)}) custom-call(bf16[64,4096]{1,0:T(8,128)(2,1)S(1)} %get-tuple-element.84.left, bf16[64,2048]{1,0:T(8,128)(2,1)S(1)} %get-tuple-element.85.right, f32[128,128]{1,0:T(8,128)S(1)} %get-tuple-element.82._.side), custom_call_target="tpu_custom_call" | custom-call | flops 4294967296 | bytes 33554432 | tf_op jit(solution)/shard_map/up_grad/pallas_call | solution.py:336
  53.8 0.0 collective-permute-done.5.got_e
  53.8 0.0 collective-permute-done.6.got_b
  53.8 0.1 fold.2
  53.9 1.5 %collective-permute-start.7 = (bf16[16,4608]{1,0:T(8,128)(2,1)S(1)}, bf16[16,4608]{1,0:T(8,128)(2,1)S(1)}, u32[]{:S(2)}, u32[]{:S(2)}) collective-permute-start(bf16[16,4608]{1,0:T(8,128)(2,1)S(1)} %get-tuple-element.89), channel_id=1, source_target_pairs={{0,8},{4,12},{8,0},{12,4},{16,24},{20,28},{24,16},{28,20},{1,9},{5... | collective-permute-start | bytes 442376 | tf_op jit(solution)/shard_map/ppermute | solution.py:537
  55.4 1.5 %collective-permute-start.8 = (bf16[16,4608]{1,0:T(8,128)(2,1)S(1)}, bf16[16,4608]{1,0:T(8,128)(2,1)S(1)}, u32[]{:S(2)}, u32[]{:S(2)}) collective-permute-start(bf16[16,4608]{1,0:T(8,128)(2,1)S(1)} %get-tuple-element.90), channel_id=1, source_target_pairs={{0,4},{4,0},{8,12},{12,8},{16,20},{20,16},{24,28},{28,24},{1,5},{5... | collective-permute-start | bytes 442376 | tf_op jit(solution)/shard_map/ppermute | solution.py:537
  56.9 3.8 %down_grad.3 = (bf16[1,2048,4096]{2,1,0:T(8,128)(2,1)}, f32[8,128]{1,0:T(8,128)S(1)}) custom-call(bf16[64,2048]{1,0:T(8,128)(2,1)S(1)} %get-tuple-element.92.left, bf16[64,4096]{1,0:T(8,128)(2,1)S(1)} %get-tuple-element.93.right, f32[128,128]{1,0:T(8,128)S(1)} %get-tuple-element.91._.side), custom_call_target="tpu_custom_call" | custom-call | flops 2147483648 | bytes 16777216 | tf_op jit(solution)/shard_map/down_grad/pallas_call | solution.py:336
  60.7 0.0 collective-permute-done.7.got_e
  60.7 0.0 collective-permute-done.8.got_b
  60.8 0.1 fold.3
  60.8 3.3 %collective-permute-start.9 = (bf16[16,5120]{1,0:T(8,128)(2,1)S(1)}, bf16[16,5120]{1,0:T(8,128)(2,1)S(1)}, u32[]{:S(2)}, u32[]{:S(2)}) collective-permute-start(bf16[16,5120]{1,0:T(8,128)(2,1)S(1)} %get-tuple-element.96), channel_id=1, source_target_pairs={{0,16},{4,20},{8,24},{12,28},{16,0},{20,4},{24,8},{28,12},{1,17},{... | collective-permute-start | bytes 491528 | tf_op jit(solution)/shard_map/ppermute | solution.py:537
  64.2 1.5 %collective-permute-start.10 = (bf16[16,4224]{1,0:T(8,128)(2,1)S(1)}, bf16[16,4224]{1,0:T(8,128)(2,1)S(1)}, u32[]{:S(2)}, u32[]{:S(2)}) collective-permute-start(bf16[16,4224]{1,0:T(8,128)(2,1)S(1)} %get-tuple-element.101.refs_0_), channel_id=1, source_target_pairs={{0,2},{1,3},{2,0},{3,1},{4,6},{5,7},{6,4},{7,5},{8,10},{9,11},{10,... | collective-permute-start | bytes 405512 | tf_op jit(solution)/shard_map/ppermute | solution.py:537
  65.7 2.5 %down_grad.4 = (bf16[1,2048,4096]{2,1,0:T(8,128)(2,1)}, f32[8,128]{1,0:T(8,128)S(1)}) custom-call(bf16[64,2048]{1,0:T(8,128)(2,1)S(1)} %get-tuple-element.92.left, bf16[64,4096]{1,0:T(8,128)(2,1)S(1)} %get-tuple-element.93.right, f32[128,128]{1,0:T(8,128)S(1)} %get-tuple-element.95._.side, ...), custom_call_target="tpu_custom_call", output_to_operand_aliasing={{0}: (3, {})} | custom-call | flops 1073741824 | bytes 8388608 | tf_op jit(solution)/shard_map/down_grad/pallas_call | solution.py:336
  68.2 1.0 %collective-permute-done.9.got = bf16[16,5120]{1,0:T(8,128)(2,1)S(1)} collective-permute-done((bf16[16,5120]{1,0:T(8,128)(2,1)S(1)}, bf16[16,5120]{1,0:T(8,128)(2,1)S(1)}, u32[]{:S(2)}, u32[]{:S(2)}) %collective-permute-start.9) | collective-permute-done | bytes 163872 | tf_op jit(solution)/shard_map/ppermute | solution.py:537
  69.2 0.1 pack.1._.refs_4_
  69.3 1.5 %collective-permute-start.13 = (bf16[16,4992]{1,0:T(8,128)(2,1)S(1)}, bf16[16,4992]{1,0:T(8,128)(2,1)S(1)}, u32[]{:S(2)}, u32[]{:S(2)}) collective-permute-start(bf16[16,4992]{1,0:T(8,128)(2,1)S(1)} %pack.1._.refs_4_), channel_id=1, source_target_pairs={{0,2},{1,3},{2,0},{3,1},{4,6},{5,7},{6,4},{7,5},{8,10},{9,11},{10,... | collective-permute-start | bytes 479240 | tf_op jit(solution)/shard_map/ppermute | solution.py:537
  70.8 0.0 collective-permute-start.11
  70.8 0.0 collective-permute-done.10.refs_1_
  70.8 0.5 collective-permute-start.12
  71.3 0.0 collective-permute-start.14
  71.3 2.5 %down_grad.5 = (bf16[1,2048,4096]{2,1,0:T(8,128)(2,1)}, f32[8,128]{1,0:T(8,128)S(1)}) custom-call(bf16[64,2048]{1,0:T(8,128)(2,1)S(1)} %get-tuple-element.92.left, bf16[64,4096]{1,0:T(8,128)(2,1)S(1)} %get-tuple-element.93.right, bf16[16,4992]{1,0:T(8,128)(2,1)S(1)} %pack.1._.refs_4_, ...), custom_call_target="tpu_custom_call", output_to_operand_aliasing={{0}: (3, {})} | custom-call | flops 1073741824 | bytes 8388608 | tf_op jit(solution)/shard_map/down_grad/pallas_call | solution.py:336
  73.9 0.7 collective-permute-done.13.rows
  74.6 0.1 collective-permute-start.15
  74.7 1.4 %collective-permute-done.15.refs_7_ = bf16[16,4992]{1,0:T(8,128)(2,1)S(1)} collective-permute-done((bf16[16,4992]{1,0:T(8,128)(2,1)S(1)}, bf16[16,4992]{1,0:T(8,128)(2,1)S(1)}, u32[]{:S(2)}, u32[]{:S(2)}) %collective-permute-start.15) | collective-permute-done | bytes 159776 | tf_op jit(solution)/shard_map/ppermute | solution.py:537
  76.0 3.2 %finish.1 = (bf16[128,4096]{1,0:T(8,128)(2,1)}, bf16[128,4096]{1,0:T(8,128)(2,1)}, f32[32,128]{1,0:T(8,128)}, f32[32,128]{1,0:T(8,128)}, f32[32,128]{1,0:T(8,128)}, /*index=5*/f32[2,4096]{1,0:T(2,128)}) custom-call(s32[2]{0:T(128)S(1)} %pad_add_fusion.place, f32[128,128]{1,0:T(8,128)S(1)} %get-tuple-element.95._.side, ...), custom_call_target="tpu_custom_call" | custom-call | tf_op jit(solution)/shard_map/finish/pallas_call | solution.py:519
  (11 shorter events, 0.1 us)
Async XLA Ops:
  3.3 10.4 %collective-permute-start = (bf16[16,4096]{1,0:T(8,128)(2,1)S(1)}, bf16[16,4096]{1,0:T(8,128)(2,1)S(1)}, u32[]{:S(2)}, u32[]{:S(2)}) collective-permute-start(bf16[16,4096]{1,0:T(8,128)(2,1)S(1)} %get-tuple-element.62), channel_id=1, source_target_pairs={{0,16},{4,20},{8,24},{12,28},{16,0},{20,4},{24,8},{28,12},{1,17},{... | collective-permute-start | bytes 393224 | tf_op jit(solution)/shard_map/ppermute | solution.py:537
  8.1 8.6 %copy-start = (s32[1,2,32]{2,1,0:T(2,128)S(1)}, s32[1,2,32]{2,1,0:T(2,128)}, u32[]{:S(2)}) copy-start(s32[1,2,32]{2,1,0:T(2,128)} %picked_h.1) | copy-start | bytes 772
  13.7 5.3 %collective-permute-start.1 = (bf16[16,4096]{1,0:T(8,128)(2,1)S(1)}, bf16[16,4096]{1,0:T(8,128)(2,1)S(1)}, u32[]{:S(2)}, u32[]{:S(2)}) collective-permute-start(bf16[16,4096]{1,0:T(8,128)(2,1)S(1)} %get-tuple-element.64._.near_t), channel_id=1, source_target_pairs={{0,8},{4,12},{8,0},{12,4},{16,24},{20,28},{24,16},{28,20},{1,9},{5... | collective-permute-start | bytes 393224 | tf_op jit(solution)/shard_map/ppermute | solution.py:537
  15.2 5.0 %collective-permute-start.2 = (bf16[16,4096]{1,0:T(8,128)(2,1)S(1)}, bf16[16,4096]{1,0:T(8,128)(2,1)S(1)}, u32[]{:S(2)}, u32[]{:S(2)}) collective-permute-start(bf16[16,4096]{1,0:T(8,128)(2,1)S(1)} %get-tuple-element.65.near_g), channel_id=1, source_target_pairs={{0,4},{4,0},{8,12},{12,8},{16,20},{20,16},{24,28},{28,24},{1,5},{5... | collective-permute-start | bytes 393224 | tf_op jit(solution)/shard_map/ppermute | solution.py:537
  16.7 5.7 %copy-start.1 = (s32[8]{0:T(128)S(1)}, s32[8]{0:T(128)}, u32[]{:S(2)}) copy-start(s32[8]{0:T(128)} %constant.38.clone) | copy-start | bytes 100
  20.2 6.7 %collective-permute-start.3 = (bf16[32,4096]{1,0:T(8,128)(2,1)S(1)}, bf16[32,4096]{1,0:T(8,128)(2,1)S(1)}, u32[]{:S(2)}, u32[]{:S(2)}) collective-permute-start(bf16[32,4096]{1,0:T(8,128)(2,1)S(1)} %get-tuple-element.67._.near_t), channel_id=1, source_target_pairs={{0,4},{4,0},{8,12},{12,8},{16,20},{20,16},{24,28},{28,24},{1,5},{5... | collective-permute-start | bytes 786440 | tf_op jit(solution)/shard_map/ppermute | solution.py:537
  21.8 6.4 %collective-permute-start.4 = (bf16[32,4096]{1,0:T(8,128)(2,1)S(1)}, bf16[32,4096]{1,0:T(8,128)(2,1)S(1)}, u32[]{:S(2)}, u32[]{:S(2)}) collective-permute-start(bf16[32,4096]{1,0:T(8,128)(2,1)S(1)} %get-tuple-element.68.near_g), channel_id=1, source_target_pairs={{0,8},{4,12},{8,0},{12,4},{16,24},{20,28},{24,16},{28,20},{1,9},{5... | collective-permute-start | bytes 786440 | tf_op jit(solution)/shard_map/ppermute | solution.py:537
  46.2 7.6 %collective-permute-start.5 = (bf16[32,4352]{1,0:T(8,128)(2,1)S(1)}, bf16[32,4352]{1,0:T(8,128)(2,1)S(1)}, u32[]{:S(2)}, u32[]{:S(2)}) collective-permute-start(bf16[32,4352]{1,0:T(8,128)(2,1)S(1)} %get-tuple-element.80), channel_id=1, source_target_pairs={{0,4},{4,0},{8,12},{12,8},{16,20},{20,16},{24,28},{28,24},{1,5},{5... | collective-permute-start | bytes 835592 | tf_op jit(solution)/shard_map/ppermute | solution.py:537
  46.7 7.1 %collective-permute-start.6 = (bf16[32,4352]{1,0:T(8,128)(2,1)S(1)}, bf16[32,4352]{1,0:T(8,128)(2,1)S(1)}, u32[]{:S(2)}, u32[]{:S(2)}) collective-permute-start(bf16[32,4352]{1,0:T(8,128)(2,1)S(1)} %get-tuple-element.81), channel_id=1, source_target_pairs={{0,8},{4,12},{8,0},{12,4},{16,24},{20,28},{24,16},{28,20},{1,9},{5... | collective-permute-start | bytes 835592 | tf_op jit(solution)/shard_map/ppermute | solution.py:537
  53.9 6.8 %collective-permute-start.7 = (bf16[16,4608]{1,0:T(8,128)(2,1)S(1)}, bf16[16,4608]{1,0:T(8,128)(2,1)S(1)}, u32[]{:S(2)}, u32[]{:S(2)}) collective-permute-start(bf16[16,4608]{1,0:T(8,128)(2,1)S(1)} %get-tuple-element.89), channel_id=1, source_target_pairs={{0,8},{4,12},{8,0},{12,4},{16,24},{20,28},{24,16},{28,20},{1,9},{5... | collective-permute-start | bytes 442376 | tf_op jit(solution)/shard_map/ppermute | solution.py:537
  55.4 5.4 %collective-permute-start.8 = (bf16[16,4608]{1,0:T(8,128)(2,1)S(1)}, bf16[16,4608]{1,0:T(8,128)(2,1)S(1)}, u32[]{:S(2)}, u32[]{:S(2)}) collective-permute-start(bf16[16,4608]{1,0:T(8,128)(2,1)S(1)} %get-tuple-element.90), channel_id=1, source_target_pairs={{0,4},{4,0},{8,12},{12,8},{16,20},{20,16},{24,28},{28,24},{1,5},{5... | collective-permute-start | bytes 442376 | tf_op jit(solution)/shard_map/ppermute | solution.py:537
  60.8 8.4 %collective-permute-start.9 = (bf16[16,5120]{1,0:T(8,128)(2,1)S(1)}, bf16[16,5120]{1,0:T(8,128)(2,1)S(1)}, u32[]{:S(2)}, u32[]{:S(2)}) collective-permute-start(bf16[16,5120]{1,0:T(8,128)(2,1)S(1)} %get-tuple-element.96), channel_id=1, source_target_pairs={{0,16},{4,20},{8,24},{12,28},{16,0},{20,4},{24,8},{28,12},{1,17},{... | collective-permute-start | bytes 491528 | tf_op jit(solution)/shard_map/ppermute | solution.py:537
  64.2 6.7 %collective-permute-start.10 = (bf16[16,4224]{1,0:T(8,128)(2,1)S(1)}, bf16[16,4224]{1,0:T(8,128)(2,1)S(1)}, u32[]{:S(2)}, u32[]{:S(2)}) collective-permute-start(bf16[16,4224]{1,0:T(8,128)(2,1)S(1)} %get-tuple-element.101.refs_0_), channel_id=1, source_target_pairs={{0,2},{1,3},{2,0},{3,1},{4,6},{5,7},{6,4},{7,5},{8,10},{9,11},{10,... | collective-permute-start | bytes 405512 | tf_op jit(solution)/shard_map/ppermute | solution.py:537
  69.3 5.3 %collective-permute-start.13 = (bf16[16,4992]{1,0:T(8,128)(2,1)S(1)}, bf16[16,4992]{1,0:T(8,128)(2,1)S(1)}, u32[]{:S(2)}, u32[]{:S(2)}) collective-permute-start(bf16[16,4992]{1,0:T(8,128)(2,1)S(1)} %pack.1._.refs_4_), channel_id=1, source_target_pairs={{0,2},{1,3},{2,0},{3,1},{4,6},{5,7},{6,4},{7,5},{8,10},{9,11},{10,... | collective-permute-start | bytes 479240 | tf_op jit(solution)/shard_map/ppermute | solution.py:537
  70.8 3.0 %collective-permute-start.11 = (bf16[16,4224]{1,0:T(8,128)(2,1)S(1)}, bf16[16,4224]{1,0:T(8,128)(2,1)S(1)}, u32[]{:S(2)}, u32[]{:S(2)}) collective-permute-start(bf16[16,4224]{1,0:T(8,128)(2,1)S(1)} %get-tuple-element.101.refs_0_), channel_id=1, source_target_pairs={{0,1},{1,0},{2,3},{3,2},{4,5},{5,4},{6,7},{7,6},{8,9},{9,8},{10,11... | collective-permute-start | bytes 405512 | tf_op jit(solution)/shard_map/ppermute | solution.py:537
  70.8 3.0 %collective-permute-start.12 = (bf16[16,4224]{1,0:T(8,128)(2,1)S(1)}, bf16[16,4224]{1,0:T(8,128)(2,1)S(1)}, u32[]{:S(2)}, u32[]{:S(2)}) collective-permute-start(bf16[16,4224]{1,0:T(8,128)(2,1)S(1)} %collective-permute-done.10.refs_1_), channel_id=1, source_target_pairs={{0,1},{1,0},{2,3},{3,2},{4,5},{5,4},{6,7},{7,6},{8,9},{9,8},{10,11... | collective-permute-start | bytes 405512 | tf_op jit(solution)/shard_map/ppermute | solution.py:537
  71.3 3.4 %collective-permute-start.14 = (bf16[16,4992]{1,0:T(8,128)(2,1)S(1)}, bf16[16,4992]{1,0:T(8,128)(2,1)S(1)}, u32[]{:S(2)}, u32[]{:S(2)}) collective-permute-start(bf16[16,4992]{1,0:T(8,128)(2,1)S(1)} %pack.1._.refs_4_), channel_id=1, source_target_pairs={{0,1},{1,0},{2,3},{3,2},{4,5},{5,4},{6,7},{7,6},{8,9},{9,8},{10,11... | collective-permute-start | bytes 479240 | tf_op jit(solution)/shard_map/ppermute | solution.py:537
  74.6 1.5 %collective-permute-start.15 = (bf16[16,4992]{1,0:T(8,128)(2,1)S(1)}, bf16[16,4992]{1,0:T(8,128)(2,1)S(1)}, u32[]{:S(2)}, u32[]{:S(2)}) collective-permute-start(bf16[16,4992]{1,0:T(8,128)(2,1)S(1)} %relay.1.refs_5_), channel_id=1, source_target_pairs={{0,1},{1,0},{2,3},{3,2},{4,5},{5,4},{6,7},{7,6},{8,9},{9,8},{10,11... | collective-permute-start | bytes 479240 | tf_op jit(solution)/shard_map/ppermute | solution.py:537

commit v5 on v4

--- a/solution.py
+++ b/solution.py
@@ -606,13 +606,13 @@
         if step == 0:
             up_grad, behind = outer(hidden, grad_pre, behind, "up_grad", 0, 4)
         elif step == 1:
-            down_grad, behind = outer(act, grad_rows, behind, "down_grad", 0, 2)
+            down_grad, behind = outer(act, grad_rows, behind, "down_grad", 0, 1)
         side, *rest = fold(keep, got, side, ids, behind)
         keep, send = rest[:-2], rest[-2:]
         behind = side
     mine, send = rest
     got = swap(send, "ctx", ctx_masks[0])
-    down_grad, behind = outer(act, grad_rows, behind, "down_grad", 2, 1, down_grad)
+    down_grad, behind = outer(act, grad_rows, behind, "down_grad", 1, 2, down_grad)
     come = swap(mine, "exp", exp_masks[0])
     pieces = [mine, come]
     mine = pack(width, got, side, ids, behind)

time: 79.7 us -> 79.8 us (level)
  no operation moved by 1% of the time
where the time goes in v5:
time: 79.8 us; the launch traced here: 79.5 us
  Pallas kernels  51.1 us (64%)
  starting transfers between devices  20.2 us (25%)
  waiting for transfers between devices  6.2 us (8%)
  other arithmetic  1.02 us (1%)
  between operations  1.02 us (1%)
    ppermute x16, starting transfers between devices, swap(): return lax.ppermute(values, axis, [(i, i ^ mask) for i in range(size)])  20.2 us
    pallas_call x1, Pallas kernels, experts(): pl.pallas_call(functools.partial(expert_body, places), in_specs=[SCALARS]...  18 us
    pallas_call x4, Pallas kernels, outer(): pl.pallas_call(body, in_specs=[WHOLE] * 2 + [ORDER] * (1 + len(before)),...  15.2 us
    pallas_call x3, Pallas kernels, bring(): pl.pallas_call(functools.partial(bring_body, first), in_specs=[ORDER] * 3...  8.65 us
    ppermute x16, waiting for transfers between devices, swap(): return lax.ppermute(values, axis, [(i, i ^ mask) for i in range(size)])  6.2 us
    pallas_call x1, Pallas kernels, finish(): pl.pallas_call(functools.partial(finish_body, parts), in_specs=[SCALARS]...  3.25 us
    pallas_call x1, Pallas kernels, normalize(): pl.pallas_call(normalize_body, grid=(tok_count // step,), in_specs=[wide,...  3.07 us
    pallas_call x1, Pallas kernels, select(): pl.pallas_call(select_body, in_specs=[SCALARS] + [ORDER] * 3, out_specs=[...  2.55 us
  transfers between devices with their start and end apart: 16, of which 7 were waited for; matrix products, arithmetic and copies ran while one was open for 1% of the time, Pallas kernels for 34%

profile of v5, /device:TPU:0, one launch (start us, length us, event | category | flops | bytes accessed | tf_op | source)
XLA Modules:
  0.0 79.5 jit_solution(18240234769604857573)
XLA Ops:
  0.6 0.1 pad_add_fusion.place
  0.7 2.6 %select.22 = (bf16[16,4096]{1,0:T(8,128)(2,1)S(1)}, bf16[16,4096]{1,0:T(8,128)(2,1)S(1)}, f32[8,32]{1,0:T(8,128)S(1)}) custom-call(s32[2]{0:T(128)S(1)} %pad_add_fusion.place, s32[1,2,32]{2,1,0:T(2,128)} %picked_h.1, bf16[128,4096]{1,0:T(8,128)(2,1)} %tokens.1, bf16[128,4096]{1,0:T(8,128)(2,1)} %grads.1), custom_call_target="tpu_custom_call" | custom-call | tf_op jit(solution)/shard_map/select/pallas_call | solution.py:114
  3.3 4.1 %collective-permute-start = (bf16[16,4096]{1,0:T(8,128)(2,1)S(1)}, bf16[16,4096]{1,0:T(8,128)(2,1)S(1)}, u32[]{:S(2)}, u32[]{:S(2)}) collective-permute-start(bf16[16,4096]{1,0:T(8,128)(2,1)S(1)} %get-tuple-element.62), channel_id=1, source_target_pairs={{0,16},{4,20},{8,24},{12,28},{16,0},{20,4},{24,8},{28,12},{1,17},{... | collective-permute-start | bytes 393224 | tf_op jit(solution)/shard_map/ppermute | solution.py:537
  7.4 0.7 convert_bitcast_fusion
  8.1 0.0 copy-start
  8.2 2.3 %bring.3 = (bf16[1,4096,256]{2,1,0:T(8,128)(2,1)S(1)}, bf16[1,256,4096]{2,1,0:T(8,128)(2,1)S(1)}, f32[8,128]{1,0:T(8,128)S(1)}) custom-call(bf16[1,4096,2048]{2,1,0:T(8,128)(2,1)} %up_h.7, bf16[1,2048,4096]{2,1,0:T(8,128)(2,1)} %down_h.7, bf16[16,4096]{1,0:T(8,128)(2,1)S(1)} %get-tuple-element.61._.near_t.near_g), custom_call_target="tpu_custom_call" | custom-call | bytes 4194304 | tf_op jit(solution)/shard_map/bring/pallas_call | solution.py:151
  10.4 3.1 %normalize.1 = (f32[128,4096]{1,0:T(8,128)S(1)}, f32[128,128]{1,0:T(8,128)S(1)}, bf16[128,4096]{1,0:T(8,128)(2,1)S(1)}, bf16[128,4096]{1,0:T(8,128)(2,1)S(1)}, f...) custom-call(bf16[128,4096]{1,0:T(8,128)(2,1)} %tokens.1, bf16[128,4096]{1,0:T(8,128)(2,1)} %grads.1, ...), custom_call_target="tpu_custom_call" | custom-call | flops 5242880 | bytes 3145728 | tf_op jit(solution)/shard_map/normalize/pallas_call | solution.py:456
  13.5 0.2 collective-permute-done.far_t.far_g
  13.7 1.5 %collective-permute-start.1 = (bf16[16,4096]{1,0:T(8,128)(2,1)S(1)}, bf16[16,4096]{1,0:T(8,128)(2,1)S(1)}, u32[]{:S(2)}, u32[]{:S(2)}) collective-permute-start(bf16[16,4096]{1,0:T(8,128)(2,1)S(1)} %get-tuple-element.64._.near_t), channel_id=1, source_target_pairs={{0,8},{4,12},{8,0},{12,4},{16,24},{20,28},{24,16},{28,20},{1,9},{5... | collective-permute-start | bytes 393224 | tf_op jit(solution)/shard_map/ppermute | solution.py:537
  15.2 1.5 %collective-permute-start.2 = (bf16[16,4096]{1,0:T(8,128)(2,1)S(1)}, bf16[16,4096]{1,0:T(8,128)(2,1)S(1)}, u32[]{:S(2)}, u32[]{:S(2)}) collective-permute-start(bf16[16,4096]{1,0:T(8,128)(2,1)S(1)} %get-tuple-element.65.near_g), channel_id=1, source_target_pairs={{0,4},{4,0},{8,12},{12,8},{16,20},{20,16},{24,28},{28,24},{1,5},{5... | collective-permute-start | bytes 393224 | tf_op jit(solution)/shard_map/ppermute | solution.py:537
  16.7 0.0 copy-start.1
  16.7 2.3 %bring.4 = (bf16[1,4096,256]{2,1,0:T(8,128)(2,1)S(1)}, bf16[1,256,4096]{2,1,0:T(8,128)(2,1)S(1)}, f32[8,128]{1,0:T(8,128)S(1)}) custom-call(bf16[1,4096,2048]{2,1,0:T(8,128)(2,1)} %up_h.7, bf16[1,2048,4096]{2,1,0:T(8,128)(2,1)} %down_h.7, bf16[16,4096]{1,0:T(8,128)(2,1)S(1)} %get-tuple-element.64._.near_t), custom_call_target="tpu_custom_call" | custom-call | bytes 4194304 | tf_op jit(solution)/shard_map/bring/pallas_call | solution.py:151
  19.0 1.1 %collective-permute-done.2.far_g = bf16[16,4096]{1,0:T(8,128)(2,1)S(1)} collective-permute-done((bf16[16,4096]{1,0:T(8,128)(2,1)S(1)}, bf16[16,4096]{1,0:T(8,128)(2,1)S(1)}, u32[]{:S(2)}, u32[]{:S(2)}) %collective-permute-start.2) | collective-permute-done | bytes 131104 | tf_op jit(solution)/shard_map/ppermute | solution.py:537
  20.2 1.6 %collective-permute-start.3 = (bf16[32,4096]{1,0:T(8,128)(2,1)S(1)}, bf16[32,4096]{1,0:T(8,128)(2,1)S(1)}, u32[]{:S(2)}, u32[]{:S(2)}) collective-permute-start(bf16[32,4096]{1,0:T(8,128)(2,1)S(1)} %get-tuple-element.67._.near_t), channel_id=1, source_target_pairs={{0,4},{4,0},{8,12},{12,8},{16,20},{20,16},{24,28},{28,24},{1,5},{5... | collective-permute-start | bytes 786440 | tf_op jit(solution)/shard_map/ppermute | solution.py:537
  21.8 0.7 collective-permute-start.4
  22.5 0.2 convert_reduce_fusion.counts
  22.6 4.1 %bring.5 = (bf16[2,4096,256]{2,1,0:T(8,128)(2,1)S(1)}, bf16[2,256,4096]{2,1,0:T(8,128)(2,1)S(1)}, f32[8,128]{1,0:T(8,128)}) custom-call(bf16[1,4096,2048]{2,1,0:T(8,128)(2,1)} %up_h.7, bf16[1,2048,4096]{2,1,0:T(8,128)(2,1)} %down_h.7, bf16[32,4096]{1,0:T(8,128)(2,1)S(1)} %get-tuple-element.67._.near_t), custom_call_target="tpu_custom_call" | custom-call | bytes 8388608 | tf_op jit(solution)/shard_map/bring/pallas_call | solution.py:151
  26.8 0.1 collective-permute-done.3.far_t
  26.9 1.3 %collective-permute-done.4.far_g = bf16[32,4096]{1,0:T(8,128)(2,1)S(1)} collective-permute-done((bf16[32,4096]{1,0:T(8,128)(2,1)S(1)}, bf16[32,4096]{1,0:T(8,128)(2,1)S(1)}, u32[]{:S(2)}, u32[]{:S(2)}) %collective-permute-start.4) | collective-permute-done | bytes 262176 | tf_op jit(solution)/shard_map/ppermute | solution.py:537
  28.2 18.0 %experts.1 = (bf16[64,4096]{1,0:T(8,128)(2,1)S(1)}, bf16[64,4096]{1,0:T(8,128)(2,1)S(1)}, bf16[64,2048]{1,0:T(8,128)(2,1)S(1)}, bf16[64,2048]{1,0:T(8,128)(2,1)S...) custom-call(s32[8]{0:T(128)S(1)} %convert_reduce_fusion.counts, ...), custom_call_target="tpu_custom_call" | custom-call | flops 4294967296 | bytes 33554432 | tf_op jit(solution)/shard_map/experts/pallas_call | solution.py:286
  46.2 0.6 collective-permute-start.5
  46.7 0.6 collective-permute-start.6
  47.4 6.4 %up_grad.1 = (bf16[1,4096,2048]{2,1,0:T(8,128)(2,1)}, f32[8,128]{1,0:T(8,128)S(1)}) custom-call(bf16[64,4096]{1,0:T(8,128)(2,1)S(1)} %get-tuple-element.84.left, bf16[64,2048]{1,0:T(8,128)(2,1)S(1)} %get-tuple-element.85.right, f32[128,128]{1,0:T(8,128)S(1)} %get-tuple-element.82._.side), custom_call_target="tpu_custom_call" | custom-call | flops 4294967296 | bytes 33554432 | tf_op jit(solution)/shard_map/up_grad/pallas_call | solution.py:336
  53.8 0.0 collective-permute-done.5.got_e
  53.8 0.0 collective-permute-done.6.got_b
  53.8 0.1 fold.2
  53.9 1.5 %collective-permute-start.7 = (bf16[16,4608]{1,0:T(8,128)(2,1)S(1)}, bf16[16,4608]{1,0:T(8,128)(2,1)S(1)}, u32[]{:S(2)}, u32[]{:S(2)}) collective-permute-start(bf16[16,4608]{1,0:T(8,128)(2,1)S(1)} %get-tuple-element.89), channel_id=1, source_target_pairs={{0,8},{4,12},{8,0},{12,4},{16,24},{20,28},{24,16},{28,20},{1,9},{5... | collective-permute-start | bytes 442376 | tf_op jit(solution)/shard_map/ppermute | solution.py:537
  55.4 1.5 %collective-permute-start.8 = (bf16[16,4608]{1,0:T(8,128)(2,1)S(1)}, bf16[16,4608]{1,0:T(8,128)(2,1)S(1)}, u32[]{:S(2)}, u32[]{:S(2)}) collective-permute-start(bf16[16,4608]{1,0:T(8,128)(2,1)S(1)} %get-tuple-element.90), channel_id=1, source_target_pairs={{0,4},{4,0},{8,12},{12,8},{16,20},{20,16},{24,28},{28,24},{1,5},{5... | collective-permute-start | bytes 442376 | tf_op jit(solution)/shard_map/ppermute | solution.py:537
  56.9 2.5 %down_grad.3 = (bf16[1,2048,4096]{2,1,0:T(8,128)(2,1)}, f32[8,128]{1,0:T(8,128)S(1)}) custom-call(bf16[64,2048]{1,0:T(8,128)(2,1)S(1)} %get-tuple-element.92.left, bf16[64,4096]{1,0:T(8,128)(2,1)S(1)} %get-tuple-element.93.right, f32[128,128]{1,0:T(8,128)S(1)} %get-tuple-element.91._.side), custom_call_target="tpu_custom_call" | custom-call | flops 1073741824 | bytes 8388608 | tf_op jit(solution)/shard_map/down_grad/pallas_call | solution.py:336
  59.4 1.1 %collective-permute-done.8.got_b = bf16[16,4608]{1,0:T(8,128)(2,1)S(1)} collective-permute-done((bf16[16,4608]{1,0:T(8,128)(2,1)S(1)}, bf16[16,4608]{1,0:T(8,128)(2,1)S(1)}, u32[]{:S(2)}, u32[]{:S(2)}) %collective-permute-start.8) | collective-permute-done | bytes 147488 | tf_op jit(solution)/shard_map/ppermute | solution.py:537
  60.5 0.1 fold.3
  60.6 3.3 %collective-permute-start.9 = (bf16[16,5120]{1,0:T(8,128)(2,1)S(1)}, bf16[16,5120]{1,0:T(8,128)(2,1)S(1)}, u32[]{:S(2)}, u32[]{:S(2)}) collective-permute-start(bf16[16,5120]{1,0:T(8,128)(2,1)S(1)} %get-tuple-element.96), channel_id=1, source_target_pairs={{0,16},{4,20},{8,24},{12,28},{16,0},{20,4},{24,8},{28,12},{1,17},{... | collective-permute-start | bytes 491528 | tf_op jit(solution)/shard_map/ppermute | solution.py:537
  63.9 1.5 %collective-permute-start.10 = (bf16[16,4224]{1,0:T(8,128)(2,1)S(1)}, bf16[16,4224]{1,0:T(8,128)(2,1)S(1)}, u32[]{:S(2)}, u32[]{:S(2)}) collective-permute-start(bf16[16,4224]{1,0:T(8,128)(2,1)S(1)} %get-tuple-element.101.refs_0_), channel_id=1, source_target_pairs={{0,2},{1,3},{2,0},{3,1},{4,6},{5,7},{6,4},{7,5},{8,10},{9,11},{10,... | collective-permute-start | bytes 405512 | tf_op jit(solution)/shard_map/ppermute | solution.py:537
  65.4 3.8 %down_grad.4 = (bf16[1,2048,4096]{2,1,0:T(8,128)(2,1)}, f32[8,128]{1,0:T(8,128)S(1)}) custom-call(bf16[64,2048]{1,0:T(8,128)(2,1)S(1)} %get-tuple-element.92.left, bf16[64,4096]{1,0:T(8,128)(2,1)S(1)} %get-tuple-element.93.right, f32[128,128]{1,0:T(8,128)S(1)} %get-tuple-element.95._.side, ...), custom_call_target="tpu_custom_call", output_to_operand_aliasing={{0}: (3, {})} | custom-call | flops 2147483648 | bytes 16777216 | tf_op jit(solution)/shard_map/down_grad/pallas_call | solution.py:336
  69.3 0.0 collective-permute-done.9.got
  69.3 0.1 pack.1._.refs_4_
  69.4 1.2 %collective-permute-start.13 = (bf16[16,4992]{1,0:T(8,128)(2,1)S(1)}, bf16[16,4992]{1,0:T(8,128)(2,1)S(1)}, u32[]{:S(2)}, u32[]{:S(2)}) collective-permute-start(bf16[16,4992]{1,0:T(8,128)(2,1)S(1)} %pack.1._.refs_4_), channel_id=1, source_target_pairs={{0,2},{1,3},{2,0},{3,1},{4,6},{5,7},{6,4},{7,5},{8,10},{9,11},{10,... | collective-permute-start | bytes 479240 | tf_op jit(solution)/shard_map/ppermute | solution.py:537
  70.6 0.0 collective-permute-start.11
  70.6 0.0 collective-permute-done.10.refs_1_
  70.6 0.5 collective-permute-start.12
  71.1 0.0 collective-permute-start.14
  71.1 2.5 %down_grad.5 = (bf16[1,2048,4096]{2,1,0:T(8,128)(2,1)}, f32[8,128]{1,0:T(8,128)S(1)}) custom-call(bf16[64,2048]{1,0:T(8,128)(2,1)S(1)} %get-tuple-element.92.left, bf16[64,4096]{1,0:T(8,128)(2,1)S(1)} %get-tuple-element.93.right, bf16[16,4992]{1,0:T(8,128)(2,1)S(1)} %pack.1._.refs_4_, ...), custom_call_target="tpu_custom_call", output_to_operand_aliasing={{0}: (3, {})} | custom-call | flops 1073741824 | bytes 8388608 | tf_op jit(solution)/shard_map/down_grad/pallas_call | solution.py:336
  73.6 0.0 collective-permute-done.11.refs_1_.refs_2_
  73.6 0.0 collective-permute-done.12.refs_2_.refs_3_
  73.6 1.0 %collective-permute-done.13.rows = bf16[16,4992]{1,0:T(8,128)(2,1)S(1)} collective-permute-done((bf16[16,4992]{1,0:T(8,128)(2,1)S(1)}, bf16[16,4992]{1,0:T(8,128)(2,1)S(1)}, u32[]{:S(2)}, u32[]{:S(2)}) %collective-permute-start.13) | collective-permute-done | bytes 159776 | tf_op jit(solution)/shard_map/ppermute | solution.py:537
  74.7 0.1 collective-permute-start.15
  74.7 1.4 %collective-permute-done.15.refs_7_ = bf16[16,4992]{1,0:T(8,128)(2,1)S(1)} collective-permute-done((bf16[16,4992]{1,0:T(8,128)(2,1)S(1)}, bf16[16,4992]{1,0:T(8,128)(2,1)S(1)}, u32[]{:S(2)}, u32[]{:S(2)}) %collective-permute-start.15) | collective-permute-done | bytes 159776 | tf_op jit(solution)/shard_map/ppermute | solution.py:537
  76.1 3.2 %finish.1 = (bf16[128,4096]{1,0:T(8,128)(2,1)}, bf16[128,4096]{1,0:T(8,128)(2,1)}, f32[32,128]{1,0:T(8,128)}, f32[32,128]{1,0:T(8,128)}, f32[32,128]{1,0:T(8,128)}, /*index=5*/f32[2,4096]{1,0:T(2,128)}) custom-call(s32[2]{0:T(128)S(1)} %pad_add_fusion.place, f32[128,128]{1,0:T(8,128)S(1)} %get-tuple-element.95._.side, ...), custom_call_target="tpu_custom_call" | custom-call | tf_op jit(solution)/shard_map/finish/pallas_call | solution.py:519
  (11 shorter events, 0.1 us)
Async XLA Ops:
  3.3 10.4 %collective-permute-start = (bf16[16,4096]{1,0:T(8,128)(2,1)S(1)}, bf16[16,4096]{1,0:T(8,128)(2,1)S(1)}, u32[]{:S(2)}, u32[]{:S(2)}) collective-permute-start(bf16[16,4096]{1,0:T(8,128)(2,1)S(1)} %get-tuple-element.62), channel_id=1, source_target_pairs={{0,16},{4,20},{8,24},{12,28},{16,0},{20,4},{24,8},{28,12},{1,17},{... | collective-permute-start | bytes 393224 | tf_op jit(solution)/shard_map/ppermute | solution.py:537
  8.1 8.6 %copy-start = (s32[1,2,32]{2,1,0:T(2,128)S(1)}, s32[1,2,32]{2,1,0:T(2,128)}, u32[]{:S(2)}) copy-start(s32[1,2,32]{2,1,0:T(2,128)} %picked_h.1) | copy-start | bytes 772
  13.7 5.3 %collective-permute-start.1 = (bf16[16,4096]{1,0:T(8,128)(2,1)S(1)}, bf16[16,4096]{1,0:T(8,128)(2,1)S(1)}, u32[]{:S(2)}, u32[]{:S(2)}) collective-permute-start(bf16[16,4096]{1,0:T(8,128)(2,1)S(1)} %get-tuple-element.64._.near_t), channel_id=1, source_target_pairs={{0,8},{4,12},{8,0},{12,4},{16,24},{20,28},{24,16},{28,20},{1,9},{5... | collective-permute-start | bytes 393224 | tf_op jit(solution)/shard_map/ppermute | solution.py:537
  15.2 5.0 %collective-permute-start.2 = (bf16[16,4096]{1,0:T(8,128)(2,1)S(1)}, bf16[16,4096]{1,0:T(8,128)(2,1)S(1)}, u32[]{:S(2)}, u32[]{:S(2)}) collective-permute-start(bf16[16,4096]{1,0:T(8,128)(2,1)S(1)} %get-tuple-element.65.near_g), channel_id=1, source_target_pairs={{0,4},{4,0},{8,12},{12,8},{16,20},{20,16},{24,28},{28,24},{1,5},{5... | collective-permute-start | bytes 393224 | tf_op jit(solution)/shard_map/ppermute | solution.py:537
  16.7 5.7 %copy-start.1 = (s32[8]{0:T(128)S(1)}, s32[8]{0:T(128)}, u32[]{:S(2)}) copy-start(s32[8]{0:T(128)} %constant.38.clone) | copy-start | bytes 100
  20.2 6.7 %collective-permute-start.3 = (bf16[32,4096]{1,0:T(8,128)(2,1)S(1)}, bf16[32,4096]{1,0:T(8,128)(2,1)S(1)}, u32[]{:S(2)}, u32[]{:S(2)}) collective-permute-start(bf16[32,4096]{1,0:T(8,128)(2,1)S(1)} %get-tuple-element.67._.near_t), channel_id=1, source_target_pairs={{0,4},{4,0},{8,12},{12,8},{16,20},{20,16},{24,28},{28,24},{1,5},{5... | collective-permute-start | bytes 786440 | tf_op jit(solution)/shard_map/ppermute | solution.py:537
  21.8 6.4 %collective-permute-start.4 = (bf16[32,4096]{1,0:T(8,128)(2,1)S(1)}, bf16[32,4096]{1,0:T(8,128)(2,1)S(1)}, u32[]{:S(2)}, u32[]{:S(2)}) collective-permute-start(bf16[32,4096]{1,0:T(8,128)(2,1)S(1)} %get-tuple-element.68.near_g), channel_id=1, source_target_pairs={{0,8},{4,12},{8,0},{12,4},{16,24},{20,28},{24,16},{28,20},{1,9},{5... | collective-permute-start | bytes 786440 | tf_op jit(solution)/shard_map/ppermute | solution.py:537
  46.2 7.6 %collective-permute-start.5 = (bf16[32,4352]{1,0:T(8,128)(2,1)S(1)}, bf16[32,4352]{1,0:T(8,128)(2,1)S(1)}, u32[]{:S(2)}, u32[]{:S(2)}) collective-permute-start(bf16[32,4352]{1,0:T(8,128)(2,1)S(1)} %get-tuple-element.80), channel_id=1, source_target_pairs={{0,4},{4,0},{8,12},{12,8},{16,20},{20,16},{24,28},{28,24},{1,5},{5... | collective-permute-start | bytes 835592 | tf_op jit(solution)/shard_map/ppermute | solution.py:537
  46.7 7.1 %collective-permute-start.6 = (bf16[32,4352]{1,0:T(8,128)(2,1)S(1)}, bf16[32,4352]{1,0:T(8,128)(2,1)S(1)}, u32[]{:S(2)}, u32[]{:S(2)}) collective-permute-start(bf16[32,4352]{1,0:T(8,128)(2,1)S(1)} %get-tuple-element.81), channel_id=1, source_target_pairs={{0,8},{4,12},{8,0},{12,4},{16,24},{20,28},{24,16},{28,20},{1,9},{5... | collective-permute-start | bytes 835592 | tf_op jit(solution)/shard_map/ppermute | solution.py:537
  53.9 5.5 %collective-permute-start.7 = (bf16[16,4608]{1,0:T(8,128)(2,1)S(1)}, bf16[16,4608]{1,0:T(8,128)(2,1)S(1)}, u32[]{:S(2)}, u32[]{:S(2)}) collective-permute-start(bf16[16,4608]{1,0:T(8,128)(2,1)S(1)} %get-tuple-element.89), channel_id=1, source_target_pairs={{0,8},{4,12},{8,0},{12,4},{16,24},{20,28},{24,16},{28,20},{1,9},{5... | collective-permute-start | bytes 442376 | tf_op jit(solution)/shard_map/ppermute | solution.py:537
  55.4 5.1 %collective-permute-start.8 = (bf16[16,4608]{1,0:T(8,128)(2,1)S(1)}, bf16[16,4608]{1,0:T(8,128)(2,1)S(1)}, u32[]{:S(2)}, u32[]{:S(2)}) collective-permute-start(bf16[16,4608]{1,0:T(8,128)(2,1)S(1)} %get-tuple-element.90), channel_id=1, source_target_pairs={{0,4},{4,0},{8,12},{12,8},{16,20},{20,16},{24,28},{28,24},{1,5},{5... | collective-permute-start | bytes 442376 | tf_op jit(solution)/shard_map/ppermute | solution.py:537
  60.6 8.7 %collective-permute-start.9 = (bf16[16,5120]{1,0:T(8,128)(2,1)S(1)}, bf16[16,5120]{1,0:T(8,128)(2,1)S(1)}, u32[]{:S(2)}, u32[]{:S(2)}) collective-permute-start(bf16[16,5120]{1,0:T(8,128)(2,1)S(1)} %get-tuple-element.96), channel_id=1, source_target_pairs={{0,16},{4,20},{8,24},{12,28},{16,0},{20,4},{24,8},{28,12},{1,17},{... | collective-permute-start | bytes 491528 | tf_op jit(solution)/shard_map/ppermute | solution.py:537
  63.9 6.6 %collective-permute-start.10 = (bf16[16,4224]{1,0:T(8,128)(2,1)S(1)}, bf16[16,4224]{1,0:T(8,128)(2,1)S(1)}, u32[]{:S(2)}, u32[]{:S(2)}) collective-permute-start(bf16[16,4224]{1,0:T(8,128)(2,1)S(1)} %get-tuple-element.101.refs_0_), channel_id=1, source_target_pairs={{0,2},{1,3},{2,0},{3,1},{4,6},{5,7},{6,4},{7,5},{8,10},{9,11},{10,... | collective-permute-start | bytes 405512 | tf_op jit(solution)/shard_map/ppermute | solution.py:537
  69.4 5.3 %collective-permute-start.13 = (bf16[16,4992]{1,0:T(8,128)(2,1)S(1)}, bf16[16,4992]{1,0:T(8,128)(2,1)S(1)}, u32[]{:S(2)}, u32[]{:S(2)}) collective-permute-start(bf16[16,4992]{1,0:T(8,128)(2,1)S(1)} %pack.1._.refs_4_), channel_id=1, source_target_pairs={{0,2},{1,3},{2,0},{3,1},{4,6},{5,7},{6,4},{7,5},{8,10},{9,11},{10,... | collective-permute-start | bytes 479240 | tf_op jit(solution)/shard_map/ppermute | solution.py:537
  70.6 3.0 %collective-permute-start.11 = (bf16[16,4224]{1,0:T(8,128)(2,1)S(1)}, bf16[16,4224]{1,0:T(8,128)(2,1)S(1)}, u32[]{:S(2)}, u32[]{:S(2)}) collective-permute-start(bf16[16,4224]{1,0:T(8,128)(2,1)S(1)} %get-tuple-element.101.refs_0_), channel_id=1, source_target_pairs={{0,1},{1,0},{2,3},{3,2},{4,5},{5,4},{6,7},{7,6},{8,9},{9,8},{10,11... | collective-permute-start | bytes 405512 | tf_op jit(solution)/shard_map/ppermute | solution.py:537
  70.6 3.0 %collective-permute-start.12 = (bf16[16,4224]{1,0:T(8,128)(2,1)S(1)}, bf16[16,4224]{1,0:T(8,128)(2,1)S(1)}, u32[]{:S(2)}, u32[]{:S(2)}) collective-permute-start(bf16[16,4224]{1,0:T(8,128)(2,1)S(1)} %collective-permute-done.10.refs_1_), channel_id=1, source_target_pairs={{0,1},{1,0},{2,3},{3,2},{4,5},{5,4},{6,7},{7,6},{8,9},{9,8},{10,11... | collective-permute-start | bytes 405512 | tf_op jit(solution)/shard_map/ppermute | solution.py:537
  71.1 3.6 %collective-permute-start.14 = (bf16[16,4992]{1,0:T(8,128)(2,1)S(1)}, bf16[16,4992]{1,0:T(8,128)(2,1)S(1)}, u32[]{:S(2)}, u32[]{:S(2)}) collective-permute-start(bf16[16,4992]{1,0:T(8,128)(2,1)S(1)} %pack.1._.refs_4_), channel_id=1, source_target_pairs={{0,1},{1,0},{2,3},{3,2},{4,5},{5,4},{6,7},{7,6},{8,9},{9,8},{10,11... | collective-permute-start | bytes 479240 | tf_op jit(solution)/shard_map/ppermute | solution.py:537
  74.7 1.5 %collective-permute-start.15 = (bf16[16,4992]{1,0:T(8,128)(2,1)S(1)}, bf16[16,4992]{1,0:T(8,128)(2,1)S(1)}, u32[]{:S(2)}, u32[]{:S(2)}) collective-permute-start(bf16[16,4992]{1,0:T(8,128)(2,1)S(1)} %relay.1.refs_5_), channel_id=1, source_target_pairs={{0,1},{1,0},{2,3},{3,2},{4,5},{5,4},{6,7},{7,6},{8,9},{9,8},{10,11... | collective-permute-start | bytes 479240 | tf_op jit(solution)/shard_map/ppermute | solution.py:537
